TPU v7x, 32 devices: a whole 2x2x4 slice. The times are simulated.
32 devices in a mesh: dp: 8 (over y, x, core), rep: 4 (over z).
Axes of the slice: x: 2, y: 2, z: 4, core: 2. Of those that a mesh axis runs over, the one named last changes fastest.
Arguments:
- image_input: bfloat16 [64, 16, 32, 1024], P(('dp', 'rep')), may hold values from -11 to 11
- heights: int32 [64], P(('dp', 'rep')), may hold values from 4 to 8
- widths: int32 [64], P(('dp', 'rep')), may hold values from 8 to 16
- w_reduce: bfloat16 [1024, 512], replicated, may hold values from -0.1875 to 0.1875
- w_spatial: bfloat16 [3, 3, 512, 512], replicated, may hold values from -0.09375 to 0.09375
- w_expand: bfloat16 [512, 2048], replicated, may hold values from -0.25 to 0.25
- w_shortcut: bfloat16 [1024, 2048], replicated, may hold values from -0.1875 to 0.1875
- gain_reduce: float32 [512], replicated, may hold values from 0.25 to 1.75
- shift_reduce: float32 [512], replicated, may hold values from -2.5 to 2.5
- gain_spatial: float32 [512], replicated, may hold values from 0.25 to 1.75
- shift_spatial: float32 [512], replicated, may hold values from -2.5 to 2.5
- gain_expand: float32 [2048], replicated, may hold values from 0.25 to 1.75
- shift_expand: float32 [2048], replicated, may hold values from -2.5 to 2.5
- gain_shortcut: float32 [2048], replicated, may hold values from 0.25 to 1.75
- shift_shortcut: float32 [2048], replicated, may hold values from -2.5 to 2.5
- w_squeeze: bfloat16 [2048, 512], replicated, may hold values from -0.125 to 0.125
- w_window: bfloat16 [3, 3, 512, 512], replicated, may hold values from -0.09375 to 0.09375
- w_widen: bfloat16 [512, 2048], replicated, may hold values from -0.25 to 0.25
- gain_squeeze: float32 [512], replicated, may hold values from 0.25 to 1.75
- shift_squeeze: float32 [512], replicated, may hold values from -2.5 to 2.5
- gain_window: float32 [512], replicated, may hold values from 0.25 to 1.75
- shift_window: float32 [512], replicated, may hold values from -2.5 to 2.5
- gain_widen: float32 [2048], replicated, may hold values from 0.25 to 1.75
- shift_widen: float32 [2048], replicated, may hold values from -2.5 to 2.5
- cotangent: bfloat16 [64, 8, 16, 2048], P(('dp', 'rep')), may hold values from -6 to 6
Outputs:
- block_out: bfloat16 [64, 8, 16, 2048], P(('dp', 'rep'))
- input_grad: bfloat16 [64, 16, 32, 1024], P(('dp', 'rep'))
- w_reduce_grad: float32 [1024, 512], replicated
- w_spatial_grad: float32 [3, 3, 512, 512], replicated
- w_expand_grad: float32 [512, 2048], replicated
- w_shortcut_grad: float32 [1024, 2048], replicated
- gain_reduce_grad: float32 [512], replicated
- shift_reduce_grad: float32 [512], replicated
- gain_spatial_grad: float32 [512], replicated
- shift_spatial_grad: float32 [512], replicated
- gain_expand_grad: float32 [2048], replicated
- shift_expand_grad: float32 [2048], replicated
- gain_shortcut_grad: float32 [2048], replicated
- shift_shortcut_grad: float32 [2048], replicated
- w_squeeze_grad: float32 [2048, 512], replicated
- w_window_grad: float32 [3, 3, 512, 512], replicated
- w_widen_grad: float32 [512, 2048], replicated
- gain_squeeze_grad: float32 [512], replicated
- shift_squeeze_grad: float32 [512], replicated
- gain_window_grad: float32 [512], replicated
- shift_window_grad: float32 [512], replicated
- gain_widen_grad: float32 [2048], replicated
- shift_widen_grad: float32 [2048], replicated
All inputs are finite; a program needn't handle non-finite values.
Results may differ from a plain program's by a relative error of at most 0.02.
Values sent between devices are 32-bit elements; how exact they have to be, the bound alone decides.
No kernel may reach another device: no remote copies, remote signals or barrier semaphores. Data moves between devices by JAX's collectives and lax.ppermute only.
A program may use at most 320 MiB of HBM per device.

v0:
```python
import math

import jax
import jax.numpy as jnp
from jax import lax
from jax.sharding import PartitionSpec as P

EPSILON = 1e-05


def make_mask(heights, widths, row_count, col_count):
    row_ids = lax.broadcasted_iota(jnp.int32, (1, row_count, 1), 1)
    col_ids = lax.broadcasted_iota(jnp.int32, (1, 1, col_count), 2)
    inside = (row_ids < heights[:, None, None]) & (col_ids < widths[:, None, None])
    return jnp.where(inside, 1.0, 0.0).astype(jnp.float32)[..., None]


def project(left, right):
    return jnp.einsum("bhwc,cd->bhwd", left, right, preferred_element_type=jnp.float32)


def project_back(left, right):
    return jnp.einsum("bhwd,cd->bhwc", left, right, preferred_element_type=jnp.float32)


def outer_sum(left, right):
    return jnp.einsum("bhwc,bhwd->cd", left, right, preferred_element_type=jnp.float32)


def local_moments(values, masking):
    masked = values * masking
    return (jnp.sum(masked, axis=(0, 1, 2)), jnp.sum(masked * values, axis=(0, 1, 2)))


def normalize(values, totals, squares, counts, norm_gain, norm_shift):
    average = totals / counts
    inverse = lax.rsqrt(squares / counts - average * average + EPSILON)
    centred = (values - average) * inverse
    return (centred, inverse, centred * norm_gain + norm_shift)


def silu_slope(values):
    logistic = jax.nn.sigmoid(values)
    return logistic * (1.0 + values * (1.0 - logistic))


def norm_back(grad_norm, centred, inverse, norm_gain, shift_grad, gain_grad, masking, counts):
    inner = grad_norm - masking * (shift_grad + centred * gain_grad) / counts
    return (inner * (inverse * norm_gain)).astype(jnp.bfloat16)


def tap_columns(active, out_rows, out_cols, stride):
    padded = jnp.pad(active, ((0, 0), (1, 1), (1, 1), (0, 0)))
    pieces = []
    for row_tap in range(3):
        for col_tap in range(3):
            pieces.append(
                padded[
                    :,
                    row_tap : row_tap + stride * out_rows : stride,
                    col_tap : col_tap + stride * out_cols : stride,
                    :,
                ]
            )
    return jnp.concatenate(pieces, axis=3)


def tap_scatter(grad_columns, out_rows, out_cols, channels, stride):
    images = grad_columns.shape[0]
    padded = jnp.zeros(
        (images, stride * out_rows + 2, stride * out_cols + 2, channels), jnp.float32
    )
    for row_tap in range(3):
        for col_tap in range(3):
            first = (row_tap * 3 + col_tap) * channels
            padded = padded.at[
                :,
                row_tap : row_tap + stride * out_rows : stride,
                col_tap : col_tap + stride * out_cols : stride,
                :,
            ].add(grad_columns[..., first : first + channels])
    return padded[:, 1:-1, 1:-1, :]


def flatten_all(arrays):
    return jnp.concatenate([element.reshape(-1) for element in arrays], axis=0)


def unflatten(flat, shapes):
    pieces = []
    start = 0
    for shape in shapes:
        extent = math.prod(shape)
        pieces.append(flat[start : start + extent].reshape(shape))
        start = start + extent
    return pieces


def on_device(
    image_input,
    heights,
    widths,
    w_reduce,
    w_spatial,
    w_expand,
    w_shortcut,
    gain_reduce,
    shift_reduce,
    gain_spatial,
    shift_spatial,
    gain_expand,
    shift_expand,
    gain_shortcut,
    shift_shortcut,
    w_squeeze,
    w_window,
    w_widen,
    gain_squeeze,
    shift_squeeze,
    gain_window,
    shift_window,
    gain_widen,
    shift_widen,
    cotangent,
):
    out_rows = cotangent.shape[1]
    out_cols = cotangent.shape[2]
    middle = w_reduce.shape[1]
    mask_in = make_mask(2 * heights, 2 * widths, 2 * out_rows, 2 * out_cols)
    mask_out = make_mask(heights, widths, out_rows, out_cols)
    masked_input = image_input * mask_in.astype(jnp.bfloat16)
    sub_input = masked_input[:, ::2, ::2, :]
    local_count = jnp.sum(mask_out)
    pre_reduce = project(masked_input, w_reduce)
    sum_reduce, square_reduce = local_moments(pre_reduce, mask_in)
    sum_reduce, square_reduce, pixel_count = lax.psum(
        (sum_reduce, square_reduce, local_count), ("dp", "rep")
    )
    count_in = 4.0 * pixel_count
    hat_reduce, inv_reduce, norm_reduce = normalize(
        pre_reduce, sum_reduce, square_reduce, count_in, gain_reduce, shift_reduce
    )
    act_reduce = (jax.nn.silu(norm_reduce) * mask_in).astype(jnp.bfloat16)
    columns = tap_columns(act_reduce, out_rows, out_cols, 2)
    flat_spatial = w_spatial.reshape(9 * middle, middle)
    pre_spatial = project(columns, flat_spatial)
    sum_spatial, square_spatial = local_moments(pre_spatial, mask_out)
    sum_spatial, square_spatial = lax.psum((sum_spatial, square_spatial), ("dp", "rep"))
    hat_spatial, inv_spatial, norm_spatial = normalize(
        pre_spatial, sum_spatial, square_spatial, pixel_count, gain_spatial, shift_spatial
    )
    act_spatial = (jax.nn.silu(norm_spatial) * mask_out).astype(jnp.bfloat16)
    pre_expand = project(act_spatial, w_expand)
    sum_expand, square_expand = local_moments(pre_expand, mask_out)
    pre_short = project(sub_input, w_shortcut)
    sum_short, square_short = local_moments(pre_short, mask_out)
    sum_expand, square_expand, sum_short, square_short = lax.psum(
        (sum_expand, square_expand, sum_short, square_short), ("dp", "rep")
    )
    hat_expand, inv_expand, norm_expand = normalize(
        pre_expand, sum_expand, square_expand, pixel_count, gain_expand, shift_expand
    )
    hat_short, inv_short, norm_short = normalize(
        pre_short, sum_short, square_short, pixel_count, gain_shortcut, shift_shortcut
    )
    joined = norm_expand + norm_short
    first_out = (jax.nn.silu(joined) * mask_out).astype(jnp.bfloat16)
    pre_squeeze = project(first_out, w_squeeze)
    sum_squeeze, square_squeeze = local_moments(pre_squeeze, mask_out)
    sum_squeeze, square_squeeze = lax.psum((sum_squeeze, square_squeeze), ("dp", "rep"))
    hat_squeeze, inv_squeeze, norm_squeeze = normalize(
        pre_squeeze, sum_squeeze, square_squeeze, pixel_count, gain_squeeze, shift_squeeze
    )
    act_squeeze = (jax.nn.silu(norm_squeeze) * mask_out).astype(jnp.bfloat16)
    window_columns = tap_columns(act_squeeze, out_rows, out_cols, 1)
    flat_window = w_window.reshape(9 * middle, middle)
    pre_window = project(window_columns, flat_window)
    sum_window, square_window = local_moments(pre_window, mask_out)
    sum_window, square_window = lax.psum((sum_window, square_window), ("dp", "rep"))
    hat_window, inv_window, norm_window = normalize(
        pre_window, sum_window, square_window, pixel_count, gain_window, shift_window
    )
    act_window = (jax.nn.silu(norm_window) * mask_out).astype(jnp.bfloat16)
    pre_widen = project(act_window, w_widen)
    sum_widen, square_widen = local_moments(pre_widen, mask_out)
    sum_widen, square_widen = lax.psum((sum_widen, square_widen), ("dp", "rep"))
    hat_widen, inv_widen, norm_widen = normalize(
        pre_widen, sum_widen, square_widen, pixel_count, gain_widen, shift_widen
    )
    final = norm_widen + first_out.astype(jnp.float32)
    block_out = (jax.nn.silu(final) * mask_out).astype(jnp.bfloat16)
    grad_final = cotangent.astype(jnp.float32) * mask_out * silu_slope(final)
    shift_grad_widen, gain_grad_widen = lax.psum(
        (jnp.sum(grad_final, axis=(0, 1, 2)), jnp.sum(grad_final * hat_widen, axis=(0, 1, 2))),
        ("dp", "rep"),
    )
    grad_pre_widen = norm_back(
        grad_final,
        hat_widen,
        inv_widen,
        gain_widen,
        shift_grad_widen,
        gain_grad_widen,
        mask_out,
        pixel_count,
    )
    grad_w_widen = outer_sum(act_window, grad_pre_widen)
    grad_norm_window = project_back(grad_pre_widen, w_widen) * mask_out * silu_slope(norm_window)
    shift_grad_window, gain_grad_window = lax.psum(
        (
            jnp.sum(grad_norm_window, axis=(0, 1, 2)),
            jnp.sum(grad_norm_window * hat_window, axis=(0, 1, 2)),
        ),
        ("dp", "rep"),
    )
    grad_pre_window = norm_back(
        grad_norm_window,
        hat_window,
        inv_window,
        gain_window,
        shift_grad_window,
        gain_grad_window,
        mask_out,
        pixel_count,
    )
    grad_w_window = outer_sum(window_columns, grad_pre_window).reshape(3, 3, middle, middle)
    grad_act_squeeze = tap_scatter(
        project_back(grad_pre_window, flat_window), out_rows, out_cols, middle, 1
    )
    grad_norm_squeeze = grad_act_squeeze * mask_out * silu_slope(norm_squeeze)
    shift_grad_squeeze, gain_grad_squeeze = lax.psum(
        (
            jnp.sum(grad_norm_squeeze, axis=(0, 1, 2)),
            jnp.sum(grad_norm_squeeze * hat_squeeze, axis=(0, 1, 2)),
        ),
        ("dp", "rep"),
    )
    grad_pre_squeeze = norm_back(
        grad_norm_squeeze,
        hat_squeeze,
        inv_squeeze,
        gain_squeeze,
        shift_grad_squeeze,
        gain_grad_squeeze,
        mask_out,
        pixel_count,
    )
    grad_w_squeeze = outer_sum(first_out, grad_pre_squeeze)
    grad_first = grad_final + project_back(grad_pre_squeeze, w_squeeze)
    grad_joined = grad_first * mask_out * silu_slope(joined)
    shift_total, gain_grad_expand, gain_grad_short = lax.psum(
        (
            jnp.sum(grad_joined, axis=(0, 1, 2)),
            jnp.sum(grad_joined * hat_expand, axis=(0, 1, 2)),
            jnp.sum(grad_joined * hat_short, axis=(0, 1, 2)),
        ),
        ("dp", "rep"),
    )
    grad_pre_expand = norm_back(
        grad_joined,
        hat_expand,
        inv_expand,
        gain_expand,
        shift_total,
        gain_grad_expand,
        mask_out,
        pixel_count,
    )
    grad_pre_short = norm_back(
        grad_joined,
        hat_short,
        inv_short,
        gain_shortcut,
        shift_total,
        gain_grad_short,
        mask_out,
        pixel_count,
    )
    grad_w_expand = outer_sum(act_spatial, grad_pre_expand)
    grad_w_short = outer_sum(sub_input, grad_pre_short)
    early_list = (grad_w_expand, grad_w_short, grad_w_squeeze, grad_w_window, grad_w_widen)
    early_shapes = [element.shape for element in early_list]
    grad_norm_spatial = (
        project_back(grad_pre_expand, w_expand) * mask_out * silu_slope(norm_spatial)
    )
    shift_grad_spatial, gain_grad_spatial = lax.psum(
        (
            jnp.sum(grad_norm_spatial, axis=(0, 1, 2)),
            jnp.sum(grad_norm_spatial * hat_spatial, axis=(0, 1, 2)),
        ),
        ("dp", "rep"),
    )
    grad_pre_spatial = norm_back(
        grad_norm_spatial,
        hat_spatial,
        inv_spatial,
        gain_spatial,
        shift_grad_spatial,
        gain_grad_spatial,
        mask_out,
        pixel_count,
    )
    grad_w_spatial = outer_sum(columns, grad_pre_spatial).reshape(3, 3, middle, middle)
    grad_columns = project_back(grad_pre_spatial, flat_spatial)
    grad_act_reduce = tap_scatter(grad_columns, out_rows, out_cols, middle, 2)
    grad_norm_reduce = grad_act_reduce * mask_in * silu_slope(norm_reduce)
    shift_grad_reduce, gain_grad_reduce = lax.psum(
        (
            jnp.sum(grad_norm_reduce, axis=(0, 1, 2)),
            jnp.sum(grad_norm_reduce * hat_reduce, axis=(0, 1, 2)),
        ),
        ("dp", "rep"),
    )
    grad_pre_reduce = norm_back(
        grad_norm_reduce,
        hat_reduce,
        inv_reduce,
        gain_reduce,
        shift_grad_reduce,
        gain_grad_reduce,
        mask_in,
        count_in,
    )
    grad_w_reduce = outer_sum(masked_input, grad_pre_reduce)
    grad_image = project_back(grad_pre_reduce, w_reduce)
    grad_image = grad_image.at[:, ::2, ::2, :].add(project_back(grad_pre_short, w_shortcut))
    input_grad = (grad_image * mask_in).astype(jnp.bfloat16)
    late_list = (grad_w_reduce, grad_w_spatial)
    late_shapes = [element.shape for element in late_list]
    all_shard = lax.psum_scatter(
        flatten_all(early_list + late_list), ("dp", "rep"), scatter_dimension=0, tiled=True
    )
    all_whole = lax.all_gather(all_shard, ("dp", "rep"), axis=0, tiled=True)
    summed = unflatten(all_whole, early_shapes + late_shapes)
    return (
        block_out,
        input_grad,
        summed[5],
        summed[6],
        summed[0],
        summed[1],
        gain_grad_reduce,
        shift_grad_reduce,
        gain_grad_spatial,
        shift_grad_spatial,
        gain_grad_expand,
        shift_total,
        gain_grad_short,
        shift_total,
        summed[2],
        summed[3],
        summed[4],
        gain_grad_squeeze,
        shift_grad_squeeze,
        gain_grad_window,
        shift_grad_window,
        gain_grad_widen,
        shift_grad_widen,
    )


def solution(mesh):
    return jax.shard_map(
        on_device,
        mesh=mesh,
        in_specs=(
            P(("dp", "rep"), None, None, None),
            P(("dp", "rep")),
            P(("dp", "rep")),
            P(),
            P(),
            P(),
            P(),
            P(),
            P(),
            P(),
            P(),
            P(),
            P(),
            P(),
            P(),
            P(),
            P(),
            P(),
            P(),
            P(),
            P(),
            P(),
            P(),
            P(),
            P(("dp", "rep"), None, None, None),
        ),
        out_specs=(
            P(("dp", "rep"), None, None, None),
            P(("dp", "rep"), None, None, None),
            P(),
            P(),
            P(),
            P(),
            P(),
            P(),
            P(),
            P(),
            P(),
            P(),
            P(),
            P(),
            P(),
            P(),
            P(),
            P(),
            P(),
            P(),
            P(),
            P(),
            P(),
        ),
        check_vma=False,
    )
```

profile of v0, /device:TPU:0, one launch (start us, length us, event | category | flops | bytes accessed | tf_op | source)
XLA Modules:
  0.0 1895.1 jit_solution(9899396274374187620)
XLA Ops:
  14.3 7.7 slice.504
  22.0 4.7 multiply_reduce_fusion.3
  26.7 42.2 %all-reduce.15 = (f32[512]{0:T(512)S(1)}, f32[]{:T(128)}, f32[512]{0:T(512)S(1)}) all-reduce(f32[512]{0:T(512)S(1)} %get-tuple-element.201, f32[]{:T(128)} %select_reduce_fusion, f32[512]{0:T(512)S(1)} %get-tuple-element.200), channel_id=1, replica_groups=mesh['dp'=8,'rep'=4] {'dp','rep'}, use_global_device_ids=true, to_apply=%region_5.6 | all-reduce | flops 1025 | bytes 8200 | tf_op jit(solution)/shard_map/psum | solution.py:136
  74.3 8.8 slice.495
  83.1 8.8 slice.496
  91.9 9.1 slice.497
  101.1 8.8 slice.498
  109.9 8.8 slice.499
  118.7 9.1 slice.500
  127.8 8.8 slice.501
  136.6 7.0 slice.502
  143.7 7.5 slice.503
  155.7 5.0 fusion.2
  163.3 40.3 %all-reduce.14 = (f32[512]{0:T(512)S(1)}, f32[512]{0:T(512)S(1)}) all-reduce(f32[512]{0:T(512)S(1)} %get-tuple-element.220, f32[512]{0:T(512)S(1)} %get-tuple-element.219), channel_id=1, replica_groups=mesh['dp'=8,'rep'=4] {'dp','rep'}, use_global_device_ids=true, to_apply=%region_9.10 | all-reduce | flops 1024 | bytes 8192 | tf_op jit(solution)/shard_map/psum | solution.py:148
  204.3 4.2 multiply_reduce_fusion.2
  208.5 40.3 %all-reduce.13 = (f32[2048]{0:T(1024)S(1)}, f32[2048]{0:T(1024)S(1)}, f32[2048]{0:T(1024)S(1)}, f32[2048]{0:T(1024)S(1)}) all-reduce(f32[2048]{0:T(1024)S(1)} %get-tuple-element.227, f32[2048]{0:T(1024)S(1)} %get-tuple-element.228, f32[2048]{0:T(1024)S(1)} %get-tuple-element.205, ...), channel_id=1, replica_groups=mesh['dp'=8,'rep'=4] {'dp','rep'}, use_global_device_ids=true, to_apply=%region_17.18 | all-reduce | flops 8192 | bytes 65536 | tf_op jit(solution)/shard_map/psum | solution.py:157
  254.7 40.4 %all-reduce.12 = (f32[512]{0:T(512)S(1)}, f32[512]{0:T(512)S(1)}) all-reduce(f32[512]{0:T(512)S(1)} %get-tuple-element.218, f32[512]{0:T(512)S(1)} %get-tuple-element.217), channel_id=1, replica_groups=mesh['dp'=8,'rep'=4] {'dp','rep'}, use_global_device_ids=true, to_apply=%region_21.22 | all-reduce | flops 1024 | bytes 8192 | tf_op jit(solution)/shard_map/psum | solution.py:170
  296.6 5.4 multiply_reduce_fusion.8
  302.0 39.9 %all-reduce.11 = (f32[512]{0:T(512)S(1)}, f32[512]{0:T(512)S(1)}) all-reduce(f32[512]{0:T(512)S(1)} %get-tuple-element.216, f32[512]{0:T(512)S(1)} %get-tuple-element.215), channel_id=1, replica_groups=mesh['dp'=8,'rep'=4] {'dp','rep'}, use_global_device_ids=true, to_apply=%region_25.26 | all-reduce | flops 1024 | bytes 8192 | tf_op jit(solution)/shard_map/psum | solution.py:179
  342.5 4.0 fusion.9
  346.6 40.2 %all-reduce.10 = (f32[2048]{0:T(1024)S(1)}, f32[2048]{0:T(1024)S(1)}) all-reduce(f32[2048]{0:T(1024)S(1)} %get-tuple-element.203, f32[2048]{0:T(1024)S(1)} %get-tuple-element.202), channel_id=1, replica_groups=mesh['dp'=8,'rep'=4] {'dp','rep'}, use_global_device_ids=true, to_apply=%region_27.28 | all-reduce | flops 4096 | bytes 32768 | tf_op jit(solution)/shard_map/psum | solution.py:186
  388.1 5.1 fusion.61
  393.2 40.0 %all-reduce.9 = (f32[2048]{0:T(1024)S(1)}, f32[2048]{0:T(1024)S(1)}) all-reduce(f32[2048]{0:T(1024)S(1)} %get-tuple-element.214, f32[2048]{0:T(1024)S(1)} %get-tuple-element.213), channel_id=1, replica_groups=mesh['dp'=8,'rep'=4] {'dp','rep'}, use_global_device_ids=true, to_apply=%region_33.34 | all-reduce | flops 4096 | bytes 32768 | tf_op jit(solution)/shard_map/psum | solution.py:193
  438.7 40.5 %all-reduce.8 = (f32[512]{0:T(512)S(1)}, f32[512]{0:T(512)S(1)}) all-reduce(f32[512]{0:T(512)S(1)} %get-tuple-element.226, f32[512]{0:T(512)S(1)} %get-tuple-element.225), channel_id=1, replica_groups=mesh['dp'=8,'rep'=4] {'dp','rep'}, use_global_device_ids=true, to_apply=%region_37.38 | all-reduce | flops 1024 | bytes 8192 | tf_op jit(solution)/shard_map/psum | solution.py:209
  481.0 3.8 fusion.76
  493.6 3.9 add_select_fusion
  523.2 39.9 %all-reduce.7 = (f32[512]{0:T(512)S(1)}, f32[512]{0:T(512)S(1)}) all-reduce(f32[512]{0:T(512)S(1)} %get-tuple-element.224, f32[512]{0:T(512)S(1)} %get-tuple-element.223), channel_id=1, replica_groups=mesh['dp'=8,'rep'=4] {'dp','rep'}, use_global_device_ids=true, to_apply=%region_42.43 | all-reduce | flops 1024 | bytes 8192 | tf_op jit(solution)/shard_map/psum | solution.py:231
  565.6 6.5 multiply_reduce_fusion.4
  572.1 40.2 %all-reduce.6 = (f32[2048]{0:T(1024)S(1)}, f32[2048]{0:T(1024)S(1)}) all-reduce(f32[2048]{0:T(1024)S(1)} %get-tuple-element.209, f32[2048]{0:T(1024)S(1)} %get-tuple-element.210), channel_id=1, replica_groups=mesh['dp'=8,'rep'=4] {'dp','rep'}, use_global_device_ids=true, to_apply=%region_46.47 | all-reduce | flops 4096 | bytes 32768 | tf_op jit(solution)/shard_map/psum | solution.py:251
  623.5 5.2 convolution_bitcast_fusion.1
  631.6 40.1 %all-reduce.5 = (f32[512]{0:T(512)S(1)}, f32[512]{0:T(512)S(1)}) all-reduce(f32[512]{0:T(512)S(1)} %get-tuple-element.222, f32[512]{0:T(512)S(1)} %get-tuple-element.221), channel_id=1, replica_groups=mesh['dp'=8,'rep'=4] {'dp','rep'}, use_global_device_ids=true, to_apply=%region_50.51 | all-reduce | flops 1024 | bytes 8192 | tf_op jit(solution)/shard_map/psum | solution.py:286
  672.5 6.1 fusion.77
  678.7 5.0 convolution_bitcast_fusion
  683.9 4.1 fusion.73
  702.9 16.1 scatter_fusion
  719.0 16.1 scatter_fusion.1
  735.0 16.1 scatter_fusion.2
  751.1 16.1 scatter_fusion.3
  767.2 16.3 scatter_fusion.4
  783.5 16.1 scatter_fusion.5
  799.6 16.1 scatter_fusion.6
  815.7 16.1 scatter_fusion.7
  831.8 16.1 scatter_fusion.8
  856.2 40.5 %all-reduce.4 = (f32[512]{0:T(512)S(1)}, f32[512]{0:T(512)S(1)}, f32[2048]{0:T(1024)S(1)}) all-reduce(f32[512]{0:T(512)S(1)} %get-tuple-element.212, f32[512]{0:T(512)S(1)} %get-tuple-element.211, f32[2048]{0:T(1024)S(1)} %get-tuple-element.208), channel_id=1, replica_groups=mesh['dp'=8,'rep'=4] {'dp','rep'}, use_global_device_ids=true, to_apply=%region_63.64 | all-reduce | flops 3072 | bytes 24576 | tf_op jit(solution)/shard_map/psum | solution.py:307
  902.6 5.4 copy.106
  911.1 9.8 copy.108
  921.0 5.3 copy.109
  929.7 10.0 copy.111
  939.7 6.7 constant_dynamic-update-slice_fusion.16
  951.6 4.9 constant_dynamic-update-slice_fusion.14
  966.0 603.6 %all-reduce.18.cloned.1.call-done = f32[10485760]{0:T(1024)} async-done(((f32[10485760]{0:T(1024)}), f32[10485760]{0:T(1024)}) %all-reduce.18.cloned.1.call-update) | async-done | bytes 41943056
  1573.6 5.3 copy.86
  1583.6 18.4 scatter_fusion.9
  1602.0 3.9 multiply_convert_fusion
  1607.8 200.5 %all-gather.2.cloned.1.call-done = f32[10485760]{0:T(1024)} async-done(((f32[327680]{0:T(1024)}), f32[10485760]{0:T(1024)}) %all-gather.2.cloned.1.call-update) | async-done | bytes 41943056 | tf_op jit(solution)/shard_map/all_gather | solution.py:333
  1811.4 14.2 fusion.72
  1825.6 11.2 reshape.640
  1836.8 9.6 fusion.71
  1846.3 4.9 slice.547
  1851.2 5.9 slice.604
  1857.1 9.2 slice.549
  1866.3 4.9 slice.551
  1871.2 11.2 reshape.641
  1882.4 5.0 slice.554
  (319 shorter events, 152.0 us)
Async XLA Ops:
  7.2 197.1 %copy-start = (bf16[512,2048]{1,0:T(8,128)(2,1)S(1)}, bf16[512,2048]{1,0:T(8,128)(2,1)}, u32[]{:S(2)}) copy-start(bf16[512,2048]{1,0:T(8,128)(2,1)} %param.48) | copy-start | bytes 6291460
  7.2 1562.4 %all-reduce.18.cloned.1.call-start = ((), (), s32[]{:S(2)}) async-start(), calls=%async_computation.1 | async-start | bytes 83886080
  21.9 133.7 %copy-start.18 = (bf16[2,8,16,1024]{3,2,1,0:T(8,128)(2,1)}, bf16[2,8,16,1024]{3,2,1,0:T(8,128)(2,1)S(1)}, u32[]{:S(2)}) copy-start(bf16[2,8,16,1024]{3,2,1,0:T(8,128)(2,1)S(1)} %slice.504) | copy-start | bytes 1572868
  22.0 47.6 %copy-start.46 = (f32[512]{0:T(512)S(1)}, f32[512]{0:T(512)}, u32[]{:S(2)}) copy-start(f32[512]{0:T(512)} %param.50) | copy-start | bytes 6148
  22.0 48.2 %copy-start.54 = (f32[512]{0:T(512)S(1)}, f32[512]{0:T(512)}, u32[]{:S(2)}) copy-start(f32[512]{0:T(512)} %param.51) | copy-start | bytes 6148
  154.5 7.3 slice-start.7
  155.7 5.1 copy-start.23
  155.7 5.1 copy-start.22
  155.7 6.1 slice-start.8
  161.8 41.8 %copy-start.64 = (f32[512]{0:T(512)S(1)}, f32[512]{0:T(512)}, u32[]{:S(2)}) copy-start(f32[512]{0:T(512)} %param.52) | copy-start | bytes 6148
  161.9 42.4 %copy-start.81 = (f32[512]{0:T(512)S(1)}, f32[512]{0:T(512)}, u32[]{:S(2)}) copy-start(f32[512]{0:T(512)} %param.53) | copy-start | bytes 6148
  163.3 45.2 %copy-start.31 = (f32[2,8,16,512]{3,2,1,0:T(8,128)}, f32[2,8,16,512]{3,2,1,0:T(8,128)S(1)}, u32[]{:S(2)}) copy-start(f32[2,8,16,512]{3,2,1,0:T(8,128)S(1)} %get-tuple-element.311) | copy-start | bytes 1572868
  204.3 44.5 %copy-start.38 = (f32[2048]{0:T(1024)S(1)}, f32[2048]{0:T(1024)}, u32[]{:S(2)}) copy-start(f32[2048]{0:T(1024)} %param.56) | copy-start | bytes 24580
  204.3 44.5 %copy-start.39 = (f32[2048]{0:T(1024)S(1)}, f32[2048]{0:T(1024)}, u32[]{:S(2)}) copy-start(f32[2048]{0:T(1024)} %param.54) | copy-start | bytes 24580
  204.3 45.1 %copy-start.48 = (f32[2048]{0:T(1024)S(1)}, f32[2048]{0:T(1024)}, u32[]{:S(2)}) copy-start(f32[2048]{0:T(1024)} %param.57) | copy-start | bytes 24580
  204.3 45.1 %copy-start.49 = (f32[2048]{0:T(1024)S(1)}, f32[2048]{0:T(1024)}, u32[]{:S(2)}) copy-start(f32[2048]{0:T(1024)} %param.55) | copy-start | bytes 24580
  253.9 41.1 %copy-start.37 = (f32[512]{0:T(512)S(1)}, f32[512]{0:T(512)}, u32[]{:S(2)}) copy-start(f32[512]{0:T(512)} %param.61) | copy-start | bytes 6148
  253.9 41.7 %copy-start.45 = (f32[512]{0:T(512)S(1)}, f32[512]{0:T(512)}, u32[]{:S(2)}) copy-start(f32[512]{0:T(512)} %param.62) | copy-start | bytes 6148
  254.7 41.7 %copy-start.6 = (f32[2,8,16,512]{3,2,1,0:T(8,128)}, f32[2,8,16,512]{3,2,1,0:T(8,128)S(1)}, u32[]{:S(2)}) copy-start(f32[2,8,16,512]{3,2,1,0:T(8,128)S(1)} %get-tuple-element.313) | copy-start | bytes 1572868
  296.6 5.4 copy-start.43
  296.6 45.3 %copy-start.65 = (f32[512]{0:T(512)S(1)}, f32[512]{0:T(512)}, u32[]{:S(2)}) copy-start(f32[512]{0:T(512)} %param.63) | copy-start | bytes 6148
  296.6 45.9 %copy-start.83 = (f32[512]{0:T(512)S(1)}, f32[512]{0:T(512)}, u32[]{:S(2)}) copy-start(f32[512]{0:T(512)} %param.64) | copy-start | bytes 6148
  342.5 44.3 %copy-start.40 = (f32[2048]{0:T(1024)S(1)}, f32[2048]{0:T(1024)}, u32[]{:S(2)}) copy-start(f32[2048]{0:T(1024)} %param.65) | copy-start | bytes 24580
  342.5 45.6 %copy-start.11 = (bf16[2,8,16,2048]{3,2,1,0:T(8,128)(2,1)S(1)}, bf16[2,8,16,2048]{3,2,1,0:T(8,128)(2,1)}, u32[]{:S(2)}) copy-start(bf16[2,8,16,2048]{3,2,1,0:T(8,128)(2,1)} %copy-done.10) | copy-start | bytes 3145732
  342.5 45.6 %copy-start.55 = (f32[2048]{0:T(1024)S(1)}, f32[2048]{0:T(1024)}, u32[]{:S(2)}) copy-start(f32[2048]{0:T(1024)} %param.66) | copy-start | bytes 24580
  479.2 5.6 copy-start.58
  479.2 5.6 copy-start.59
  612.4 1275.1 %copy-start.36 = (f32[2048]{0:T(1024)}, f32[2048]{0:T(1024)S(1)}, u32[]{:S(2)}) copy-start(f32[2048]{0:T(1024)S(1)} %get-tuple-element.374) | copy-start | bytes 24580
  623.4 5.2 copy-start.28
  623.4 5.2 copy-start.34
  623.4 5.2 copy-start.84
  628.6 43.0 %copy-start.35 = (f32[2,8,16,512]{3,2,1,0:T(8,128)S(1)}, f32[2,8,16,512]{3,2,1,0:T(8,128)}, u32[]{:S(2)}) copy-start(f32[2,8,16,512]{3,2,1,0:T(8,128)} %get-tuple-element.318) | copy-start | bytes 1572868
  671.7 6.9 copy-start.62
  671.7 6.9 copy-start.63
  672.5 6.1 copy-start.42
  678.6 5.1 copy-start.66
  678.6 5.1 copy-start.67
  678.6 5.1 copy-start.68
  678.6 5.1 copy-start.69
  678.6 5.1 copy-start.70
  678.6 5.1 copy-start.71
  735.0 48.5 %copy-start.14 = (f32[128,2,512]{2,1,0:T(2,128)S(1)}, f32[128,2,512]{2,1,0:T(2,128)}, u32[]{:S(2)}) copy-start(f32[128,2,512]{2,1,0:T(2,128)} %copy.81) | copy-start | bytes 1572868
  751.1 48.5 %copy-start.15 = (f32[128,2,512]{2,1,0:T(2,128)S(1)}, f32[128,2,512]{2,1,0:T(2,128)}, u32[]{:S(2)}) copy-start(f32[128,2,512]{2,1,0:T(2,128)} %copy.82) | copy-start | bytes 1572868
  767.2 48.5 %copy-start.16 = (f32[128,2,512]{2,1,0:T(2,128)S(1)}, f32[128,2,512]{2,1,0:T(2,128)}, u32[]{:S(2)}) copy-start(f32[128,2,512]{2,1,0:T(2,128)} %copy.83) | copy-start | bytes 1572868
  783.5 48.3 %copy-start.17 = (f32[128,2,512]{2,1,0:T(2,128)S(1)}, f32[128,2,512]{2,1,0:T(2,128)}, u32[]{:S(2)}) copy-start(f32[128,2,512]{2,1,0:T(2,128)} %copy.84) | copy-start | bytes 1572868
  896.7 29.5 %copy-start.56 = (f32[512]{0:T(512)}, f32[512]{0:T(512)S(1)}, u32[]{:S(2)}) copy-start(f32[512]{0:T(512)S(1)} %get-tuple-element.367) | copy-start | bytes 6148
  896.7 29.5 %copy-start.57 = (f32[512]{0:T(512)}, f32[512]{0:T(512)S(1)}, u32[]{:S(2)}) copy-start(f32[512]{0:T(512)S(1)} %get-tuple-element.368) | copy-start | bytes 6148
  902.6 5.5 copy-start.8
  921.0 5.3 copy-start.7
  921.0 5.3 copy-start.47
  939.7 7.3 copy-start.5
  939.7 9.7 slice-start.1
  939.7 11.5 slice-start.2
  951.6 8.8 slice-start.4
  951.6 8.9 slice-start.5
  956.5 5.7 slice-start.6
  966.0 842.3 %all-gather.2.cloned.1.call-start = ((), (), s32[]{:S(2)}) async-start(), calls=%async_computation | async-start | bytes 43253760 | tf_op jit(solution)/shard_map/all_gather | solution.py:333
  966.0 606.2 %copy-start.26 = (bf16[1024,512]{1,0:T(8,128)(2,1)S(1)}, bf16[1024,512]{1,0:T(8,128)(2,1)}, u32[]{:S(2)}) copy-start(bf16[1024,512]{1,0:T(8,128)(2,1)} %param.46) | copy-start | bytes 3145732
  1573.6 5.3 copy-start.74
  1573.6 5.3 copy-start.75
  1573.6 5.3 copy-start.76
  1573.6 5.3 copy-start.77
  1573.6 5.5 copy-start.30
  1882.4 5.6 copy-start.1
  (32 other events, 96.5 us)
Sparse Core Ops, SparseCore 0:
  966.1 603.4 all-reduce.17
  1573.0 235.2 all-gather.1
where the time goes:
time: 1910 us; the launch traced here: 1900 us
  waiting for transfers between devices  804 us (42%)
  blocking collectives  485 us (25%)
  local copies, waits for them, and re-layouts  287 us (15%)
  other arithmetic  231 us (12%)
  matrix products  71.7 us (4%)
    unnamed x3, waiting for transfers between devices  604 us
    all_gather x1, waiting for transfers between devices, on_device(): all_whole = lax.all_gather(all_shard, ('dp', 'rep'), axis=0, tiled=True)  200 us
    scatter-add x11, other arithmetic, tap_scatter(): padded = padded.at[:, row_tap:row_tap + stride * out_rows:stride, col_tap...  147 us
    slice x9, local copies, waits for them, and re-layouts, tap_columns(): padded[:, row_tap:row_tap + stride * out_rows:stride, col_tap:col_tap + s...  76.8 us
    unnamed x217, local copies, waits for them, and re-layouts  71.5 us
    slice x10, local copies, waits for them, and re-layouts, unflatten(): pieces.append(flat[start:start + extent].reshape(shape))  56.8 us
    psum x1, blocking collectives, on_device(): lax.psum((sum_reduce, square_reduce, local_count), ('dp', 'rep'))  42.2 us
    psum x1, blocking collectives, on_device(): lax.psum((jnp.sum(grad_norm_window, axis=(0, 1, 2)), jnp.sum(grad_norm_wi...  40.5 us
  transfers between devices with their start and end apart: 2, of which 2 were waited for; matrix products, arithmetic and copies ran while one was open for 2% of the time, Pallas kernels for 0%

commit v1 on v0

v1 whole, which is shorter than its diff:
```python
import functools

import jax
import jax.numpy as jnp
import numpy as np
from jax import lax
from jax.experimental import pallas as pl
from jax.experimental.pallas import tpu as pltpu
from jax.sharding import PartitionSpec as P

EPSILON = 1e-05
F32 = jnp.float32
BF16 = jnp.bfloat16
AXES = ("dp", "rep")
LANES = 128
TILE = 512
ROWS = TILE // LANES


def dot(left, right):
    return jnp.dot(left, right, preferred_element_type=F32)


def dot_nt(left, right):
    return lax.dot_general(left, right, (((1,), (1,)), ((), ())), preferred_element_type=F32)


def pack(vector):
    return jnp.concatenate(
        [vector[:, LANES * k : LANES * (k + 1)] for k in range(vector.shape[1] // LANES)], axis=0
    )


def unpack(rows):
    return jnp.concatenate([rows[k : k + 1, :] for k in range(rows.shape[0])], axis=1)


def col_sum(values):
    return jnp.sum(values, axis=0, keepdims=True)


def stat_tile(first, second):
    return jnp.concatenate([pack(col_sum(first)), pack(col_sum(second))], axis=0)


def coefficients(stat_ref, count_ref, param_ref, factor=1.0):
    stat, param = stat_ref[...], param_ref[...]
    count = count_ref[0:ROWS, :] * factor
    average = stat[0:ROWS] / count
    inverse = lax.rsqrt(stat[ROWS : 2 * ROWS] / count - average * average + EPSILON)
    return (
        unpack(average),
        unpack(inverse),
        unpack(param[0:ROWS]),
        unpack(param[ROWS : 2 * ROWS]),
    )


def back_coefficients(grad_rows_shift, grad_rows_gain, count_ref, factor=1.0):
    count = count_ref[0:ROWS, :] * factor
    return unpack(grad_rows_shift / count), unpack(grad_rows_gain / count)


def logistic(values):
    return 0.5 * jnp.tanh(0.5 * values) + 0.5


def silu(values):
    return values * logistic(values)


def slope(values):
    gate = logistic(values)
    return gate * (1.0 + values * (1.0 - gate))


def column(mask_ref):
    return mask_ref[:, 0:1]


def pixel_ids(pixels, width):
    return lax.broadcasted_iota(jnp.int32, (pixels, 1), 0)


def shift_cols(values, step, width):
    pixels = values.shape[0]
    place = lax.rem(pixel_ids(pixels, width), width)
    rolled = pltpu.roll(values, (-step) % pixels, 0)
    keep = place < width - step if step > 0 else place >= -step
    return jnp.where(keep, rolled, 0.0)


def shift_rows(values, step, width, height):
    pixels = values.shape[0]
    place = lax.rem(lax.div(pixel_ids(pixels, width), width), height)
    rolled = pltpu.roll(values, (-step * width) % pixels, 0)
    keep = place < height - step if step > 0 else place >= -step
    return jnp.where(keep, rolled, 0.0)


def full(shape):
    zeros = (0,) * len(shape)
    return pl.BlockSpec(shape, lambda *_: zeros)


def cols(rows, width):
    return pl.BlockSpec((rows, width), lambda n, *_: (0, n))


def tile_at(index, rows=8):
    return pl.BlockSpec((rows, LANES), lambda *_: (index, 0))


def tile_n(offset=0, rows=8):
    return pl.BlockSpec((rows, LANES), lambda n, *_: (offset + n, 0))


def call(kernel, grid, in_specs, out_specs, out_shape, scratch=(), mib=40, flops=0, nbytes=0):
    return pl.pallas_call(
        kernel,
        grid=grid,
        in_specs=in_specs,
        out_specs=out_specs,
        out_shape=out_shape,
        scratch_shapes=scratch,
        compiler_params=pltpu.CompilerParams(
            vmem_limit_bytes=mib << 20, dimension_semantics=("arbitrary",) * len(grid)
        ),
        cost_estimate=pl.CostEstimate(flops=flops, bytes_accessed=nbytes, transcendentals=0),
    )


def shaped(shape, dtype=F32):
    return jax.ShapeDtypeStruct(shape, dtype)


def reduce_kernel(quarter, x_ref, perm_ref, mask_ref, all_mask_ref, w_ref, xp_ref, pre_ref, stat_ref, acc_ref):
    step = pl.program_id(0)
    mask = column(mask_ref)
    masking = jnp.concatenate([mask] * 4, axis=0)
    planes = (dot(perm_ref[...], x_ref[...]) * masking).astype(BF16)
    pre = dot(planes, w_ref[...])
    for q in range(4):
        xp_ref[q] = planes[q * quarter : (q + 1) * quarter]
        pre_ref[q] = pre[q * quarter : (q + 1) * quarter]

    @pl.when(step == 0)
    def _():
        acc_ref[...] = jnp.zeros_like(acc_ref)

    acc_ref[0:1, :] += col_sum(pre)
    acc_ref[1:2, :] += col_sum(pre * pre)

    @pl.when(step == pl.num_programs(0) - 1)
    def _():
        stat_ref[0:8, :] = jnp.concatenate([pack(acc_ref[0:1, :]), pack(acc_ref[1:2, :])], axis=0)
        stat_ref[8:16, :] = jnp.broadcast_to(col_sum(all_mask_ref[...]), (8, LANES))


def product_kernel(x_ref, w_ref, out_ref, stat_ref):
    pre = dot(x_ref[0], w_ref[...])
    out_ref[...] = pre
    stat_ref[...] = stat_tile(pre, pre * pre)


def spatial_kernel(width, height, pre_ref, stat_ref, count_ref, param_ref, mask_ref, w_ref, act_ref, out_ref, out_stat_ref, y_ref):
    r = pl.program_id(0)
    mask = column(mask_ref)

    @pl.when(r == 0)
    def _():
        average, inverse, gain, shift = coefficients(stat_ref, count_ref, param_ref, 4.0)
        for q in range(4):
            norm = (pre_ref[q] - average) * inverse * gain + shift
            act_ref[q] = (silu(norm) * mask).astype(BF16)

    row_parity = jnp.where(r == 1, 0, 1)
    row_shift = jnp.where(r == 0, 1, 0)
    even, odd = act_ref[2 * row_parity], act_ref[2 * row_parity + 1]
    straight = dot(even, w_ref[0, 1]) + dot(odd, w_ref[0, 2])
    moved = dot(odd, w_ref[0, 0])

    @pl.when(r < 2)
    def _():
        y_ref[2 * row_shift] = straight
        y_ref[2 * row_shift + 1] = moved

    @pl.when(r == 2)
    def _():
        upper = y_ref[2] + shift_cols(y_ref[3], -1, width)
        lower = y_ref[0] + straight + shift_cols(y_ref[1] + moved, -1, width)
        pre = lower + shift_rows(upper, -1, width, height)
        out_ref[...] = pre
        masked = pre * mask
        out_stat_ref[...] = stat_tile(masked, masked * pre)


def expand_kernel(pre_ref, stat_ref, count_ref, param_ref, mask_ref, w_ref, act_ref, out_ref, out_stat_ref):
    @pl.when(pl.program_id(0) == 0)
    def _():
        average, inverse, gain, shift = coefficients(stat_ref, count_ref, param_ref)
        norm = (pre_ref[...] - average) * inverse * gain + shift
        act_ref[...] = (silu(norm) * column(mask_ref)).astype(BF16)

    pre = dot(act_ref[...], w_ref[...])
    out_ref[...] = pre
    out_stat_ref[...] = stat_tile(pre, pre * pre)


def join_kernel(pe_ref, ps_ref, se_ref, ss_ref, count_ref, qe_ref, qs_ref, mask_ref, w_ref, first_ref, out_ref, out_stat_ref):
    n = pl.program_id(0)
    average_e, inverse_e, gain_e, shift_e = coefficients(se_ref, count_ref, qe_ref)
    average_s, inverse_s, gain_s, shift_s = coefficients(ss_ref, count_ref, qs_ref)
    joined = (pe_ref[...] - average_e) * inverse_e * gain_e + shift_e
    joined += (ps_ref[...] - average_s) * inverse_s * gain_s + shift_s
    first = (silu(joined) * column(mask_ref)).astype(BF16)
    first_ref[...] = first
    part = dot(first, w_ref[...])

    @pl.when(n == 0)
    def _():
        out_ref[...] = part

    @pl.when(n > 0)
    def _():
        out_ref[...] += part

    @pl.when(n == pl.num_programs(0) - 1)
    def _():
        pre = out_ref[...]
        out_stat_ref[...] = stat_tile(pre, pre * pre)


def store_padded(target_ref, values, step, width, height, images):
    area = width * height
    channels = values.shape[1]
    zeros = jnp.zeros((width, channels), BF16)
    for k in range(3):
        moved = values if k == 1 else shift_cols(values, step * (k - 1), width)
        moved = moved.astype(BF16)
        for b in range(images):
            target_ref[k, b, 0:width, :] = zeros
            target_ref[k, b, area + width : area + 2 * width, :] = zeros
            target_ref[k, b, width : area + width, :] = moved[b * area : (b + 1) * area]


def window_rows(ref, k, first, area, images):
    return jnp.concatenate([ref[k, b, pl.ds(first, area), :] for b in range(images)], axis=0)


def window_kernel(width, height, images, pre_ref, stat_ref, count_ref, param_ref, mask_ref, w_ref, act_ref, out_ref, out_stat_ref, pad_ref):
    r = pl.program_id(0)

    @pl.when(r == 0)
    def _():
        average, inverse, gain, shift = coefficients(stat_ref, count_ref, param_ref)
        norm = (pre_ref[...] - average) * inverse * gain + shift
        act = silu(norm) * column(mask_ref)
        act_ref[...] = act.astype(BF16)
        store_padded(pad_ref, act, 1, width, height, images)

    first = pl.multiple_of(r * width, width)
    part = dot(window_rows(pad_ref, 0, first, width * height, images), w_ref[0, 0])
    for k in (1, 2):
        part += dot(window_rows(pad_ref, k, first, width * height, images), w_ref[0, k])

    @pl.when(r == 0)
    def _():
        out_ref[...] = part

    @pl.when(r > 0)
    def _():
        out_ref[...] += part

    @pl.when(r == 2)
    def _():
        pre = out_ref[...]
        masked = pre * column(mask_ref)
        out_stat_ref[...] = stat_tile(masked, masked * pre)


def final_kernel(pre_ref, stat_ref, count_ref, param_ref, mask_ref, first_ref, cot_ref, out_ref, grad_ref, sum_ref):
    average, inverse, gain, shift = coefficients(stat_ref, count_ref, param_ref)
    mask = column(mask_ref)
    hat = (pre_ref[...] - average) * inverse
    final = hat * gain + shift + first_ref[...].astype(F32)
    gate = logistic(final)
    out_ref[...] = (final * gate * mask).astype(BF16)
    grad = cot_ref[...].astype(F32) * mask * (gate * (1.0 + final * (1.0 - gate)))
    grad_ref[...] = grad
    sum_ref[...] = stat_tile(grad, grad * hat)


def norm_back(grad, hat, scale, shift_term, gain_term, mask):
    return ((grad - mask * (shift_term + hat * gain_term)) * scale).astype(BF16)


def widen_back_kernel(
    grad_ref, pre_ref, stat_ref, gsum_ref, count_ref, param_ref, mask_ref, w_ref, in_ref, in_stat_ref, in_param_ref,
    gpre_ref, out_ref, sum_ref,
):
    n = pl.program_id(0)
    mask = column(mask_ref)
    average, inverse, gain, _ = coefficients(stat_ref, count_ref, param_ref)
    gsum = gsum_ref[...]
    shift_term, gain_term = back_coefficients(gsum[0:ROWS], gsum[ROWS : 2 * ROWS], count_ref)
    hat = (pre_ref[...] - average) * inverse
    gpre = norm_back(grad_ref[...], hat, inverse * gain, shift_term, gain_term, mask)
    gpre_ref[...] = gpre
    part = dot_nt(gpre, w_ref[...])

    @pl.when(n == 0)
    def _():
        out_ref[...] = part

    @pl.when(n > 0)
    def _():
        out_ref[...] += part

    @pl.when(n == pl.num_programs(0) - 1)
    def _():
        finish_back(in_ref[...], in_stat_ref, count_ref, in_param_ref, mask, out_ref, sum_ref)


def finish_back(pre, stat_ref, count_ref, param_ref, mask, out_ref, sum_ref):
    average, inverse, gain, shift = coefficients(stat_ref, count_ref, param_ref)
    hat = (pre - average) * inverse
    grad = out_ref[...] * mask * slope(hat * gain + shift)
    out_ref[...] = grad
    sum_ref[...] = stat_tile(grad, grad * hat)


def pre_grad(grad_ref, pre_ref, stat_ref, gsum_ref, count_ref, param_ref, mask):
    average, inverse, gain, _ = coefficients(stat_ref, count_ref, param_ref)
    gsum = gsum_ref[...]
    shift_term, gain_term = back_coefficients(gsum[0:ROWS], gsum[ROWS : 2 * ROWS], count_ref)
    hat = (pre_ref[...] - average) * inverse
    return norm_back(grad_ref[...], hat, inverse * gain, shift_term, gain_term, mask)


def window_back_kernel(
    width, height, images,
    grad_ref, pre_ref, stat_ref, gsum_ref, count_ref, param_ref, mask_ref, w_ref, in_ref, in_stat_ref, in_param_ref,
    pad_ref, out_ref, sum_ref,
):
    r = pl.program_id(0)
    mask = column(mask_ref)

    @pl.when(r == 0)
    def _():
        gpre = pre_grad(grad_ref, pre_ref, stat_ref, gsum_ref, count_ref, param_ref, mask)
        store_padded(pad_ref, gpre.astype(F32), -1, width, height, images)

    first = pl.multiple_of((2 - r) * width, width)
    part = dot_nt(window_rows(pad_ref, 0, first, width * height, images), w_ref[0, 0])
    for k in (1, 2):
        part += dot_nt(window_rows(pad_ref, k, first, width * height, images), w_ref[0, k])

    @pl.when(r == 0)
    def _():
        out_ref[...] = part

    @pl.when(r > 0)
    def _():
        out_ref[...] += part

    @pl.when(r == 2)
    def _():
        finish_back(in_ref[...], in_stat_ref, count_ref, in_param_ref, mask, out_ref, sum_ref)


def squeeze_back_kernel(
    grad_ref, pre_ref, stat_ref, gsum_ref, count_ref, param_ref, mask_ref, w_ref,
    gfinal_ref, pe_ref, ps_ref, se_ref, ss_ref, qe_ref, qs_ref,
    gpre_ref, gj_ref, sum_ref,
):
    mask = column(mask_ref)

    @pl.when(pl.program_id(0) == 0)
    def _():
        gpre_ref[...] = pre_grad(grad_ref, pre_ref, stat_ref, gsum_ref, count_ref, param_ref, mask)

    gfirst = gfinal_ref[...] + dot_nt(gpre_ref[...], w_ref[...])
    average_e, inverse_e, gain_e, shift_e = coefficients(se_ref, count_ref, qe_ref)
    average_s, inverse_s, gain_s, shift_s = coefficients(ss_ref, count_ref, qs_ref)
    hat_e = (pe_ref[...] - average_e) * inverse_e
    hat_s = (ps_ref[...] - average_s) * inverse_s
    joined = hat_e * gain_e + shift_e + (hat_s * gain_s + shift_s)
    grad = gfirst * mask * slope(joined)
    gj_ref[...] = grad
    sum_ref[...] = jnp.concatenate(
        [stat_tile(grad, grad * hat_e), pack(col_sum(grad * hat_s)), jnp.zeros((ROWS, LANES), F32)], axis=0
    )


def expand_back_kernel(
    gj_ref, pe_ref, ps_ref, se_ref, ss_ref, gsum_ref, count_ref, qe_ref, qs_ref, mask_ref, w_ref,
    in_ref, in_stat_ref, in_param_ref,
    ge_ref, gs_ref, out_ref, sum_ref,
):
    n = pl.program_id(0)
    mask = column(mask_ref)
    average_e, inverse_e, gain_e, _ = coefficients(se_ref, count_ref, qe_ref)
    average_s, inverse_s, gain_s, _ = coefficients(ss_ref, count_ref, qs_ref)
    gsum = gsum_ref[...]
    shift_term, gain_e_term = back_coefficients(gsum[0:ROWS], gsum[ROWS : 2 * ROWS], count_ref)
    _, gain_s_term = back_coefficients(gsum[0:ROWS], gsum[2 * ROWS : 3 * ROWS], count_ref)
    grad = gj_ref[...]
    hat_e = (pe_ref[...] - average_e) * inverse_e
    hat_s = (ps_ref[...] - average_s) * inverse_s
    ge = norm_back(grad, hat_e, inverse_e * gain_e, shift_term, gain_e_term, mask)
    ge_ref[...] = ge
    gs_ref[...] = norm_back(grad, hat_s, inverse_s * gain_s, shift_term, gain_s_term, mask)
    part = dot_nt(ge, w_ref[...])

    @pl.when(n == 0)
    def _():
        out_ref[...] = part

    @pl.when(n > 0)
    def _():
        out_ref[...] += part

    @pl.when(n == pl.num_programs(0) - 1)
    def _():
        finish_back(in_ref[...], in_stat_ref, count_ref, in_param_ref, mask, out_ref, sum_ref)


def spatial_back_kernel(
    width, height,
    grad_ref, pre_ref, stat_ref, gsum_ref, count_ref, param_ref, mask_ref, w_ref, in_ref, in_stat_ref, in_param_ref,
    shift_ref, out_ref, sum_ref,
):
    r = pl.program_id(0)
    mask = column(mask_ref)

    @pl.when(r == 0)
    def _():
        gpre = pre_grad(grad_ref, pre_ref, stat_ref, gsum_ref, count_ref, param_ref, mask).astype(F32)
        below = shift_rows(gpre, 1, width, height)
        shift_ref[0] = gpre.astype(BF16)
        shift_ref[1] = shift_cols(gpre, 1, width).astype(BF16)
        shift_ref[2] = below.astype(BF16)
        shift_ref[3] = shift_cols(below, 1, width).astype(BF16)

    row_parity = jnp.where(r == 1, 0, 1)
    row_shift = jnp.where(r == 0, 1, 0)
    straight, moved = shift_ref[2 * row_shift], shift_ref[2 * row_shift + 1]
    even = dot_nt(straight, w_ref[0, 1])
    odd = dot_nt(moved, w_ref[0, 0]) + dot_nt(straight, w_ref[0, 2])

    @pl.when(r < 2)
    def _():
        out_ref[2 * row_parity] = even
        out_ref[2 * row_parity + 1] = odd

    @pl.when(r == 2)
    def _():
        out_ref[2] += even
        out_ref[3] += odd
        average, inverse, gain, shift = coefficients(in_stat_ref, count_ref, in_param_ref, 4.0)
        total = total_hat = jnp.zeros((1, out_ref.shape[2]), F32)
        for q in range(4):
            hat = (in_ref[q] - average) * inverse
            grad = out_ref[q] * mask * slope(hat * gain + shift)
            out_ref[q] = grad
            total += col_sum(grad)
            total_hat += col_sum(grad * hat)
        sum_ref[...] = jnp.concatenate([pack(total), pack(total_hat)], axis=0)


def short_back_kernel(g_ref, w_ref, out_ref):
    part = dot_nt(g_ref[...], w_ref[...])

    @pl.when(pl.program_id(0) == 0)
    def _():
        out_ref[...] = part

    @pl.when(pl.program_id(0) > 0)
    def _():
        out_ref[...] += part


def reduce_back_kernel(
    quarter, grad_ref, pre_ref, stat_ref, gsum_ref, count_ref, param_ref, mask_ref, w_ref, short_ref, perm_ref,
    gpre_ref, out_ref,
):
    mask = column(mask_ref)
    masking = jnp.concatenate([mask] * 4, axis=0)
    average, inverse, gain, _ = coefficients(stat_ref, count_ref, param_ref, 4.0)
    gsum = gsum_ref[...]
    shift_term, gain_term = back_coefficients(gsum[0:ROWS], gsum[ROWS : 2 * ROWS], count_ref, 4.0)
    grad = jnp.concatenate([grad_ref[q] for q in range(4)], axis=0)
    pre = jnp.concatenate([pre_ref[q] for q in range(4)], axis=0)
    hat = (pre - average) * inverse
    gpre = norm_back(grad, hat, inverse * gain, shift_term, gain_term, masking)
    for q in range(4):
        gpre_ref[q] = gpre[q * quarter : (q + 1) * quarter]
    image = dot_nt(gpre, w_ref[...])
    image = jnp.concatenate([image[0:quarter] + short_ref[...], image[quarter:]], axis=0)
    image = (image * masking).astype(BF16)
    out_ref[...] = dot(perm_ref[...], image).astype(BF16)


def outer_kernel(pick, left_blocks, core_ref, *refs):
    left_ref, right_ref = refs[0], refs[1]
    keep_ref, send_ref, turned_ref = refs[-3], refs[-2], refs[-1]
    b = pl.program_id(0)

    @pl.when(lax.rem(b, left_blocks[1]) == 0)
    def _():
        left = left_ref[...] if len(left_ref.shape) == 2 else left_ref[0]
        turned_ref[...] = left.T

    half = TILE // 2
    right = pick(right_ref, b)
    core = core_ref[0]
    keep_ref[...] = dot(turned_ref[pl.ds(pl.multiple_of(core * half, half), half), :], right)
    send_ref[...] = dot(turned_ref[pl.ds(pl.multiple_of((1 - core) * half, half), half), :], right)


def outer(core, left, left_spec, right, right_spec, pick, blocks, per_left, place, total, into):
    half = TILE // 2
    pixels = left_spec.block_shape[-2]
    shape = shaped((total * half, TILE))
    out_spec = pl.BlockSpec((half, TILE), lambda b, *_: (place + b, 0))
    aliases = {} if into is None else {3: 0, 4: 1}
    extra = () if into is None else tuple(into)
    return pl.pallas_call(
        functools.partial(outer_kernel, pick, (None, per_left)),
        grid_spec=pltpu.PrefetchScalarGridSpec(
            num_scalar_prefetch=1,
            grid=(blocks,),
            in_specs=[left_spec, right_spec] + [pl.BlockSpec(memory_space=pl.ANY)] * len(extra),
            out_specs=[out_spec, out_spec],
            scratch_shapes=[pltpu.VMEM((TILE, pixels), BF16)],
        ),
        out_shape=[shape, shape],
        input_output_aliases=aliases,
        compiler_params=pltpu.CompilerParams(
            vmem_limit_bytes=24 << 20, dimension_semantics=("arbitrary",)
        ),
        cost_estimate=pl.CostEstimate(
            flops=2 * blocks * pixels * TILE * TILE,
            bytes_accessed=blocks * TILE * TILE * 4,
            transcendentals=0,
        ),
    )(core, left, right, *extra)


def assemble_kernel(core_ref, mine_ref, other_ref, out_ref):
    half = TILE // 2
    core = core_ref[0]
    out_ref[pl.ds(pl.multiple_of(core * half, half), half), :] = mine_ref[...]
    out_ref[pl.ds(pl.multiple_of((1 - core) * half, half), half), :] = other_ref[...]


def assemble(core, mine, other, place, blocks, shape, where):
    half = TILE // 2
    in_spec = pl.BlockSpec((half, TILE), lambda b, *_: (place + b, 0))
    return pl.pallas_call(
        assemble_kernel,
        grid_spec=pltpu.PrefetchScalarGridSpec(
            num_scalar_prefetch=1,
            grid=(blocks,),
            in_specs=[in_spec, in_spec],
            out_specs=pl.BlockSpec((TILE, TILE), lambda b, *_: where(b)),
        ),
        out_shape=shaped(shape),
        compiler_params=pltpu.CompilerParams(
            vmem_limit_bytes=16 << 20, dimension_semantics=("arbitrary",)
        ),
        cost_estimate=pl.CostEstimate(
            flops=0, bytes_accessed=2 * blocks * TILE * TILE * 4, transcendentals=0
        ),
    )(core, mine, other)


def bits_of(first, size):
    found = []
    while size > 1:
        found.append(first)
        first, size = first * 2, size // 2
    return found


def mesh_bits(dp, rep):
    side = int(round(dp**0.5))
    if side * side == dp:
        return 1, bits_of(rep, side), bits_of(rep * side, side), bits_of(2, rep // 2)
    side = int(round((dp // 2) ** 0.5))
    return rep, bits_of(2 * rep, side), bits_of(2 * rep * side, side), bits_of(1, rep)


def swap(values, bit, devices):
    return lax.ppermute(values, AXES, [(i, i ^ bit) for i in range(devices)])


def sync_all(tile, devices):
    copies = jnp.broadcast_to(tile[None], (devices,) + tile.shape)
    return jnp.sum(lax.all_to_all(copies, AXES, 0, 0, tiled=True), axis=0)


def sync_hops(tile, bits, devices):
    for bit in bits:
        tile = tile + swap(tile, bit, devices)
    return tile


def device_bit(flat, bit):
    return lax.rem(lax.div(flat, bit), 2)


def scatter_sum(keep, send, flat, core, order, devices):
    received = swap(send, core, devices)
    for bit in order:
        rows = keep.shape[0] // 2
        own = device_bit(flat, bit)
        start, away = own * rows, (1 - own) * rows
        send = lax.dynamic_slice_in_dim(keep, away, rows) + lax.dynamic_slice_in_dim(received, away, rows)
        keep = lax.dynamic_slice_in_dim(keep, start, rows) + lax.dynamic_slice_in_dim(received, start, rows)
        received = swap(send, bit, devices)
    return keep + received


def gather_back(shard, flat, core, order, devices):
    for bit in reversed(order):
        other = swap(shard, bit, devices)
        own = device_bit(flat, bit)
        shard = jnp.where(
            own == 0, jnp.concatenate([shard, other], axis=0), jnp.concatenate([other, shard], axis=0)
        )
    return shard, swap(shard, core, devices)


def permutation(width):
    size = 8 * 2 * width
    matrix = np.zeros((size, size), np.float32)
    place = 0
    for row_parity in range(2):
        for col_parity in range(2):
            for i in range(4):
                for j in range(width):
                    matrix[place, (2 * i + row_parity) * 2 * width + 2 * j + col_parity] = 1.0
                    place += 1
    return matrix


def param_tiles(gain, shift):
    blocks = gain.shape[0] // TILE
    pair = jnp.stack([gain.reshape(blocks, ROWS, LANES), shift.reshape(blocks, ROWS, LANES)], axis=1)
    return pair.reshape(blocks * 8, LANES)


def vector(tiles, first, step):
    return tiles.reshape(-1, step, LANES)[:, first : first + ROWS].reshape(-1)


def on_device(dp, rep, *arrays):
    (image_input, heights, widths, w_reduce, w_spatial, w_expand, w_shortcut,
     gain_reduce, shift_reduce, gain_spatial, shift_spatial, gain_expand, shift_expand,
     gain_shortcut, shift_shortcut, w_squeeze, w_window, w_widen,
     gain_squeeze, shift_squeeze, gain_window, shift_window, gain_widen, shift_widen, cotangent) = arrays
    images, height, width, c_out = cotangent.shape
    c_in, mid = w_reduce.shape
    pixels = images * height * width
    quarter = 64
    steps = pixels // quarter
    blocks = c_out // TILE
    devices = dp * rep
    core_bit, x_bits, y_bits, z_bits = mesh_bits(dp, rep)
    hop_bits = [core_bit] + y_bits + x_bits + z_bits
    flat = lax.axis_index(AXES)
    core = device_bit(flat, core_bit).astype(jnp.int32).reshape(1)
    sync = functools.partial(sync_all, devices=devices)
    sync_wide = functools.partial(sync_hops, bits=hop_bits, devices=devices)

    row_ids = lax.broadcasted_iota(jnp.int32, (1, height, 1, LANES), 1)
    col_ids = lax.broadcasted_iota(jnp.int32, (1, 1, width, LANES), 2)
    inside = (row_ids < heights[:, None, None, None]) & (col_ids < widths[:, None, None, None])
    mask = jnp.where(inside, 1.0, 0.0).astype(F32).reshape(pixels, LANES)
    params = jnp.concatenate(
        [
            param_tiles(gain_reduce, shift_reduce), param_tiles(gain_spatial, shift_spatial),
            param_tiles(gain_squeeze, shift_squeeze), param_tiles(gain_window, shift_window),
            param_tiles(gain_expand, shift_expand), param_tiles(gain_shortcut, shift_shortcut),
            param_tiles(gain_widen, shift_widen),
        ],
        axis=0,
    )
    p_reduce, p_spatial, p_squeeze, p_window = (tile_at(k) for k in range(4))
    p_expand, p_short, p_widen = (tile_n(4 + blocks * k) for k in range(3))
    turn = permutation(width)
    perm, perm_back = jnp.asarray(turn, BF16), jnp.asarray(turn.T.copy(), BF16)
    image = image_input.reshape(images * 4 * height * width, c_in)
    cot = cotangent.reshape(pixels, c_out)

    mask_spec, wide_f32 = full((pixels, LANES)), shaped((pixels, c_out))
    mid_f32, mid_spec = shaped((pixels, mid)), full((pixels, mid))
    wide_spec, tap_spec = cols(pixels, TILE), pl.BlockSpec((1, 3, mid, mid), lambda r: (r, 0, 0, 0))
    plane_block = lambda c: pl.BlockSpec((4, quarter, c), lambda k: (0, k, 0))
    one_tile, wide_tiles = shaped((8, LANES)), shaped((8 * blocks, LANES))
    padded = (3, images, (height + 2) * width, mid)

    planes, pre_reduce, stat = call(
        functools.partial(reduce_kernel, quarter),
        (steps,),
        [
            pl.BlockSpec((4 * quarter, c_in), lambda k: (k, 0)), full(perm.shape),
            pl.BlockSpec((quarter, LANES), lambda k: (k, 0)), mask_spec, full((c_in, mid)),
        ],
        [plane_block(c_in), plane_block(mid), full((16, LANES))],
        [shaped((4, pixels, c_in), BF16), shaped((4, pixels, mid)), shaped((16, LANES))],
        [pltpu.VMEM((8, mid), F32)],
        flops=8 * pixels * c_in * mid, nbytes=8 << 20,
    )(image, perm, mask, mask, w_reduce)
    s_reduce = sync(stat)
    count_spec = tile_at(1)

    pre_short, stat_short = call(
        product_kernel,
        (blocks,),
        [pl.BlockSpec((1, pixels, c_in), lambda n: (0, 0, 0)), cols(c_in, TILE)],
        [wide_spec, tile_n()],
        [wide_f32, wide_tiles],
        flops=2 * pixels * c_in * c_out, nbytes=6 << 20,
    )(planes, w_shortcut)

    act_reduce, pre_spatial, stat = call(
        functools.partial(spatial_kernel, width, height),
        (3,),
        [full((4, pixels, mid)), tile_at(0), count_spec, p_reduce, mask_spec, tap_spec],
        [full((4, pixels, mid)), mid_spec, full((8, LANES))],
        [shaped((4, pixels, mid), BF16), mid_f32, one_tile],
        [pltpu.VMEM((4, pixels, mid), F32)],
        flops=18 * pixels * mid * mid, nbytes=8 << 20,
    )(pre_reduce, s_reduce, s_reduce, params, mask, w_spatial)
    s_spatial = sync(stat)

    def widen_out(pre, stat, p_spec, weights):
        return call(
            expand_kernel,
            (blocks,),
            [mid_spec, tile_at(0), count_spec, p_spec, mask_spec, cols(mid, TILE)],
            [mid_spec, wide_spec, tile_n()],
            [shaped((pixels, mid), BF16), wide_f32, wide_tiles],
            flops=2 * pixels * mid * c_out, nbytes=5 << 20,
        )(pre, stat, s_reduce, params, mask, weights)

    act_spatial, pre_expand, stat = widen_out(pre_spatial, s_spatial, p_spatial, w_expand)
    s_both = sync_wide(jnp.concatenate([stat, stat_short], axis=0))
    e_spec, s_spec = tile_n(), tile_n(blocks)

    first_out, pre_squeeze, stat = call(
        join_kernel,
        (blocks,),
        [
            wide_spec, wide_spec, e_spec, s_spec, count_spec, p_expand, p_short, mask_spec,
            pl.BlockSpec((TILE, mid), lambda n: (n, 0)),
        ],
        [wide_spec, mid_spec, full((8, LANES))],
        [shaped((pixels, c_out), BF16), mid_f32, one_tile],
        flops=2 * pixels * mid * c_out, nbytes=8 << 20,
    )(pre_expand, pre_short, s_both, s_both, s_reduce, params, params, mask, w_squeeze)
    s_squeeze = sync(stat)

    act_squeeze, pre_window, stat = call(
        functools.partial(window_kernel, width, height, images),
        (3,),
        [mid_spec, tile_at(0), count_spec, p_squeeze, mask_spec, tap_spec],
        [mid_spec, mid_spec, full((8, LANES))],
        [shaped((pixels, mid), BF16), mid_f32, one_tile],
        [pltpu.VMEM(padded, BF16)],
        flops=18 * pixels * mid * mid, nbytes=6 << 20,
    )(pre_squeeze, s_squeeze, s_reduce, params, mask, w_window)
    s_window = sync(stat)

    act_window, pre_widen, stat = widen_out(pre_window, s_window, p_window, w_widen)
    s_widen = sync_wide(stat)

    block_out, grad_final, gsum = call(
        final_kernel,
        (blocks,),
        [wide_spec, tile_n(), count_spec, p_widen, mask_spec, wide_spec, wide_spec],
        [wide_spec, wide_spec, tile_n()],
        [shaped((pixels, c_out), BF16), wide_f32, wide_tiles],
        nbytes=7 << 20,
    )(pre_widen, s_widen, s_reduce, params, mask, first_out, cot)
    g_widen = sync_wide(gsum)

    gpre_widen, grad_window, gsum = call(
        widen_back_kernel,
        (blocks,),
        [
            wide_spec, wide_spec, tile_n(), tile_n(), count_spec, p_widen, mask_spec, cols(mid, TILE),
            mid_spec, tile_at(0), p_window,
        ],
        [wide_spec, mid_spec, full((8, LANES))],
        [shaped((pixels, c_out), BF16), mid_f32, one_tile],
        flops=2 * pixels * mid * c_out, nbytes=8 << 20,
    )(grad_final, pre_widen, s_widen, g_widen, s_reduce, params, mask, w_widen, pre_window, s_window, params)
    g_window = sync(gsum)

    gpad_window, grad_squeeze, gsum = call(
        functools.partial(window_back_kernel, width, height, images),
        (3,),
        [
            mid_spec, mid_spec, tile_at(0), tile_at(0), count_spec, p_window, mask_spec, tap_spec,
            mid_spec, tile_at(0), p_squeeze,
        ],
        [full(padded), mid_spec, full((8, LANES))],
        [shaped(padded, BF16), mid_f32, one_tile],
        flops=18 * pixels * mid * mid, nbytes=8 << 20,
    )(grad_window, pre_window, s_window, g_window, s_reduce, params, mask, w_window, pre_squeeze, s_squeeze, params)
    g_squeeze = sync(gsum)

    gpre_squeeze, grad_joined, gsum = call(
        squeeze_back_kernel,
        (blocks,),
        [
            mid_spec, mid_spec, tile_at(0), tile_at(0), count_spec, p_squeeze, mask_spec,
            pl.BlockSpec((TILE, mid), lambda n: (n, 0)),
            wide_spec, wide_spec, wide_spec, e_spec, s_spec, p_expand, p_short,
        ],
        [mid_spec, wide_spec, tile_n(rows=16)],
        [shaped((pixels, mid), BF16), wide_f32, shaped((16 * blocks, LANES))],
        flops=2 * pixels * mid * c_out, nbytes=11 << 20,
    )(
        grad_squeeze, pre_squeeze, s_squeeze, g_squeeze, s_reduce, params, mask, w_squeeze,
        grad_final, pre_expand, pre_short, s_both, s_both, params, params,
    )
    g_both = sync_wide(gsum)

    gpre_expand, gpre_short, grad_spatial, gsum = call(
        expand_back_kernel,
        (blocks,),
        [
            wide_spec, wide_spec, wide_spec, e_spec, s_spec, tile_n(rows=16), count_spec, p_expand, p_short,
            mask_spec, cols(mid, TILE), mid_spec, tile_at(0), p_spatial,
        ],
        [wide_spec, wide_spec, mid_spec, full((8, LANES))],
        [shaped((pixels, c_out), BF16), shaped((pixels, c_out), BF16), mid_f32, one_tile],
        flops=2 * pixels * mid * c_out, nbytes=11 << 20,
    )(
        grad_joined, pre_expand, pre_short, s_both, s_both, g_both, s_reduce, params, params, mask, w_expand,
        pre_spatial, s_spatial, params,
    )
    g_spatial = sync(gsum)

    gshift_spatial, grad_reduce, gsum = call(
        functools.partial(spatial_back_kernel, width, height),
        (3,),
        [
            mid_spec, mid_spec, tile_at(0), tile_at(0), count_spec, p_spatial, mask_spec, tap_spec,
            full((4, pixels, mid)), tile_at(0), p_reduce,
        ],
        [full((4, pixels, mid)), full((4, pixels, mid)), full((8, LANES))],
        [shaped((4, pixels, mid), BF16), shaped((4, pixels, mid)), one_tile],
        flops=18 * pixels * mid * mid, nbytes=12 << 20,
    )(grad_spatial, pre_spatial, s_spatial, g_spatial, s_reduce, params, mask, w_spatial, pre_reduce, s_reduce, params)
    g_reduce = sync(gsum)

    back_short = call(
        short_back_kernel,
        (blocks,),
        [wide_spec, cols(c_in, TILE)],
        full((pixels, c_in)),
        shaped((pixels, c_in)),
        flops=2 * pixels * c_in * c_out, nbytes=6 << 20,
    )(gpre_short, w_shortcut)

    gpre_reduce, image_grad = call(
        functools.partial(reduce_back_kernel, quarter),
        (steps,),
        [
            plane_block(mid), plane_block(mid), tile_at(0), tile_at(0), count_spec, p_reduce,
            pl.BlockSpec((quarter, LANES), lambda k: (k, 0)), full((c_in, mid)),
            pl.BlockSpec((quarter, c_in), lambda k: (k, 0)), full(perm.shape),
        ],
        [plane_block(mid), pl.BlockSpec((4 * quarter, c_in), lambda k: (k, 0))],
        [shaped((4, pixels, mid), BF16), shaped((images * 4 * height * width, c_in), BF16)],
        flops=8 * pixels * c_in * mid, nbytes=10 << 20,
    )(grad_reduce, pre_reduce, s_reduce, g_reduce, s_reduce, params, mask, w_reduce, back_short, perm_back)

    area = width * height

    def whole(ref, b):
        return ref[...]

    def window_taps(ref, b):
        r, c = lax.div(b, 3), lax.rem(b, 3)
        first = pl.multiple_of((2 - r) * width, width)
        return window_rows(ref, c, first, area, images)

    def spatial_taps(ref, b):
        r, c = lax.div(b, 3), lax.rem(b, 3)
        return ref[2 * jnp.where(r == 0, 1, 0) + jnp.where(c == 0, 1, 0)]

    def spatial_plane(b, *_):
        r, c = lax.div(b, 3), lax.rem(b, 3)
        return (2 * jnp.where(r == 1, 0, 1) + jnp.where(c == 1, 0, 1), 0, 0)

    in_blocks = c_in // TILE
    left_const = pl.BlockSpec((pixels, TILE), lambda b, *_: (0, 0))
    right_n = pl.BlockSpec((pixels, TILE), lambda b, *_: (0, b))
    made = outer(core, act_squeeze, left_const, gpad_window, full(padded), window_taps, 9, 9, 0, 9 + in_blocks * blocks, None)
    one = outer(
        core, planes.reshape(4 * pixels, c_in), pl.BlockSpec((pixels, TILE), lambda b, *_: (0, lax.div(b, blocks))),
        gpre_short, pl.BlockSpec((pixels, TILE), lambda b, *_: (0, lax.rem(b, blocks))),
        whole, in_blocks * blocks, blocks, 9, 9 + in_blocks * blocks, made,
    )
    made = outer(core, act_window, left_const, gpre_widen, right_n, whole, blocks, blocks, 0, 9 + blocks + in_blocks, None)
    made = outer(
        core, act_reduce, pl.BlockSpec((1, pixels, mid), spatial_plane), gshift_spatial, full((4, pixels, mid)),
        spatial_taps, 9, 1, blocks, 9 + blocks + in_blocks, made,
    )
    two = outer(
        core, planes.reshape(4 * pixels, c_in), pl.BlockSpec((4 * pixels, TILE), lambda b, *_: (0, b)),
        gpre_reduce.reshape(4 * pixels, mid), full((4 * pixels, mid)), whole, in_blocks, 1,
        9 + blocks, 9 + blocks + in_blocks, made,
    )
    made = outer(core, first_out, right_n, gpre_squeeze, full((pixels, mid)), whole, blocks, 1, 0, 2 * blocks, None)
    three = outer(core, act_spatial, left_const, gpre_expand, right_n, whole, blocks, blocks, blocks, 2 * blocks, made)

    order_one = x_bits + y_bits + z_bits
    order_two = y_bits + z_bits[:1] + x_bits + z_bits[1:]
    order_three = z_bits[:1] + x_bits + y_bits + z_bits[1:]
    orders = (order_one, order_two, order_three)
    shards = [
        scatter_sum(keep, send, flat, core_bit, order, devices)
        for (keep, send), order in zip((one, two, three), orders)
    ]
    halves = [gather_back(shard, flat, core_bit, order, devices) for shard, order in zip(shards, orders)]
    tall, flat_cols = lambda b: (b, 0), lambda b: (0, b)
    grad_w_window = assemble(core, *halves[0], 0, 9, (9 * mid, mid), tall).reshape(3, 3, mid, mid)
    grad_w_short = assemble(
        core, *halves[0], 9, in_blocks * blocks, (c_in, c_out), lambda b: (lax.div(b, blocks), lax.rem(b, blocks))
    )
    grad_w_widen = assemble(core, *halves[1], 0, blocks, (mid, c_out), flat_cols)
    grad_w_spatial = assemble(core, *halves[1], blocks, 9, (9 * mid, mid), tall).reshape(3, 3, mid, mid)
    grad_w_reduce = assemble(core, *halves[1], 9 + blocks, in_blocks, (c_in, mid), tall)
    grad_w_squeeze = assemble(core, *halves[2], 0, blocks, (c_out, mid), tall)
    grad_w_expand = assemble(core, *halves[2], blocks, blocks, (mid, c_out), flat_cols)

    shift_total = vector(g_both, 0, 16)
    return (
        block_out.reshape(cotangent.shape),
        image_grad.reshape(image_input.shape),
        grad_w_reduce,
        grad_w_spatial,
        grad_w_expand,
        grad_w_short,
        vector(g_reduce, ROWS, 8),
        vector(g_reduce, 0, 8),
        vector(g_spatial, ROWS, 8),
        vector(g_spatial, 0, 8),
        vector(g_both, ROWS, 16),
        shift_total,
        vector(g_both, 2 * ROWS, 16),
        shift_total,
        grad_w_squeeze,
        grad_w_window,
        grad_w_widen,
        vector(g_squeeze, ROWS, 8),
        vector(g_squeeze, 0, 8),
        vector(g_window, ROWS, 8),
        vector(g_window, 0, 8),
        vector(g_widen, ROWS, 8),
        vector(g_widen, 0, 8),
    )


def solution(mesh):
    split = P(AXES, None, None, None)
    return jax.shard_map(
        functools.partial(on_device, mesh.shape["dp"], mesh.shape["rep"]),
        mesh=mesh,
        in_specs=(split, P(AXES), P(AXES)) + (P(),) * 21 + (split,),
        out_specs=(split, split) + (P(),) * 21,
        check_vma=False,
    )
```

time: 1910 us -> 986 us (0.52)
  blocking collectives: 485 us -> 59.6 us
  waiting for transfers between devices: 804 us -> 563 us
  local copies, waits for them, and re-layouts: 287 us -> 89.5 us
  other arithmetic: 231 us -> 96.3 us
  Pallas kernels: 0 us -> 107 us
  matrix products: 71.7 us -> 0 us
  starting transfers between devices: 0.08 us -> 58 us
    unnamed x3 -> x0, waiting for transfers between devices: 604 us -> none
    ppermute x0 -> x50, waiting for transfers between devices: none -> 552 us  [swap(): return lax.ppermute(values, AXES, [(i, i ^ bit) for i in range(devices)])]
    psum x12 -> x0, blocking collectives: 485 us -> none  [the longest x1 42.2 us: on_device(): lax.psum((sum_reduce, square_reduce, local_count), ('dp', 'rep'))]
    all_gather x1 -> x0, waiting for transfers between devices: 200 us -> none  [on_device(): all_whole = lax.all_gather(all_shard, ('dp', 'rep'), axis=0, tiled=True)]
    scatter-add x12 -> x0, other arithmetic: 166 us -> none  [the longest x11 147 us: tap_scatter(): padded = padded.at[:, row_tap:row_tap + stride * out_rows:stride, col_tap...]
    slice x32 -> x2, local copies, waits for them, and re-layouts: 160 us -> 1.21 us  [vector(): return tiles.reshape(-1, step, LANES)[:, first:first + ROWS].reshape(-1)]
    pallas_call x0 -> x29, Pallas kernels: none -> 107 us  [the longest x7 35.2 us: assemble(): pl.pallas_call(assemble_kernel, grid_spec=pltpu.PrefetchScalarGridSpec(nu...]
    dot_general x21 -> x0, matrix products: 71.7 us -> none  [the longest x7 25.4 us: project(): jnp.einsum('bhwc,cd->bhwd', left, right, preferred_element_type=jnp.float32)]
  transfers between devices with their start and end apart: 2 -> 53, of which waited for: 2 -> 40; matrix products, arithmetic and copies ran while one was open for 2% -> 10% of each run, Pallas kernels for 0% -> 6%
where the time goes in v1:
time: 986 us; the launch traced here: 976 us
  waiting for transfers between devices  563 us (57%)
  Pallas kernels  107 us (11%)
  other arithmetic  96.3 us (10%)
  local copies, waits for them, and re-layouts  89.5 us (9%)
  blocking collectives  59.6 us (6%)
  starting transfers between devices  58 us (6%)
    ppermute x50, waiting for transfers between devices, swap(): return lax.ppermute(values, AXES, [(i, i ^ bit) for i in range(devices)])  552 us
    unnamed x214, local copies, waits for them, and re-layouts  83.9 us
    all_to_all x5, blocking collectives, sync_all(): return jnp.sum(lax.all_to_all(copies, AXES, 0, 0, tiled=True), axis=0)  59.6 us
    add x9, other arithmetic, scatter_sum(): lax.dynamic_slice_in_dim(keep, start, rows)  51.5 us
    ppermute x50, starting transfers between devices, swap(): return lax.ppermute(values, AXES, [(i, i ^ bit) for i in range(devices)])  44.5 us
    pallas_call x7, Pallas kernels, assemble(): pl.pallas_call(assemble_kernel, grid_spec=pltpu.PrefetchScalarGridSpec(nu...  35.2 us
    select_n x12, other arithmetic, gather_back(): jnp.where(own == 0, jnp.concatenate([shard, other], axis=0), jnp.concaten...  32.5 us
    pallas_call x7, Pallas kernels, outer(): pl.pallas_call(functools.partial(outer_kernel, pick, (None, per_left)), g...  28.2 us
  transfers between devices with their start and end apart: 53, of which 40 were waited for; matrix products, arithmetic and copies ran while one was open for 10% of the time, Pallas kernels for 6%

profile of v1, /device:TPU:0, one launch (start us, length us, event | category | flops | bytes accessed | tf_op | source)
XLA Modules:
  0.0 975.6 jit_solution(11784846409201429412)
XLA Ops:
  11.0 7.3 all-to-all-start
  18.7 9.9 %all-to-all-done = f32[32,16,128]{2,1,0:T(8,128)S(1)} async-done(((f32[32,16,128]{2,1,0:T(8,128)}), f32[32,16,128]{2,1,0:T(8,128)S(1)}, u32[]{:S(2)}, u32[]{:S(2)}) %all-to-all-start) | async-done | bytes 262176 | tf_op jit(solution)/shard_map/all_to_all | solution.py:601
  30.9 3.2 shard_map.435
  57.1 3.1 collective-permute-done.2
  61.0 3.1 collective-permute-done.3
  65.9 3.5 collective-permute-done.4
  74.9 13.1 %all_to_all.40 = f32[32,8,128]{2,1,0:T(8,128)} all-to-all(f32[32,8,128]{2,1,0:T(8,128)S(1)} %broadcast_in_dim.28), channel_id=1, replica_groups=mesh['dp'=8,'rep'=4] {'dp','rep'}, dimensions={0} | all-to-all | bytes 262144 | tf_op jit(solution)/shard_map/all_to_all | solution.py:601
  95.1 10.8 %all_to_all.41 = f32[32,8,128]{2,1,0:T(8,128)} all-to-all(f32[32,8,128]{2,1,0:T(8,128)S(1)} %broadcast_in_dim.29), channel_id=1, replica_groups=mesh['dp'=8,'rep'=4] {'dp','rep'}, dimensions={0} | all-to-all | bytes 262144 | tf_op jit(solution)/shard_map/all_to_all | solution.py:601
  120.1 3.7 collective-permute-done.8
  124.2 4.3 collective-permute-done.9
  140.1 3.7 collective-permute-done.13
  144.3 4.2 collective-permute-done.14
  153.1 10.8 %all_to_all.42 = f32[32,8,128]{2,1,0:T(8,128)} all-to-all(f32[32,8,128]{2,1,0:T(8,128)S(1)} %broadcast_in_dim.30), channel_id=1, replica_groups=mesh['dp'=8,'rep'=4] {'dp','rep'}, dimensions={0} | all-to-all | bytes 262144 | tf_op jit(solution)/shard_map/all_to_all | solution.py:601
  173.7 11.0 %all_to_all.43 = f32[32,8,128]{2,1,0:T(8,128)} all-to-all(f32[32,8,128]{2,1,0:T(8,128)S(1)} %broadcast_in_dim.31), channel_id=1, replica_groups=mesh['dp'=8,'rep'=4] {'dp','rep'}, dimensions={0} | all-to-all | bytes 262144 | tf_op jit(solution)/shard_map/all_to_all | solution.py:601
  193.0 3.5 shard_map.444
  204.4 3.2 collective-permute-done.17
  207.6 3.9 collective-permute-done.18
  214.0 5.6 shard_map.457
  224.4 3.2 shard_map.445
  232.4 5.1 shard_map.458
  237.5 3.6 copy-done.3
  241.1 14.0 %all_to_all.44 = f32[32,8,128]{2,1,0:T(8,128)} all-to-all(f32[32,8,128]{2,1,0:T(8,128)S(1)} %broadcast_in_dim.32), channel_id=1, replica_groups=mesh['dp'=8,'rep'=4] {'dp','rep'}, dimensions={0} | all-to-all | bytes 262144 | tf_op jit(solution)/shard_map/all_to_all | solution.py:601
  258.4 4.4 shard_map.446
  265.8 3.5 all-to-all-start.7
  280.1 6.0 shard_map.450
  286.0 3.1 copy-done
  293.0 4.0 shard_map.448
  296.9 3.2 copy-done.1
  303.2 3.2 copy-done.2
  306.7 12.0 %dynamic-slice_add_fusion.1 = (f32[2176,512]{1,0:T(8,128)}, f32[2176,512]{1,0:T(8,128)}) fusion(f32[4352,512]{1,0:T(8,128)} %collective-permute-done.40, s32[]{:T(128)S(6)} %select_n.238, f32[4352,512]{1,0:T(8,128)} %copy-done.3, s32[]{:T(128)S(6)} %select_n.240), kind=kLoop, calls=%fused_computation.4 | loop fusion | flops 2228224 | bytes 26738696 | tf_op jit(solution)/shard_map/add | solution.py:621
  320.4 10.7 %dynamic-slice_add_fusion.3 = (f32[1920,512]{1,0:T(8,128)}, f32[1920,512]{1,0:T(8,128)}) fusion(f32[3840,512]{1,0:T(8,128)} %collective-permute-done.20, s32[]{:T(128)S(6)} %select_n.206, f32[3840,512]{1,0:T(8,128)} %copy-done.2, s32[]{:T(128)S(6)} %select_n.208), kind=kLoop, calls=%fused_computation.8 | loop fusion | flops 1966080 | bytes 23592968 | tf_op jit(solution)/shard_map/add | solution.py:621
  332.6 84.8 %collective-permute-done.41 = f32[2176,512]{1,0:T(8,128)} collective-permute-done((f32[2176,512]{1,0:T(8,128)}, f32[2176,512]{1,0:T(8,128)}, u32[]{:S(2)}, u32[]{:S(2)}) %collective-permute-start.41) | collective-permute-done | bytes 4456480 | tf_op jit(solution)/shard_map/ppermute | solution.py:596
  417.4 6.1 dynamic-slice_add_fusion.5
  425.2 48.5 %collective-permute-done.42 = f32[1088,512]{1,0:T(8,128)} collective-permute-done((f32[1088,512]{1,0:T(8,128)}, f32[1088,512]{1,0:T(8,128)}, u32[]{:S(2)}, u32[]{:S(2)}) %collective-permute-start.42) | collective-permute-done | bytes 2228256 | tf_op jit(solution)/shard_map/ppermute | solution.py:596
  473.7 3.5 dynamic-slice_add_fusion.11
  478.9 6.3 dynamic-slice_add_fusion.9
  485.5 19.5 %collective-permute-done.43 = f32[544,512]{1,0:T(8,128)} collective-permute-done((f32[544,512]{1,0:T(8,128)}, f32[544,512]{1,0:T(8,128)}, u32[]{:S(2)}, u32[]{:S(2)}) %collective-permute-start.43) | collective-permute-done | bytes 1114144 | tf_op jit(solution)/shard_map/ppermute | solution.py:596
  516.9 39.0 %collective-permute-done.44 = f32[272,512]{1,0:T(8,128)} collective-permute-done((f32[272,512]{1,0:T(8,128)S(1)}, f32[272,512]{1,0:T(8,128)}, u32[]{:S(2)}, u32[]{:S(2)}) %collective-permute-start.44) | collective-permute-done | bytes 557088 | tf_op jit(solution)/shard_map/ppermute | solution.py:596
  557.2 3.6 collective-permute-start.45
  560.7 3.3 dynamic-slice_add_fusion.15
  565.5 17.8 %collective-permute-done.45 = f32[272,512]{1,0:T(8,128)} collective-permute-done((f32[272,512]{1,0:T(8,128)S(1)}, f32[272,512]{1,0:T(8,128)}, u32[]{:S(2)}, u32[]{:S(2)}) %collective-permute-start.45) | collective-permute-done | bytes 557088 | tf_op jit(solution)/shard_map/ppermute | solution.py:596
  589.0 31.1 %collective-permute-done.46 = f32[544,512]{1,0:T(8,128)} collective-permute-done((f32[544,512]{1,0:T(8,128)S(1)}, f32[544,512]{1,0:T(8,128)}, u32[]{:S(2)}, u32[]{:S(2)}) %collective-permute-start.46) | collective-permute-done | bytes 1114144 | tf_op jit(solution)/shard_map/ppermute | solution.py:596
  626.3 19.9 %collective-permute-done.25 = f32[240,512]{1,0:T(8,128)S(1)} collective-permute-done((f32[240,512]{1,0:T(8,128)S(1)}, f32[240,512]{1,0:T(8,128)S(1)}, u32[]{:S(2)}, u32[]{:S(2)}) %collective-permute-start.25) | collective-permute-done | bytes 491552 | tf_op jit(solution)/shard_map/ppermute | solution.py:596
  648.0 20.6 %collective-permute-done.26 = f32[480,512]{1,0:T(8,128)} collective-permute-done((f32[480,512]{1,0:T(8,128)S(1)}, f32[480,512]{1,0:T(8,128)}, u32[]{:S(2)}, u32[]{:S(2)}) %collective-permute-start.26) | collective-permute-done | bytes 983072 | tf_op jit(solution)/shard_map/ppermute | solution.py:596
  672.4 6.5 dynamic-slice_add_fusion.7
  679.0 5.6 maximum_select_fusion.2
  686.3 29.9 %collective-permute-done.27 = f32[960,512]{1,0:T(8,128)S(1)} collective-permute-done((f32[960,512]{1,0:T(8,128)S(1)}, f32[960,512]{1,0:T(8,128)S(1)}, u32[]{:S(2)}, u32[]{:S(2)}) %collective-permute-start.27) | collective-permute-done | bytes 1966112 | tf_op jit(solution)/shard_map/ppermute | solution.py:596
  719.2 40.4 %collective-permute-done.31 = f32[1024,512]{1,0:T(8,128)} collective-permute-done((f32[1024,512]{1,0:T(8,128)}, f32[1024,512]{1,0:T(8,128)}, u32[]{:S(2)}, u32[]{:S(2)}) %collective-permute-start.31) | collective-permute-done | bytes 2097184 | tf_op jit(solution)/shard_map/ppermute | solution.py:596
  764.0 40.2 %collective-permute-done.32 = f32[512,512]{1,0:T(8,128)S(1)} collective-permute-done((f32[512,512]{1,0:T(8,128)}, f32[512,512]{1,0:T(8,128)S(1)}, u32[]{:S(2)}, u32[]{:S(2)}) %collective-permute-start.32) | collective-permute-done | bytes 1048608 | tf_op jit(solution)/shard_map/ppermute | solution.py:596
  805.0 11.4 %collective-permute-done.33 = f32[256,512]{1,0:T(8,128)S(1)} collective-permute-done((f32[256,512]{1,0:T(8,128)S(1)}, f32[256,512]{1,0:T(8,128)S(1)}, u32[]{:S(2)}, u32[]{:S(2)}) %collective-permute-start.33) | collective-permute-done | bytes 524320 | tf_op jit(solution)/shard_map/ppermute | solution.py:596
  816.4 3.5 collective-permute-start.34
  819.8 9.2 collective-permute-done.34
  829.2 6.9 maximum_select_fusion.mine_ref
  836.3 7.0 collective-permute-done.35
  843.9 6.9 maximum_select_fusion.1.mine_ref
  850.8 6.3 collective-permute-done.36
  858.7 22.7 %collective-permute-done.37 = f32[512,512]{1,0:T(8,128)S(1)} collective-permute-done((f32[512,512]{1,0:T(8,128)S(1)}, f32[512,512]{1,0:T(8,128)S(1)}, u32[]{:S(2)}, u32[]{:S(2)}) %collective-permute-start.37) | collective-permute-done | bytes 1048608 | tf_op jit(solution)/shard_map/ppermute | solution.py:596
  883.1 44.6 %collective-permute-done.38 = f32[1024,512]{1,0:T(8,128)} collective-permute-done((f32[1024,512]{1,0:T(8,128)S(1)}, f32[1024,512]{1,0:T(8,128)}, u32[]{:S(2)}, u32[]{:S(2)}) %collective-permute-start.38) | collective-permute-done | bytes 2097184 | tf_op jit(solution)/shard_map/ppermute | solution.py:596
  927.6 4.5 maximum_select_fusion.3.mine_ref
  935.7 3.6 collective-permute-done.39.other_ref
  946.6 4.2 shard_map.462
  950.8 8.2 shard_map.453
  959.0 7.3 shard_map.459
  966.3 8.2 shard_map.461
  (371 shorter events, 208.7 us)
Async XLA Ops:
  11.0 17.5 %all-to-all-start = ((f32[32,16,128]{2,1,0:T(8,128)}), f32[32,16,128]{2,1,0:T(8,128)S(1)}, u32[]{:S(2)}, u32[]{:S(2)}) async-start(f32[32,16,128]{2,1,0:T(8,128)} %broadcast_in_dim.26), calls=%async_computation | async-start | bytes 524288 | tf_op jit(solution)/shard_map/all_to_all | solution.py:601
  35.7 11.1 %all-to-all-start.1 = ((f32[32,8,128]{2,1,0:T(8,128)}), f32[32,8,128]{2,1,0:T(8,128)S(1)}, u32[]{:S(2)}, u32[]{:S(2)}) async-start(f32[32,8,128]{2,1,0:T(8,128)} %broadcast_in_dim.27), calls=%async_computation.1 | async-start | bytes 262144 | tf_op jit(solution)/shard_map/all_to_all | solution.py:601
  51.2 1.2 collective-permute-start
  52.4 3.9 collective-permute-start.1
  56.3 3.9 collective-permute-start.2
  60.3 3.9 collective-permute-start.3
  64.2 5.2 collective-permute-start.4
  111.3 1.2 collective-permute-start.5
  112.6 3.7 collective-permute-start.6
  116.3 3.7 collective-permute-start.7
  120.1 3.7 collective-permute-start.8
  123.8 4.6 collective-permute-start.9
  131.4 1.2 collective-permute-start.10
  132.6 3.7 collective-permute-start.11
  136.4 3.7 collective-permute-start.12
  140.1 3.7 collective-permute-start.13
  143.8 4.6 collective-permute-start.14
  198.5 1.2 collective-permute-start.15
  199.7 3.9 collective-permute-start.16
  203.6 3.9 collective-permute-start.17
  207.5 3.9 collective-permute-start.18
  211.5 8.1 collective-permute-start.19
  241.1 65.7 %collective-permute-start.40 = (f32[4352,512]{1,0:T(8,128)}, f32[4352,512]{1,0:T(8,128)}, u32[]{:S(2)}, u32[]{:S(2)}) collective-permute-start(f32[4352,512]{1,0:T(8,128)} %get-tuple-element.132), channel_id=1, source_target_pairs={{0,4},{1,5},{2,6},{3,7},{4,0},{5,1},{6,2},{7,3},{8,12},{9,13},{10,... | collective-permute-start | bytes 26738696 | tf_op jit(solution)/shard_map/ppermute | solution.py:596
  265.8 23.4 %all-to-all-start.7 = ((f32[32,8,128]{2,1,0:T(8,128)}), f32[32,8,128]{2,1,0:T(8,128)}, u32[]{:S(2)}, u32[]{:S(2)}) async-start(f32[32,8,128]{2,1,0:T(8,128)} %broadcast_in_dim.33), calls=%async_computation.7 | async-start | bytes 262144 | tf_op jit(solution)/shard_map/all_to_all | solution.py:601
  306.4 14.0 %collective-permute-start.20 = (f32[3840,512]{1,0:T(8,128)}, f32[3840,512]{1,0:T(8,128)}, u32[]{:S(2)}, u32[]{:S(2)}) collective-permute-start(f32[3840,512]{1,0:T(8,128)} %get-tuple-element.119), channel_id=1, source_target_pairs={{0,4},{1,5},{2,6},{3,7},{4,0},{5,1},{6,2},{7,3},{8,12},{9,13},{10,... | collective-permute-start | bytes 23592968 | tf_op jit(solution)/shard_map/ppermute | solution.py:596
  318.7 98.7 %collective-permute-start.41 = (f32[2176,512]{1,0:T(8,128)}, f32[2176,512]{1,0:T(8,128)}, u32[]{:S(2)}, u32[]{:S(2)}) collective-permute-start(f32[2176,512]{1,0:T(8,128)} %get-tuple-element.134), channel_id=1, source_target_pairs={{0,8},{1,9},{2,10},{3,11},{4,12},{5,13},{6,14},{7,15},{8,0},{9,1},... | collective-permute-start | bytes 13369352 | tf_op jit(solution)/shard_map/ppermute | solution.py:596
  331.1 147.8 %collective-permute-start.21 = (f32[1920,512]{1,0:T(8,128)}, f32[1920,512]{1,0:T(8,128)}, u32[]{:S(2)}, u32[]{:S(2)}) collective-permute-start(f32[1920,512]{1,0:T(8,128)} %get-tuple-element.136), channel_id=1, source_target_pairs={{0,16},{1,17},{2,18},{3,19},{4,20},{5,21},{6,22},{7,23},{8,24},{9,... | collective-permute-start | bytes 11796488 | tf_op jit(solution)/shard_map/ppermute | solution.py:596
  423.5 50.2 %collective-permute-start.42 = (f32[1088,512]{1,0:T(8,128)}, f32[1088,512]{1,0:T(8,128)}, u32[]{:S(2)}, u32[]{:S(2)}) collective-permute-start(f32[1088,512]{1,0:T(8,128)} %get-tuple-element.138), channel_id=1, source_target_pairs={{0,16},{1,17},{2,18},{3,19},{4,20},{5,21},{6,22},{7,23},{8,24},{9,... | collective-permute-start | bytes 6684680 | tf_op jit(solution)/shard_map/ppermute | solution.py:596
  477.2 27.8 %collective-permute-start.43 = (f32[544,512]{1,0:T(8,128)}, f32[544,512]{1,0:T(8,128)}, u32[]{:S(2)}, u32[]{:S(2)}) collective-permute-start(f32[544,512]{1,0:T(8,128)} %get-tuple-element.144), channel_id=1, source_target_pairs={{0,1},{1,0},{2,3},{3,2},{4,5},{5,4},{6,7},{7,6},{8,9},{9,8},{10,11... | collective-permute-start | bytes 3342344 | tf_op jit(solution)/shard_map/ppermute | solution.py:596
  478.9 30.1 %copy-start.53 = (bf16[256,2048]{1,0:T(8,128)(2,1)S(1)}, bf16[256,2048]{1,0:T(8,128)(2,1)}, u32[]{:S(2)}) copy-start(bf16[256,2048]{1,0:T(8,128)(2,1)} %copy-done.51) | copy-start | bytes 3145732
  478.9 30.1 %copy-start.73 = (bf16[256,512]{1,0:T(8,128)(2,1)S(1)}, bf16[256,512]{1,0:T(8,128)(2,1)}, u32[]{:S(2)}) copy-start(bf16[256,512]{1,0:T(8,128)(2,1)} %copy-done.72) | copy-start | bytes 786436
  485.2 26.7 %copy-start.59 = (bf16[256,512]{1,0:T(8,128)(2,1)S(1)}, bf16[256,512]{1,0:T(8,128)(2,1)}, u32[]{:S(2)}) copy-start(bf16[256,512]{1,0:T(8,128)(2,1)} %copy-done.58) | copy-start | bytes 786436
  485.2 75.5 %collective-permute-start.22 = (f32[960,512]{1,0:T(8,128)}, f32[960,512]{1,0:T(8,128)}, u32[]{:S(2)}, u32[]{:S(2)}) collective-permute-start(f32[960,512]{1,0:T(8,128)} %get-tuple-element.142), channel_id=1, source_target_pairs={{0,1},{1,0},{2,3},{3,2},{4,5},{5,4},{6,7},{7,6},{8,9},{9,8},{10,11... | collective-permute-start | bytes 5898248 | tf_op jit(solution)/shard_map/ppermute | solution.py:596
  506.3 49.5 %collective-permute-start.44 = (f32[272,512]{1,0:T(8,128)S(1)}, f32[272,512]{1,0:T(8,128)}, u32[]{:S(2)}, u32[]{:S(2)}) collective-permute-start(f32[272,512]{1,0:T(8,128)S(1)} %dynamic-slice_add_fusion.16), channel_id=1, source_target_pairs={{0,2},{1,3},{2,0},{3,1},{4,6},{5,7},{6,4},{7,5},{8,10},{9,11},{10,... | collective-permute-start | bytes 1671176 | tf_op jit(solution)/shard_map/ppermute | solution.py:596
  511.9 44.0 %copy-start.82 = (f32[544,512]{1,0:T(8,128)S(1)}, f32[544,512]{1,0:T(8,128)}, u32[]{:S(2)}) copy-start(f32[544,512]{1,0:T(8,128)} %get-tuple-element.143) | copy-start | bytes 3342340
  516.9 43.9 %copy-start.81 = (f32[960,512]{1,0:T(8,128)S(1)}, f32[960,512]{1,0:T(8,128)}, u32[]{:S(2)}) copy-start(f32[960,512]{1,0:T(8,128)} %get-tuple-element.141) | copy-start | bytes 5898244
  516.9 155.5 %collective-permute-start.30 = (f32[2048,512]{1,0:T(8,128)}, f32[2048,512]{1,0:T(8,128)}, u32[]{:S(2)}, u32[]{:S(2)}) collective-permute-start(f32[2048,512]{1,0:T(8,128)} %get-tuple-element.126), channel_id=1, source_target_pairs={{0,4},{1,5},{2,6},{3,7},{4,0},{5,1},{6,2},{7,3},{8,12},{9,13},{10,... | collective-permute-start | bytes 12582920 | tf_op jit(solution)/shard_map/ppermute | solution.py:596
  557.2 26.1 %collective-permute-start.45 = (f32[272,512]{1,0:T(8,128)S(1)}, f32[272,512]{1,0:T(8,128)}, u32[]{:S(2)}, u32[]{:S(2)}) collective-permute-start(f32[272,512]{1,0:T(8,128)S(1)} %add_add_fusion), channel_id=1, source_target_pairs={{0,2},{1,3},{2,0},{3,1},{4,6},{5,7},{6,4},{7,5},{8,10},{9,11},{10,... | collective-permute-start | bytes 1671176 | tf_op jit(solution)/shard_map/ppermute | solution.py:596
  564.0 21.3 %collective-permute-start.23 = (f32[480,512]{1,0:T(8,128)}, f32[480,512]{1,0:T(8,128)S(1)}, u32[]{:S(2)}, u32[]{:S(2)}) collective-permute-start(f32[480,512]{1,0:T(8,128)} %get-tuple-element.148), channel_id=1, source_target_pairs={{0,8},{1,9},{2,10},{3,11},{4,12},{5,13},{6,14},{7,15},{8,0},{9,1},... | collective-permute-start | bytes 2949128 | tf_op jit(solution)/shard_map/ppermute | solution.py:596
  585.1 35.0 %collective-permute-start.46 = (f32[544,512]{1,0:T(8,128)S(1)}, f32[544,512]{1,0:T(8,128)}, u32[]{:S(2)}, u32[]{:S(2)}) collective-permute-start(f32[544,512]{1,0:T(8,128)S(1)} %maximum_select_fusion.8), channel_id=1, source_target_pairs={{0,1},{1,0},{2,3},{3,2},{4,5},{5,4},{6,7},{7,6},{8,9},{9,8},{10,11... | collective-permute-start | bytes 3342344 | tf_op jit(solution)/shard_map/ppermute | solution.py:596
  586.2 37.5 %collective-permute-start.24 = (f32[240,512]{1,0:T(8,128)}, f32[240,512]{1,0:T(8,128)}, u32[]{:S(2)}, u32[]{:S(2)}) collective-permute-start(f32[240,512]{1,0:T(8,128)} %dynamic-slice_add_fusion.19), channel_id=1, source_target_pairs={{0,2},{1,3},{2,0},{3,1},{4,6},{5,7},{6,4},{7,5},{8,10},{9,11},{10,... | collective-permute-start | bytes 1474568 | tf_op jit(solution)/shard_map/ppermute | solution.py:596
  589.0 34.7 %copy-start.84 = (f32[480,512]{1,0:T(8,128)S(1)}, f32[480,512]{1,0:T(8,128)}, u32[]{:S(2)}) copy-start(f32[480,512]{1,0:T(8,128)} %get-tuple-element.147) | copy-start | bytes 2949124
  622.2 56.8 %collective-permute-start.47 = (f32[1088,512]{1,0:T(8,128)S(1)}, f32[1088,512]{1,0:T(8,128)}, u32[]{:S(2)}, u32[]{:S(2)}) collective-permute-start(f32[1088,512]{1,0:T(8,128)S(1)} %maximum_select_fusion.5), channel_id=1, source_target_pairs={{0,16},{1,17},{2,18},{3,19},{4,20},{5,21},{6,22},{7,23},{8,24},{9,... | collective-permute-start | bytes 6684680 | tf_op jit(solution)/shard_map/ppermute | solution.py:596
  624.9 21.3 %collective-permute-start.25 = (f32[240,512]{1,0:T(8,128)S(1)}, f32[240,512]{1,0:T(8,128)S(1)}, u32[]{:S(2)}, u32[]{:S(2)}) collective-permute-start(f32[240,512]{1,0:T(8,128)S(1)} %add_add_fusion.1), channel_id=1, source_target_pairs={{0,2},{1,3},{2,0},{3,1},{4,6},{5,7},{6,4},{7,5},{8,10},{9,11},{10,... | collective-permute-start | bytes 1474568 | tf_op jit(solution)/shard_map/ppermute | solution.py:596
  646.3 22.2 %collective-permute-start.26 = (f32[480,512]{1,0:T(8,128)S(1)}, f32[480,512]{1,0:T(8,128)}, u32[]{:S(2)}, u32[]{:S(2)}) collective-permute-start(f32[480,512]{1,0:T(8,128)S(1)} %maximum_select_fusion.10), channel_id=1, source_target_pairs={{0,8},{1,9},{2,10},{3,11},{4,12},{5,13},{6,14},{7,15},{8,0},{9,1},... | collective-permute-start | bytes 2949128 | tf_op jit(solution)/shard_map/ppermute | solution.py:596
  670.4 45.8 %collective-permute-start.27 = (f32[960,512]{1,0:T(8,128)S(1)}, f32[960,512]{1,0:T(8,128)S(1)}, u32[]{:S(2)}, u32[]{:S(2)}) collective-permute-start(f32[960,512]{1,0:T(8,128)S(1)} %maximum_select_fusion.7), channel_id=1, source_target_pairs={{0,1},{1,0},{2,3},{3,2},{4,5},{5,4},{6,7},{7,6},{8,9},{9,8},{10,11... | collective-permute-start | bytes 5898248 | tf_op jit(solution)/shard_map/ppermute | solution.py:596
  678.9 80.7 %collective-permute-start.31 = (f32[1024,512]{1,0:T(8,128)}, f32[1024,512]{1,0:T(8,128)}, u32[]{:S(2)}, u32[]{:S(2)}) collective-permute-start(f32[1024,512]{1,0:T(8,128)} %get-tuple-element.140), channel_id=1, source_target_pairs={{0,1},{1,0},{2,3},{3,2},{4,5},{5,4},{6,7},{7,6},{8,9},{9,8},{10,11... | collective-permute-start | bytes 6291464 | tf_op jit(solution)/shard_map/ppermute | solution.py:596
  684.5 75.1 %copy-start.79 = (f32[1024,512]{1,0:T(8,128)S(1)}, f32[1024,512]{1,0:T(8,128)}, u32[]{:S(2)}) copy-start(f32[1024,512]{1,0:T(8,128)} %get-tuple-element.139) | copy-start | bytes 6291460
  684.5 144.7 %collective-permute-start.48 = (f32[2176,512]{1,0:T(8,128)}, f32[2176,512]{1,0:T(8,128)}, u32[]{:S(2)}, u32[]{:S(2)}) collective-permute-start(f32[2176,512]{1,0:T(8,128)} %maximum_select_fusion.2), channel_id=1, source_target_pairs={{0,8},{1,9},{2,10},{3,11},{4,12},{5,13},{6,14},{7,15},{8,0},{9,1},... | collective-permute-start | bytes 13369352 | tf_op jit(solution)/shard_map/ppermute | solution.py:596
  718.6 125.3 %collective-permute-start.28 = (f32[1920,512]{1,0:T(8,128)}, f32[1920,512]{1,0:T(8,128)}, u32[]{:S(2)}, u32[]{:S(2)}) collective-permute-start(f32[1920,512]{1,0:T(8,128)} %maximum_select_fusion.4), channel_id=1, source_target_pairs={{0,16},{1,17},{2,18},{3,19},{4,20},{5,21},{6,22},{7,23},{8,24},{9,... | collective-permute-start | bytes 11796488 | tf_op jit(solution)/shard_map/ppermute | solution.py:596
  762.6 41.6 %collective-permute-start.32 = (f32[512,512]{1,0:T(8,128)}, f32[512,512]{1,0:T(8,128)S(1)}, u32[]{:S(2)}, u32[]{:S(2)}) collective-permute-start(f32[512,512]{1,0:T(8,128)} %get-tuple-element.146), channel_id=1, source_target_pairs={{0,8},{1,9},{2,10},{3,11},{4,12},{5,13},{6,14},{7,15},{8,0},{9,1},... | collective-permute-start | bytes 3145736 | tf_op jit(solution)/shard_map/ppermute | solution.py:596
  804.4 11.9 %collective-permute-start.33 = (f32[256,512]{1,0:T(8,128)S(1)}, f32[256,512]{1,0:T(8,128)S(1)}, u32[]{:S(2)}, u32[]{:S(2)}) collective-permute-start(f32[256,512]{1,0:T(8,128)S(1)} %get-tuple-element.150), channel_id=1, source_target_pairs={{0,16},{1,17},{2,18},{3,19},{4,20},{5,21},{6,22},{7,23},{8,24},{9,... | collective-permute-start | bytes 1572872 | tf_op jit(solution)/shard_map/ppermute | solution.py:596
  816.4 12.7 %collective-permute-start.34 = (f32[128,512]{1,0:T(8,128)S(1)}, f32[128,512]{1,0:T(8,128)S(1)}, u32[]{:S(2)}, u32[]{:S(2)}) collective-permute-start(f32[128,512]{1,0:T(8,128)S(1)} %dynamic-slice_add_fusion.20), channel_id=1, source_target_pairs={{0,2},{1,3},{2,0},{3,1},{4,6},{5,7},{6,4},{7,5},{8,10},{9,11},{10,... | collective-permute-start | bytes 786440 | tf_op jit(solution)/shard_map/ppermute | solution.py:596
  829.1 14.1 %collective-permute-start.35 = (f32[128,512]{1,0:T(8,128)S(1)}, f32[128,512]{1,0:T(8,128)S(1)}, u32[]{:S(2)}, u32[]{:S(2)}) collective-permute-start(f32[128,512]{1,0:T(8,128)S(1)} %add_add_fusion.2), channel_id=1, source_target_pairs={{0,2},{1,3},{2,0},{3,1},{4,6},{5,7},{6,4},{7,5},{8,10},{9,11},{10,... | collective-permute-start | bytes 786440 | tf_op jit(solution)/shard_map/ppermute | solution.py:596
  836.2 122.9 %collective-permute-start.49 = (f32[4352,512]{1,0:T(8,128)S(1)}, f32[4352,512]{1,0:T(8,128)}, u32[]{:S(2)}, u32[]{:S(2)}) collective-permute-start(f32[4352,512]{1,0:T(8,128)S(1)} %maximum_select_fusion.mine_ref), channel_id=1, source_target_pairs={{0,4},{1,5},{2,6},{3,7},{4,0},{5,1},{6,2},{7,3},{8,12},{9,13},{10,... | collective-permute-start | bytes 26738696 | tf_op jit(solution)/shard_map/ppermute | solution.py:596
  843.3 13.8 %collective-permute-start.36 = (f32[256,512]{1,0:T(8,128)S(1)}, f32[256,512]{1,0:T(8,128)S(1)}, u32[]{:S(2)}, u32[]{:S(2)}) collective-permute-start(f32[256,512]{1,0:T(8,128)S(1)} %maximum_select_fusion.11), channel_id=1, source_target_pairs={{0,16},{1,17},{2,18},{3,19},{4,20},{5,21},{6,22},{7,23},{8,24},{9,... | collective-permute-start | bytes 1572872 | tf_op jit(solution)/shard_map/ppermute | solution.py:596
  850.8 93.4 %collective-permute-start.29 = (f32[3840,512]{1,0:T(8,128)S(1)}, f32[3840,512]{1,0:T(8,128)}, u32[]{:S(2)}, u32[]{:S(2)}) collective-permute-start(f32[3840,512]{1,0:T(8,128)S(1)} %maximum_select_fusion.1.mine_ref), channel_id=1, source_target_pairs={{0,4},{1,5},{2,6},{3,7},{4,0},{5,1},{6,2},{7,3},{8,12},{9,13},{10,... | collective-permute-start | bytes 23592968 | tf_op jit(solution)/shard_map/ppermute | solution.py:596
  857.2 24.2 %collective-permute-start.37 = (f32[512,512]{1,0:T(8,128)S(1)}, f32[512,512]{1,0:T(8,128)S(1)}, u32[]{:S(2)}, u32[]{:S(2)}) collective-permute-start(f32[512,512]{1,0:T(8,128)S(1)} %maximum_select_fusion.9), channel_id=1, source_target_pairs={{0,8},{1,9},{2,10},{3,11},{4,12},{5,13},{6,14},{7,15},{8,0},{9,1},... | collective-permute-start | bytes 3145736 | tf_op jit(solution)/shard_map/ppermute | solution.py:596
  881.8 50.4 %copy-start.61 = (f32[32,128]{1,0:T(8,128)S(1)}, f32[32,128]{1,0:T(8,128)}, u32[]{:S(2)}) copy-start(f32[32,128]{1,0:T(8,128)} %copy-done.60) | copy-start | bytes 49156
  881.8 51.0 %copy-start.64 = (f32[8,128]{1,0:T(8,128)S(1)}, f32[8,128]{1,0:T(8,128)}, u32[]{:S(2)}) copy-start(f32[8,128]{1,0:T(8,128)} %copy-done.63) | copy-start | bytes 12292
  881.8 53.4 %copy-start.66 = (f32[8,128]{1,0:T(8,128)S(1)}, f32[8,128]{1,0:T(8,128)}, u32[]{:S(2)}) copy-start(f32[8,128]{1,0:T(8,128)} %copy-done.65) | copy-start | bytes 12292
  881.8 45.8 %collective-permute-start.38 = (f32[1024,512]{1,0:T(8,128)S(1)}, f32[1024,512]{1,0:T(8,128)}, u32[]{:S(2)}, u32[]{:S(2)}) collective-permute-start(f32[1024,512]{1,0:T(8,128)S(1)} %maximum_select_fusion.6), channel_id=1, source_target_pairs={{0,1},{1,0},{2,3},{3,2},{4,5},{5,4},{6,7},{7,6},{8,9},{9,8},{10,11... | collective-permute-start | bytes 6291464 | tf_op jit(solution)/shard_map/ppermute | solution.py:596
  932.1 7.2 collective-permute-start.39
  934.6 40.0 %copy-start.88 = (f32[4,4,128]{2,1,0:T(4,128)}, f32[4,4,128]{2,1,0:T(4,128)S(1)}, u32[]{:S(2)}) copy-start(f32[4,4,128]{2,1,0:T(4,128)S(1)} %get-tuple-element.152) | copy-start | bytes 24580
  (92 other events, 527.2 us)

commit v2 on v1

--- a/solution.py
+++ b/solution.py
@@ -15,6 +15,12 @@
 LANES = 128
 TILE = 512
 ROWS = TILE // LANES
+MIB = 60
+SCHEDULE = (
+    7, 2, 3, 1, 0, 4, 5, 6, 7, 4, 2, 6, 3, 5, 7, 0, 1, 3, 2, 4, 3, 6, 2, 5, 3, 0, 2, 1, 0, 5,
+    1, 4, 0, 6, 5, 4, 1, 6, 5, 5, 4, 4, 6, 6, 5, 4, 6, 5, 4, 6, 5, 4, 6, 6, 5, 4,
+)
+FIRST = 5
 
 
 def dot(left, right):
@@ -43,9 +49,17 @@
     return jnp.concatenate([pack(col_sum(first)), pack(col_sum(second))], axis=0)
 
 
+def put(ref, tile):
+    ref[...] = jnp.broadcast_to(tile, ref.shape)
+
+
+def total(ref):
+    return ref[...] if len(ref.shape) == 2 else jnp.sum(ref[...], axis=0)
+
+
 def coefficients(stat_ref, count_ref, param_ref, factor=1.0):
-    stat, param = stat_ref[...], param_ref[...]
-    count = count_ref[0:ROWS, :] * factor
+    stat, param = total(stat_ref), param_ref[...]
+    count = total(count_ref)[0:ROWS, :] * factor
     average = stat[0:ROWS] / count
     inverse = lax.rsqrt(stat[ROWS : 2 * ROWS] / count - average * average + EPSILON)
     return (
@@ -57,7 +71,7 @@
 
 
 def back_coefficients(grad_rows_shift, grad_rows_gain, count_ref, factor=1.0):
-    count = count_ref[0:ROWS, :] * factor
+    count = total(count_ref)[0:ROWS, :] * factor
     return unpack(grad_rows_shift / count), unpack(grad_rows_gain / count)
 
 
@@ -115,7 +129,7 @@
     return pl.BlockSpec((rows, LANES), lambda n, *_: (offset + n, 0))
 
 
-def call(kernel, grid, in_specs, out_specs, out_shape, scratch=(), mib=40, flops=0, nbytes=0):
+def call(kernel, grid, in_specs, out_specs, out_shape, scratch=(), mib=MIB, flops=0, nbytes=0):
     return pl.pallas_call(
         kernel,
         grid=grid,
@@ -153,8 +167,8 @@
 
     @pl.when(step == pl.num_programs(0) - 1)
     def _():
-        stat_ref[0:8, :] = jnp.concatenate([pack(acc_ref[0:1, :]), pack(acc_ref[1:2, :])], axis=0)
-        stat_ref[8:16, :] = jnp.broadcast_to(col_sum(all_mask_ref[...]), (8, LANES))
+        count = jnp.broadcast_to(col_sum(all_mask_ref[...]), (8, LANES))
+        put(stat_ref, jnp.concatenate([pack(acc_ref[0:1, :]), pack(acc_ref[1:2, :]), count], axis=0))
 
 
 def product_kernel(x_ref, w_ref, out_ref, stat_ref):
@@ -192,7 +206,7 @@
         pre = lower + shift_rows(upper, -1, width, height)
         out_ref[...] = pre
         masked = pre * mask
-        out_stat_ref[...] = stat_tile(masked, masked * pre)
+        put(out_stat_ref, stat_tile(masked, masked * pre))
 
 
 def expand_kernel(pre_ref, stat_ref, count_ref, param_ref, mask_ref, w_ref, act_ref, out_ref, out_stat_ref):
@@ -204,7 +218,7 @@
 
     pre = dot(act_ref[...], w_ref[...])
     out_ref[...] = pre
-    out_stat_ref[...] = stat_tile(pre, pre * pre)
+    put(out_stat_ref, stat_tile(pre, pre * pre))
 
 
 def join_kernel(pe_ref, ps_ref, se_ref, ss_ref, count_ref, qe_ref, qs_ref, mask_ref, w_ref, first_ref, out_ref, out_stat_ref):
@@ -228,7 +242,7 @@
     @pl.when(n == pl.num_programs(0) - 1)
     def _():
         pre = out_ref[...]
-        out_stat_ref[...] = stat_tile(pre, pre * pre)
+        put(out_stat_ref, stat_tile(pre, pre * pre))
 
 
 def store_padded(target_ref, values, step, width, height, images):
@@ -276,7 +290,7 @@
     def _():
         pre = out_ref[...]
         masked = pre * column(mask_ref)
-        out_stat_ref[...] = stat_tile(masked, masked * pre)
+        put(out_stat_ref, stat_tile(masked, masked * pre))
 
 
 def final_kernel(pre_ref, stat_ref, count_ref, param_ref, mask_ref, first_ref, cot_ref, out_ref, grad_ref, sum_ref):
@@ -288,7 +302,7 @@
     out_ref[...] = (final * gate * mask).astype(BF16)
     grad = cot_ref[...].astype(F32) * mask * (gate * (1.0 + final * (1.0 - gate)))
     grad_ref[...] = grad
-    sum_ref[...] = stat_tile(grad, grad * hat)
+    put(sum_ref, stat_tile(grad, grad * hat))
 
 
 def norm_back(grad, hat, scale, shift_term, gain_term, mask):
@@ -302,7 +316,7 @@
     n = pl.program_id(0)
     mask = column(mask_ref)
     average, inverse, gain, _ = coefficients(stat_ref, count_ref, param_ref)
-    gsum = gsum_ref[...]
+    gsum = total(gsum_ref)
     shift_term, gain_term = back_coefficients(gsum[0:ROWS], gsum[ROWS : 2 * ROWS], count_ref)
     hat = (pre_ref[...] - average) * inverse
     gpre = norm_back(grad_ref[...], hat, inverse * gain, shift_term, gain_term, mask)
@@ -327,12 +341,12 @@
     hat = (pre - average) * inverse
     grad = out_ref[...] * mask * slope(hat * gain + shift)
     out_ref[...] = grad
-    sum_ref[...] = stat_tile(grad, grad * hat)
+    put(sum_ref, stat_tile(grad, grad * hat))
 
 
 def pre_grad(grad_ref, pre_ref, stat_ref, gsum_ref, count_ref, param_ref, mask):
     average, inverse, gain, _ = coefficients(stat_ref, count_ref, param_ref)
-    gsum = gsum_ref[...]
+    gsum = total(gsum_ref)
     shift_term, gain_term = back_coefficients(gsum[0:ROWS], gsum[ROWS : 2 * ROWS], count_ref)
     hat = (pre_ref[...] - average) * inverse
     return norm_back(grad_ref[...], hat, inverse * gain, shift_term, gain_term, mask)
@@ -402,7 +416,7 @@
     mask = column(mask_ref)
     average_e, inverse_e, gain_e, _ = coefficients(se_ref, count_ref, qe_ref)
     average_s, inverse_s, gain_s, _ = coefficients(ss_ref, count_ref, qs_ref)
-    gsum = gsum_ref[...]
+    gsum = total(gsum_ref)
     shift_term, gain_e_term = back_coefficients(gsum[0:ROWS], gsum[ROWS : 2 * ROWS], count_ref)
     _, gain_s_term = back_coefficients(gsum[0:ROWS], gsum[2 * ROWS : 3 * ROWS], count_ref)
     grad = gj_ref[...]
@@ -459,14 +473,14 @@
         out_ref[2] += even
         out_ref[3] += odd
         average, inverse, gain, shift = coefficients(in_stat_ref, count_ref, in_param_ref, 4.0)
-        total = total_hat = jnp.zeros((1, out_ref.shape[2]), F32)
+        whole_sum = whole_hat = jnp.zeros((1, out_ref.shape[2]), F32)
         for q in range(4):
             hat = (in_ref[q] - average) * inverse
             grad = out_ref[q] * mask * slope(hat * gain + shift)
             out_ref[q] = grad
-            total += col_sum(grad)
-            total_hat += col_sum(grad * hat)
-        sum_ref[...] = jnp.concatenate([pack(total), pack(total_hat)], axis=0)
+            whole_sum += col_sum(grad)
+            whole_hat += col_sum(grad * hat)
+        put(sum_ref, jnp.concatenate([pack(whole_sum), pack(whole_hat)], axis=0))
 
 
 def short_back_kernel(g_ref, w_ref, out_ref):
@@ -488,7 +502,7 @@
     mask = column(mask_ref)
     masking = jnp.concatenate([mask] * 4, axis=0)
     average, inverse, gain, _ = coefficients(stat_ref, count_ref, param_ref, 4.0)
-    gsum = gsum_ref[...]
+    gsum = total(gsum_ref)
     shift_term, gain_term = back_coefficients(gsum[0:ROWS], gsum[ROWS : 2 * ROWS], count_ref, 4.0)
     grad = jnp.concatenate([grad_ref[q] for q in range(4)], axis=0)
     pre = jnp.concatenate([pre_ref[q] for q in range(4)], axis=0)
@@ -502,78 +516,132 @@
     out_ref[...] = dot(perm_ref[...], image).astype(BF16)
 
 
-def outer_kernel(pick, left_blocks, core_ref, *refs):
-    left_ref, right_ref = refs[0], refs[1]
-    keep_ref, send_ref, turned_ref = refs[-3], refs[-2], refs[-1]
-    b = pl.program_id(0)
-
-    @pl.when(lax.rem(b, left_blocks[1]) == 0)
+def turn_left(left_ref, turned_ref, per_left):
+    @pl.when(lax.rem(pl.program_id(0), per_left) == 0)
     def _():
         left = left_ref[...] if len(left_ref.shape) == 2 else left_ref[0]
         turned_ref[...] = left.T
 
+
+def halves_kernel(pick, per_left, core_ref, left_ref, right_ref, keep_ref, send_ref, turned_ref):
+    turn_left(left_ref, turned_ref, per_left)
     half = TILE // 2
-    right = pick(right_ref, b)
-    core = core_ref[0]
-    keep_ref[...] = dot(turned_ref[pl.ds(pl.multiple_of(core * half, half), half), :], right)
-    send_ref[...] = dot(turned_ref[pl.ds(pl.multiple_of((1 - core) * half, half), half), :], right)
-
-
-def outer(core, left, left_spec, right, right_spec, pick, blocks, per_left, place, total, into):
+    right = pick(right_ref, pl.program_id(0))
+    mine = pl.multiple_of(core_ref[0] * half, half)
+    away = pl.multiple_of((1 - core_ref[0]) * half, half)
+    send_ref[0] = dot(turned_ref[pl.ds(away, half), :], right)
+    keep_ref[0] = dot(turned_ref[pl.ds(mine, half), :], right)
+
+
+def outer_halves(core, left, left_spec, right, right_spec, pick, blocks, per_left):
     half = TILE // 2
     pixels = left_spec.block_shape[-2]
-    shape = shaped((total * half, TILE))
-    out_spec = pl.BlockSpec((half, TILE), lambda b, *_: (place + b, 0))
-    aliases = {} if into is None else {3: 0, 4: 1}
-    extra = () if into is None else tuple(into)
+    shape = shaped((blocks, half, TILE))
+    out_spec = pl.BlockSpec((1, half, TILE), lambda b, *_: (b, 0, 0))
     return pl.pallas_call(
-        functools.partial(outer_kernel, pick, (None, per_left)),
+        functools.partial(halves_kernel, pick, per_left),
         grid_spec=pltpu.PrefetchScalarGridSpec(
             num_scalar_prefetch=1,
             grid=(blocks,),
-            in_specs=[left_spec, right_spec] + [pl.BlockSpec(memory_space=pl.ANY)] * len(extra),
+            in_specs=[left_spec, right_spec],
             out_specs=[out_spec, out_spec],
             scratch_shapes=[pltpu.VMEM((TILE, pixels), BF16)],
         ),
         out_shape=[shape, shape],
-        input_output_aliases=aliases,
-        compiler_params=pltpu.CompilerParams(
-            vmem_limit_bytes=24 << 20, dimension_semantics=("arbitrary",)
-        ),
-        cost_estimate=pl.CostEstimate(
-            flops=2 * blocks * pixels * TILE * TILE,
-            bytes_accessed=blocks * TILE * TILE * 4,
-            transcendentals=0,
-        ),
-    )(core, left, right, *extra)
-
-
-def assemble_kernel(core_ref, mine_ref, other_ref, out_ref):
-    half = TILE // 2
-    core = core_ref[0]
-    out_ref[pl.ds(pl.multiple_of(core * half, half), half), :] = mine_ref[...]
-    out_ref[pl.ds(pl.multiple_of((1 - core) * half, half), half), :] = other_ref[...]
-
-
-def assemble(core, mine, other, place, blocks, shape, where):
-    half = TILE // 2
-    in_spec = pl.BlockSpec((half, TILE), lambda b, *_: (place + b, 0))
+        compiler_params=outer_params(),
+        cost_estimate=outer_cost(blocks, pixels),
+    )(core, left, right)
+
+
+def outer_params():
+    return pltpu.CompilerParams(vmem_limit_bytes=MIB << 20, dimension_semantics=("arbitrary",))
+
+
+def outer_cost(blocks, pixels):
+    return pl.CostEstimate(
+        flops=2 * blocks * pixels * TILE * TILE, bytes_accessed=blocks * TILE * TILE * 4, transcendentals=0
+    )
+
+
+def spread_kernel(pick, per_left, left_ref, right_ref, *refs):
+    out_ref, turned_ref = refs[-2], refs[-1]
+    turn_left(left_ref, turned_ref, per_left)
+    out_ref[...] = dot(turned_ref[...], pick(right_ref, pl.program_id(0))).reshape(out_ref.shape)
+
+
+def outer_spread(shares, left, left_spec, right, right_spec, pick, blocks, per_left, place, total, into):
+    rows = TILE // shares
+    pixels = left_spec.block_shape[-2]
+    extra = () if into is None else (into,)
     return pl.pallas_call(
-        assemble_kernel,
+        functools.partial(spread_kernel, pick, per_left),
+        grid=(blocks,),
+        in_specs=[left_spec, right_spec] + [pl.BlockSpec(memory_space=pl.ANY)] * len(extra),
+        out_specs=pl.BlockSpec((shares, rows, TILE), lambda b: (0, place + b, 0)),
+        out_shape=shaped((shares, total * rows, TILE)),
+        scratch_shapes=[pltpu.VMEM((TILE, pixels), BF16)],
+        input_output_aliases={2: 0} if extra else {},
+        compiler_params=outer_params(),
+        cost_estimate=outer_cost(blocks, pixels),
+    )(left, right, *extra)
+
+
+def assemble_kernel(chunks, place_ref, own_ref, near_ref, far_ref, both_ref, *refs):
+    out_ref = refs[-1]
+    rows = TILE // 4 // chunks
+    for k, ref in enumerate((own_ref, near_ref, far_ref, both_ref)):
+        for c in range(chunks):
+            start = pl.multiple_of(place_ref[k * chunks + c], rows)
+            out_ref[pl.ds(start, rows), :] = ref[0, c * rows : (c + 1) * rows, :]
+
+
+def assemble(places, pieces, first, blocks, shape, where, chunks=1, into=None):
+    in_spec = pl.BlockSpec((1, TILE // 4, TILE), lambda b, *_: (first + b, 0, 0))
+    extra = () if into is None else (into,)
+    return pl.pallas_call(
+        functools.partial(assemble_kernel, chunks),
         grid_spec=pltpu.PrefetchScalarGridSpec(
             num_scalar_prefetch=1,
             grid=(blocks,),
-            in_specs=[in_spec, in_spec],
+            in_specs=[in_spec] * 4 + [pl.BlockSpec(memory_space=pl.ANY)] * len(extra),
             out_specs=pl.BlockSpec((TILE, TILE), lambda b, *_: where(b)),
         ),
         out_shape=shaped(shape),
-        compiler_params=pltpu.CompilerParams(
-            vmem_limit_bytes=16 << 20, dimension_semantics=("arbitrary",)
-        ),
+        input_output_aliases={5: 0} if extra else {},
+        compiler_params=outer_params(),
         cost_estimate=pl.CostEstimate(
             flops=0, bytes_accessed=2 * blocks * TILE * TILE * 4, transcendentals=0
         ),
-    )(core, mine, other)
+    )(places, *pieces, *extra)
+
+
+def regroup_kernel(starts, in_ref, *refs):
+    out_ref, rows = refs[-1], in_ref.shape[1]
+    for k, start in enumerate(starts):
+        out_ref[start : start + rows, :] = in_ref[k]
+
+
+def regroup(gathered, starts, total, place, blocks, shape, where, into=None):
+    devices, rows = gathered.shape[0], gathered.shape[1] // total
+    extra = () if into is None else (into,)
+    if rows % 8:
+        order = np.argsort(np.asarray(starts))
+        gathered = gathered.reshape(devices, total, rows, TILE)[order].transpose(1, 0, 2, 3)
+        gathered = gathered.reshape(1, total * TILE, TILE)
+        devices, rows, starts = 1, TILE, (0,)
+    return pl.pallas_call(
+        functools.partial(regroup_kernel, starts),
+        grid=(blocks,),
+        in_specs=[pl.BlockSpec((devices, rows, TILE), lambda b: (0, place + b, 0))]
+        + [pl.BlockSpec(memory_space=pl.ANY)] * len(extra),
+        out_specs=pl.BlockSpec((TILE, TILE), where),
+        out_shape=shaped(shape),
+        input_output_aliases={1: 0} if extra else {},
+        compiler_params=outer_params(),
+        cost_estimate=pl.CostEstimate(
+            flops=0, bytes_accessed=2 * blocks * TILE * TILE * 4, transcendentals=0
+        ),
+    )(gathered, *extra)
 
 
 def bits_of(first, size):
@@ -597,8 +665,7 @@
 
 
 def sync_all(tile, devices):
-    copies = jnp.broadcast_to(tile[None], (devices,) + tile.shape)
-    return jnp.sum(lax.all_to_all(copies, AXES, 0, 0, tiled=True), axis=0)
+    return lax.all_to_all(tile, AXES, 0, 0, tiled=True)
 
 
 def sync_hops(tile, bits, devices):
@@ -611,26 +678,101 @@
     return lax.rem(lax.div(flat, bit), 2)
 
 
-def scatter_sum(keep, send, flat, core, order, devices):
-    received = swap(send, core, devices)
-    for bit in order:
-        rows = keep.shape[0] // 2
-        own = device_bit(flat, bit)
-        start, away = own * rows, (1 - own) * rows
-        send = lax.dynamic_slice_in_dim(keep, away, rows) + lax.dynamic_slice_in_dim(received, away, rows)
-        keep = lax.dynamic_slice_in_dim(keep, start, rows) + lax.dynamic_slice_in_dim(received, start, rows)
-        received = swap(send, bit, devices)
-    return keep + received
-
-
-def gather_back(shard, flat, core, order, devices):
-    for bit in reversed(order):
-        other = swap(shard, bit, devices)
-        own = device_bit(flat, bit)
-        shard = jnp.where(
-            own == 0, jnp.concatenate([shard, other], axis=0), jnp.concatenate([other, shard], axis=0)
-        )
-    return shard, swap(shard, core, devices)
+def after(values, *others):
+    return lax.optimization_barrier((values,) + others)[0]
+
+
+def half_sum(keep, received, which):
+    rows = keep.shape[1] // 2
+    first = lax.dynamic_slice_in_dim(keep, which * rows, rows, axis=1)
+    return first + lax.dynamic_slice_in_dim(received, which * rows, rows, axis=1)
+
+
+def join_halves(own, values, other):
+    return jnp.where(
+        own == 0, jnp.concatenate([values, other], axis=1), jnp.concatenate([other, values], axis=1)
+    )
+
+
+class Halving:
+    def __init__(self, keep, order, flat, devices, send=None, core=None):
+        self.keep, self.order, self.flat, self.devices = keep, list(order), flat, devices
+        self.received = None
+        self.moves = []
+        if send is not None:
+            self.moves.append(lambda token: self.cross(send, core, token))
+        self.moves += [functools.partial(self.halve, bit) for bit in self.order] + [self.add]
+
+    def cross(self, send, core, token):
+        send = after(send, token)
+        self.received = swap(send, core, self.devices)
+        return send
+
+    def halve(self, bit, token):
+        own = device_bit(self.flat, bit)
+        if self.received is None:
+            keep, rows = after(self.keep, token), self.keep.shape[1] // 2
+            send = lax.dynamic_slice_in_dim(keep, (1 - own) * rows, rows, axis=1)
+            self.received = swap(send, bit, self.devices)
+            self.keep = lax.dynamic_slice_in_dim(keep, own * rows, rows, axis=1)
+            return send
+        keep, received = after((self.keep, self.received), token)
+        send = half_sum(keep, received, 1 - own)
+        self.received = swap(send, bit, self.devices)
+        keep, received = after((keep, received), send)
+        self.keep = half_sum(keep, received, own)
+        return send
+
+    def add(self, token):
+        keep, received = after((self.keep, self.received), token)
+        self.keep = keep + received
+        return self.keep
+
+
+class Return:
+    def __init__(self, source, core, flat, devices):
+        self.source, self.core, self.flat, self.devices = source, core, flat, devices
+        self.order = source.order
+        back = list(reversed(self.order))
+        self.moves = [functools.partial(self.widen, a, b) for a, b in zip([None] + back[:-1], back)]
+        self.moves.append(self.cross)
+
+    def widen(self, joined, bit, token):
+        if joined is None:
+            self.own = after(self.source.keep, token)
+        else:
+            own, other = after((self.own, self.near), token)
+            self.own = join_halves(device_bit(self.flat, joined), own, other)
+        self.near = swap(self.own, bit, self.devices)
+        if bit == self.order[0]:
+            self.far = swap(self.own, self.core, self.devices)
+        return self.own
+
+    def cross(self, token):
+        self.near = after(self.near, token)
+        self.both = swap(self.near, self.core, self.devices)
+        return self.near
+
+    def pieces(self):
+        return self.own, self.near, self.far, self.both
+
+    def places(self):
+        half, quarter = TILE // 2, TILE // 4
+        core, own = device_bit(self.flat, self.core), device_bit(self.flat, self.order[0])
+        return jnp.stack(
+            [c * half + o * quarter for c in (core, 1 - core) for o in (own, 1 - own)]
+        ).astype(jnp.int32)
+
+
+def run_streams(streams, schedule, token, to_end=True):
+    for k in schedule:
+        if streams[k].moves:
+            token = streams[k].moves.pop(0)(token)
+    while to_end and any(s.moves for s in streams):
+        for s in streams:
+            if s.moves:
+                token = s.moves.pop(0)(token)
+    return token
 
 
 def permutation(width):
@@ -670,6 +812,7 @@
     devices = dp * rep
     core_bit, x_bits, y_bits, z_bits = mesh_bits(dp, rep)
     hop_bits = [core_bit] + y_bits + x_bits + z_bits
+    xs, ys, zs, rep_bits = x_bits, y_bits, z_bits, bits_of(1, rep)
     flat = lax.axis_index(AXES)
     core = device_bit(flat, core_bit).astype(jnp.int32).reshape(1)
     sync = functools.partial(sync_all, devices=devices)
@@ -699,7 +842,29 @@
     mid_f32, mid_spec = shaped((pixels, mid)), full((pixels, mid))
     wide_spec, tap_spec = cols(pixels, TILE), pl.BlockSpec((1, 3, mid, mid), lambda r: (r, 0, 0, 0))
     plane_block = lambda c: pl.BlockSpec((4, quarter, c), lambda k: (0, k, 0))
-    one_tile, wide_tiles = shaped((8, LANES)), shaped((8 * blocks, LANES))
+    area, in_blocks = width * height, c_in // TILE
+    left_const = pl.BlockSpec((pixels, TILE), lambda b, *_: (0, 0))
+    right_n = pl.BlockSpec((pixels, TILE), lambda b, *_: (0, b))
+
+    def whole(ref, b):
+        return ref[...]
+
+    def window_taps(ref, b):
+        r, c = lax.div(b, 3), lax.rem(b, 3)
+        first = pl.multiple_of((2 - r) * width, width)
+        return window_rows(ref, c, first, area, images)
+
+    def spatial_taps(place, ref, b):
+        r, c = lax.div(place + b, 3), lax.rem(place + b, 3)
+        return ref[2 * jnp.where(r == 0, 1, 0) + jnp.where(c == 0, 1, 0)]
+
+    def spatial_plane(place, b, *_):
+        r, c = lax.div(place + b, 3), lax.rem(place + b, 3)
+        return (2 * jnp.where(r == 1, 0, 1) + jnp.where(c == 1, 0, 1), 0, 0)
+
+    one_tile, wide_tiles = shaped((devices, 8, LANES)), shaped((8 * blocks, LANES))
+    all_tiles = full((devices, 8, LANES))
+    count_spec = pl.BlockSpec((devices, 8, LANES), lambda *_: (0, 1, 0))
     padded = (3, images, (height + 2) * width, mid)
 
     planes, pre_reduce, stat = call(
@@ -709,13 +874,12 @@
             pl.BlockSpec((4 * quarter, c_in), lambda k: (k, 0)), full(perm.shape),
             pl.BlockSpec((quarter, LANES), lambda k: (k, 0)), mask_spec, full((c_in, mid)),
         ],
-        [plane_block(c_in), plane_block(mid), full((16, LANES))],
-        [shaped((4, pixels, c_in), BF16), shaped((4, pixels, mid)), shaped((16, LANES))],
+        [plane_block(c_in), plane_block(mid), full((devices, 16, LANES))],
+        [shaped((4, pixels, c_in), BF16), shaped((4, pixels, mid)), shaped((devices, 16, LANES))],
         [pltpu.VMEM((8, mid), F32)],
         flops=8 * pixels * c_in * mid, nbytes=8 << 20,
     )(image, perm, mask, mask, w_reduce)
     s_reduce = sync(stat)
-    count_spec = tile_at(1)
 
     pre_short, stat_short = call(
         product_kernel,
@@ -729,8 +893,8 @@
     act_reduce, pre_spatial, stat = call(
         functools.partial(spatial_kernel, width, height),
         (3,),
-        [full((4, pixels, mid)), tile_at(0), count_spec, p_reduce, mask_spec, tap_spec],
-        [full((4, pixels, mid)), mid_spec, full((8, LANES))],
+        [full((4, pixels, mid)), all_tiles, count_spec, p_reduce, mask_spec, tap_spec],
+        [full((4, pixels, mid)), mid_spec, all_tiles],
         [shaped((4, pixels, mid), BF16), mid_f32, one_tile],
         [pltpu.VMEM((4, pixels, mid), F32)],
         flops=18 * pixels * mid * mid, nbytes=8 << 20,
@@ -741,7 +905,7 @@
         return call(
             expand_kernel,
             (blocks,),
-            [mid_spec, tile_at(0), count_spec, p_spec, mask_spec, cols(mid, TILE)],
+            [mid_spec, all_tiles, count_spec, p_spec, mask_spec, cols(mid, TILE)],
             [mid_spec, wide_spec, tile_n()],
             [shaped((pixels, mid), BF16), wide_f32, wide_tiles],
             flops=2 * pixels * mid * c_out, nbytes=5 << 20,
@@ -758,7 +922,7 @@
             wide_spec, wide_spec, e_spec, s_spec, count_spec, p_expand, p_short, mask_spec,
             pl.BlockSpec((TILE, mid), lambda n: (n, 0)),
         ],
-        [wide_spec, mid_spec, full((8, LANES))],
+        [wide_spec, mid_spec, all_tiles],
         [shaped((pixels, c_out), BF16), mid_f32, one_tile],
         flops=2 * pixels * mid * c_out, nbytes=8 << 20,
     )(pre_expand, pre_short, s_both, s_both, s_reduce, params, params, mask, w_squeeze)
@@ -767,8 +931,8 @@
     act_squeeze, pre_window, stat = call(
         functools.partial(window_kernel, width, height, images),
         (3,),
-        [mid_spec, tile_at(0), count_spec, p_squeeze, mask_spec, tap_spec],
-        [mid_spec, mid_spec, full((8, LANES))],
+        [mid_spec, all_tiles, count_spec, p_squeeze, mask_spec, tap_spec],
+        [mid_spec, mid_spec, all_tiles],
         [shaped((pixels, mid), BF16), mid_f32, one_tile],
         [pltpu.VMEM(padded, BF16)],
         flops=18 * pixels * mid * mid, nbytes=6 << 20,
@@ -793,32 +957,37 @@
         (blocks,),
         [
             wide_spec, wide_spec, tile_n(), tile_n(), count_spec, p_widen, mask_spec, cols(mid, TILE),
-            mid_spec, tile_at(0), p_window,
+            mid_spec, all_tiles, p_window,
         ],
-        [wide_spec, mid_spec, full((8, LANES))],
+        [wide_spec, mid_spec, all_tiles],
         [shaped((pixels, c_out), BF16), mid_f32, one_tile],
         flops=2 * pixels * mid * c_out, nbytes=8 << 20,
     )(grad_final, pre_widen, s_widen, g_widen, s_reduce, params, mask, w_widen, pre_window, s_window, params)
-    g_window = sync(gsum)
+    early_made = outer_spread(dp, act_window, left_const, gpre_widen, right_n, whole, blocks, blocks, 0, 9 + blocks, None)
+    g_window = after(sync(gsum), early_made)
 
     gpad_window, grad_squeeze, gsum = call(
         functools.partial(window_back_kernel, width, height, images),
         (3,),
         [
-            mid_spec, mid_spec, tile_at(0), tile_at(0), count_spec, p_window, mask_spec, tap_spec,
-            mid_spec, tile_at(0), p_squeeze,
+            mid_spec, mid_spec, all_tiles, all_tiles, count_spec, p_window, mask_spec, tap_spec,
+            mid_spec, all_tiles, p_squeeze,
         ],
-        [full(padded), mid_spec, full((8, LANES))],
+        [full(padded), mid_spec, all_tiles],
         [shaped(padded, BF16), mid_f32, one_tile],
         flops=18 * pixels * mid * mid, nbytes=8 << 20,
     )(grad_window, pre_window, s_window, g_window, s_reduce, params, mask, w_window, pre_squeeze, s_squeeze, params)
+    early_made = outer_spread(
+        dp, act_squeeze, left_const, gpad_window, full(padded), window_taps, 9, 9, blocks, 9 + blocks, early_made
+    )
+    early_sum = lax.psum_scatter(early_made.reshape(-1, TILE), "dp", scatter_dimension=0, tiled=True)
     g_squeeze = sync(gsum)
 
     gpre_squeeze, grad_joined, gsum = call(
         squeeze_back_kernel,
         (blocks,),
         [
-            mid_spec, mid_spec, tile_at(0), tile_at(0), count_spec, p_squeeze, mask_spec,
+            mid_spec, mid_spec, all_tiles, all_tiles, count_spec, p_squeeze, mask_spec,
             pl.BlockSpec((TILE, mid), lambda n: (n, 0)),
             wide_spec, wide_spec, wide_spec, e_spec, s_spec, p_expand, p_short,
         ],
@@ -830,35 +999,71 @@
         grad_final, pre_expand, pre_short, s_both, s_both, params, params,
     )
     g_both = sync_wide(gsum)
+    order_squeeze, order_expand = xs + ys + zs, ys + xs + zs
+    order_short = (xs + ys + zs, ys + xs + zs)
+    halving = lambda made, order: Halving(made[0], order, flat, devices, made[1], core_bit)
+    s_squeeze_grad = halving(
+        outer_halves(core, first_out, right_n, gpre_squeeze, full((pixels, mid)), whole, blocks, 1), order_squeeze
+    )
+    g_both = after(g_both, s_squeeze_grad.keep)
+    token = s_squeeze_grad.moves.pop(0)(g_both)
 
     gpre_expand, gpre_short, grad_spatial, gsum = call(
         expand_back_kernel,
         (blocks,),
         [
             wide_spec, wide_spec, wide_spec, e_spec, s_spec, tile_n(rows=16), count_spec, p_expand, p_short,
-            mask_spec, cols(mid, TILE), mid_spec, tile_at(0), p_spatial,
+            mask_spec, cols(mid, TILE), mid_spec, all_tiles, p_spatial,
         ],
-        [wide_spec, wide_spec, mid_spec, full((8, LANES))],
+        [wide_spec, wide_spec, mid_spec, all_tiles],
         [shaped((pixels, c_out), BF16), shaped((pixels, c_out), BF16), mid_f32, one_tile],
         flops=2 * pixels * mid * c_out, nbytes=11 << 20,
     )(
         grad_joined, pre_expand, pre_short, s_both, s_both, g_both, s_reduce, params, params, mask, w_expand,
         pre_spatial, s_spatial, params,
     )
-    g_spatial = sync(gsum)
+    s_expand_grad = halving(
+        outer_halves(core, act_spatial, left_const, gpre_expand, right_n, whole, blocks, blocks), order_expand
+    )
+    s_short_grad = [
+        halving(
+            outer_halves(
+                core, planes.reshape(4 * pixels, c_in), pl.BlockSpec((pixels, TILE), lambda b, *_, k=k: (0, k)),
+                gpre_short, right_n, whole, blocks, blocks,
+            ),
+            order_short[k % 2],
+        )
+        for k in range(in_blocks)
+    ]
+    g_spatial = after(
+        sync(gsum), s_expand_grad.keep, [s.keep for s in s_short_grad], s_squeeze_grad.received
+    )
+    for stream in [s_expand_grad] + s_short_grad:
+        token = stream.moves.pop(0)(g_spatial)
 
     gshift_spatial, grad_reduce, gsum = call(
         functools.partial(spatial_back_kernel, width, height),
         (3,),
         [
-            mid_spec, mid_spec, tile_at(0), tile_at(0), count_spec, p_spatial, mask_spec, tap_spec,
-            full((4, pixels, mid)), tile_at(0), p_reduce,
+            mid_spec, mid_spec, all_tiles, all_tiles, count_spec, p_spatial, mask_spec, tap_spec,
+            full((4, pixels, mid)), all_tiles, p_reduce,
         ],
-        [full((4, pixels, mid)), full((4, pixels, mid)), full((8, LANES))],
+        [full((4, pixels, mid)), full((4, pixels, mid)), all_tiles],
         [shaped((4, pixels, mid), BF16), shaped((4, pixels, mid)), one_tile],
         flops=18 * pixels * mid * mid, nbytes=12 << 20,
     )(grad_spatial, pre_spatial, s_spatial, g_spatial, s_reduce, params, mask, w_spatial, pre_reduce, s_reduce, params)
-    g_reduce = sync(gsum)
+    order_spatial, order_reduce = (zs[:1] + xs + ys + zs[1:], xs + ys + zs), ys + xs + zs
+    spatial_parts = ((0, 5), (5, 4))
+    late = [
+        halving(
+            outer_halves(
+                core, act_reduce, pl.BlockSpec((1, pixels, mid), functools.partial(spatial_plane, place)),
+                gshift_spatial, full((4, pixels, mid)), functools.partial(spatial_taps, place), count, 1,
+            ),
+            order,
+        )
+        for (place, count), order in zip(spatial_parts, order_spatial)
+    ]
 
     back_short = call(
         short_back_kernel,
@@ -868,12 +1073,19 @@
         shaped((pixels, c_in)),
         flops=2 * pixels * c_in * c_out, nbytes=6 << 20,
     )(gpre_short, w_shortcut)
+    crossed = [s.received for s in [s_expand_grad] + s_short_grad]
+    g_reduce = after(sync(gsum), [s.keep for s in late], back_short, crossed)
+    spread = TILE // dp
+    early = Halving(early_sum.reshape(9 + blocks, spread, TILE), rep_bits, flat, devices)
+    middle = [s_squeeze_grad, s_expand_grad] + s_short_grad
+    token = run_streams(middle + late + [None, early], SCHEDULE[:FIRST], g_reduce, False)
+    g_reduce = after(g_reduce, token)
 
     gpre_reduce, image_grad = call(
         functools.partial(reduce_back_kernel, quarter),
         (steps,),
         [
-            plane_block(mid), plane_block(mid), tile_at(0), tile_at(0), count_spec, p_reduce,
+            plane_block(mid), plane_block(mid), all_tiles, all_tiles, count_spec, p_reduce,
             pl.BlockSpec((quarter, LANES), lambda k: (k, 0)), full((c_in, mid)),
             pl.BlockSpec((quarter, c_in), lambda k: (k, 0)), full(perm.shape),
         ],
@@ -881,66 +1093,63 @@
         [shaped((4, pixels, mid), BF16), shaped((images * 4 * height * width, c_in), BF16)],
         flops=8 * pixels * c_in * mid, nbytes=10 << 20,
     )(grad_reduce, pre_reduce, s_reduce, g_reduce, s_reduce, params, mask, w_reduce, back_short, perm_back)
-
-    area = width * height
-
-    def whole(ref, b):
-        return ref[...]
-
-    def window_taps(ref, b):
-        r, c = lax.div(b, 3), lax.rem(b, 3)
-        first = pl.multiple_of((2 - r) * width, width)
-        return window_rows(ref, c, first, area, images)
-
-    def spatial_taps(ref, b):
-        r, c = lax.div(b, 3), lax.rem(b, 3)
-        return ref[2 * jnp.where(r == 0, 1, 0) + jnp.where(c == 0, 1, 0)]
-
-    def spatial_plane(b, *_):
-        r, c = lax.div(b, 3), lax.rem(b, 3)
-        return (2 * jnp.where(r == 1, 0, 1) + jnp.where(c == 1, 0, 1), 0, 0)
-
-    in_blocks = c_in // TILE
-    left_const = pl.BlockSpec((pixels, TILE), lambda b, *_: (0, 0))
-    right_n = pl.BlockSpec((pixels, TILE), lambda b, *_: (0, b))
-    made = outer(core, act_squeeze, left_const, gpad_window, full(padded), window_taps, 9, 9, 0, 9 + in_blocks * blocks, None)
-    one = outer(
-        core, planes.reshape(4 * pixels, c_in), pl.BlockSpec((pixels, TILE), lambda b, *_: (0, lax.div(b, blocks))),
-        gpre_short, pl.BlockSpec((pixels, TILE), lambda b, *_: (0, lax.rem(b, blocks))),
-        whole, in_blocks * blocks, blocks, 9, 9 + in_blocks * blocks, made,
-    )
-    made = outer(core, act_window, left_const, gpre_widen, right_n, whole, blocks, blocks, 0, 9 + blocks + in_blocks, None)
-    made = outer(
-        core, act_reduce, pl.BlockSpec((1, pixels, mid), spatial_plane), gshift_spatial, full((4, pixels, mid)),
-        spatial_taps, 9, 1, blocks, 9 + blocks + in_blocks, made,
-    )
-    two = outer(
-        core, planes.reshape(4 * pixels, c_in), pl.BlockSpec((4 * pixels, TILE), lambda b, *_: (0, b)),
-        gpre_reduce.reshape(4 * pixels, mid), full((4 * pixels, mid)), whole, in_blocks, 1,
-        9 + blocks, 9 + blocks + in_blocks, made,
-    )
-    made = outer(core, first_out, right_n, gpre_squeeze, full((pixels, mid)), whole, blocks, 1, 0, 2 * blocks, None)
-    three = outer(core, act_spatial, left_const, gpre_expand, right_n, whole, blocks, blocks, blocks, 2 * blocks, made)
-
-    order_one = x_bits + y_bits + z_bits
-    order_two = y_bits + z_bits[:1] + x_bits + z_bits[1:]
-    order_three = z_bits[:1] + x_bits + y_bits + z_bits[1:]
-    orders = (order_one, order_two, order_three)
-    shards = [
-        scatter_sum(keep, send, flat, core_bit, order, devices)
-        for (keep, send), order in zip((one, two, three), orders)
-    ]
-    halves = [gather_back(shard, flat, core_bit, order, devices) for shard, order in zip(shards, orders)]
+    late.append(
+        halving(
+            outer_halves(
+                core, planes.reshape(4 * pixels, c_in), pl.BlockSpec((4 * pixels, TILE), lambda b, *_: (0, b)),
+                gpre_reduce.reshape(4 * pixels, mid), full((4 * pixels, mid)), whole, in_blocks, 1,
+            ),
+            order_reduce,
+        )
+    )
+
     tall, flat_cols = lambda b: (b, 0), lambda b: (0, b)
-    grad_w_window = assemble(core, *halves[0], 0, 9, (9 * mid, mid), tall).reshape(3, 3, mid, mid)
-    grad_w_short = assemble(
-        core, *halves[0], 9, in_blocks * blocks, (c_in, c_out), lambda b: (lax.div(b, blocks), lax.rem(b, blocks))
-    )
-    grad_w_widen = assemble(core, *halves[1], 0, blocks, (mid, c_out), flat_cols)
-    grad_w_spatial = assemble(core, *halves[1], blocks, 9, (9 * mid, mid), tall).reshape(3, 3, mid, mid)
-    grad_w_reduce = assemble(core, *halves[1], 9 + blocks, in_blocks, (c_in, mid), tall)
-    grad_w_squeeze = assemble(core, *halves[2], 0, blocks, (c_out, mid), tall)
-    grad_w_expand = assemble(core, *halves[2], blocks, blocks, (mid, c_out), flat_cols)
+    backs = [Return(stream, core_bit, flat, devices) for stream in late]
+    for stream, back in zip(late, backs):
+        stream.moves.extend(back.moves)
+    token = run_streams(middle + late + [early], SCHEDULE[FIRST:], after(token, late[2].keep))
+
+    def starts_of(first, order, rows):
+        found = []
+        for k in range(devices):
+            start, left = first(k), rows
+            for bit in order:
+                left //= 2
+                start += (k // bit % 2) * left
+            found.append(start)
+        return tuple(found)
+
+    spread_starts = starts_of(lambda k: (k // rep) * spread, rep_bits, spread)
+
+    def gathered(shard):
+        everything = lax.all_gather(shard.reshape(-1, TILE), AXES, axis=0, tiled=False)
+        return functools.partial(regroup, everything, total=shard.shape[0])
+
+    regrouped = gathered(early.keep)
+    grad_w_widen = regrouped(spread_starts, place=0, blocks=blocks, shape=(mid, c_out), where=flat_cols)
+    grad_w_window = regrouped(spread_starts, place=blocks, blocks=9, shape=(9 * mid, mid), where=tall)
+
+    half_starts = lambda order: starts_of(lambda k: (k // core_bit % 2) * (TILE // 2), order, TILE // 2)
+    regrouped = gathered(jnp.concatenate([s.keep for s in middle], axis=0))
+    grad_w_squeeze = regrouped(half_starts(order_squeeze), place=0, blocks=blocks, shape=(c_out, mid), where=tall)
+    grad_w_expand = regrouped(
+        half_starts(order_expand), place=blocks, blocks=blocks, shape=(mid, c_out), where=flat_cols
+    )
+    grad_w_short = None
+    for k in range(in_blocks):
+        grad_w_short = regrouped(
+            half_starts(order_short[k % 2]), place=(2 + k) * blocks, blocks=blocks, shape=(c_in, c_out),
+            where=lambda b, k=k: (k, b), into=grad_w_short,
+        )
+
+    grad_w_spatial = None
+    for (place, count), back in zip(spatial_parts, backs):
+        grad_w_spatial = assemble(
+            back.places(), back.pieces(), 0, count, (9 * mid, mid), lambda b, place=place: (place + b, 0),
+            into=grad_w_spatial,
+        )
+    grad_w_reduce = assemble(backs[2].places(), backs[2].pieces(), 0, in_blocks, (c_in, mid), tall)
+    grad_w_window, grad_w_spatial = (g.reshape(3, 3, mid, mid) for g in (grad_w_window, grad_w_spatial))
 
     shift_total = vector(g_both, 0, 16)
     return (
@@ -950,10 +1159,10 @@
         grad_w_spatial,
         grad_w_expand,
         grad_w_short,
-        vector(g_reduce, ROWS, 8),
-        vector(g_reduce, 0, 8),
-        vector(g_spatial, ROWS, 8),
-        vector(g_spatial, 0, 8),
+        vector(jnp.sum(g_reduce, axis=0), ROWS, 8),
+        vector(jnp.sum(g_reduce, axis=0), 0, 8),
+        vector(jnp.sum(g_spatial, axis=0), ROWS, 8),
+        vector(jnp.sum(g_spatial, axis=0), 0, 8),
         vector(g_both, ROWS, 16),
         shift_total,
         vector(g_both, 2 * ROWS, 16),
@@ -961,10 +1170,10 @@
         grad_w_squeeze,
         grad_w_window,
         grad_w_widen,
-        vector(g_squeeze, ROWS, 8),
-        vector(g_squeeze, 0, 8),
-        vector(g_window, ROWS, 8),
-        vector(g_window, 0, 8),
+        vector(jnp.sum(g_squeeze, axis=0), ROWS, 8),
+        vector(jnp.sum(g_squeeze, axis=0), 0, 8),
+        vector(jnp.sum(g_window, axis=0), ROWS, 8),
+        vector(jnp.sum(g_window, axis=0), 0, 8),
         vector(g_widen, ROWS, 8),
         vector(g_widen, 0, 8),
     )

time: 986 us -> 704 us (0.71)
  waiting for transfers between devices: 563 us -> 323 us
  Pallas kernels: 107 us -> 193 us
  local copies, waits for them, and re-layouts: 89.5 us -> 9.57 us
  other arithmetic: 96.3 us -> 51.5 us
  blocking collectives: 59.6 us -> 34.1 us
  starting transfers between devices: 58 us -> 73.5 us
  between operations: 2.23 us -> 15.1 us
    ppermute x50 -> x75, waiting for transfers between devices: 552 us -> 306 us  [swap(): return lax.ppermute(values, AXES, [(i, i ^ bit) for i in range(devices)])]
    unnamed x214 -> x108, local copies, waits for them, and re-layouts: 83.9 us -> 4.77 us
    pallas_call x17 -> x21, Pallas kernels: 70.6 us -> 115 us  [the longest x6 34.5 us: regroup(): pl.pallas_call(functools.partial(regroup_kernel, starts), grid=(blocks,),...]
    select_n x12 -> x9, other arithmetic: 32.5 us -> 1.9 us  [join_halves(): jnp.where(own == 0, jnp.concatenate([values, other], axis=1), jnp.concate...]
    all_to_all x5 -> x3, blocking collectives: 59.6 us -> 34.1 us  [sync_all(): return lax.all_to_all(tile, AXES, 0, 0, tiled=True)]
    add x15 -> x65, other arithmetic: 56.4 us -> 40 us  [the longest x57 39 us: half_sum(): first + lax.dynamic_slice_in_dim(received, which * rows, rows, axis=1)]
    all_to_all x3 -> x5, starting transfers between devices: 13.5 us -> 21.9 us  [sync_all(): return lax.all_to_all(tile, AXES, 0, 0, tiled=True)]
    ppermute x50 -> x75, starting transfers between devices: 44.5 us -> 51.3 us  [swap(): return lax.ppermute(values, AXES, [(i, i ^ bit) for i in range(devices)])]
  transfers between devices with their start and end apart: 53 -> 83, of which waited for: 40 -> 51; matrix products, arithmetic and copies ran while one was open for 10% -> 7% of each run, Pallas kernels for 6% -> 16%
where the time goes in v2:
time: 704 us; the launch traced here: 700 us
  waiting for transfers between devices  323 us (46%)
  Pallas kernels  193 us (27%)
  starting transfers between devices  73.5 us (10%)
  other arithmetic  51.5 us (7%)
  blocking collectives  34.1 us (5%)
  between operations  15.1 us (2%)
  local copies, waits for them, and re-layouts  9.57 us (1%)
    ppermute x75, waiting for transfers between devices, swap(): return lax.ppermute(values, AXES, [(i, i ^ bit) for i in range(devices)])  306 us
    ppermute x75, starting transfers between devices, swap(): return lax.ppermute(values, AXES, [(i, i ^ bit) for i in range(devices)])  51.3 us
    add x57, other arithmetic, half_sum(): first + lax.dynamic_slice_in_dim(received, which * rows, rows, axis=1)  39 us
    pallas_call x6, Pallas kernels, regroup(): pl.pallas_call(functools.partial(regroup_kernel, starts), grid=(blocks,),...  34.5 us
    all_to_all x3, blocking collectives, sync_all(): return lax.all_to_all(tile, AXES, 0, 0, tiled=True)  34.1 us
    pallas_call x7, Pallas kernels, outer_halves(): pl.pallas_call(functools.partial(halves_kernel, pick, per_left), grid_spe...  33.5 us
    all_to_all x5, starting transfers between devices, sync_all(): return lax.all_to_all(tile, AXES, 0, 0, tiled=True)  21.9 us
    all_to_all x5, waiting for transfers between devices, sync_all(): return lax.all_to_all(tile, AXES, 0, 0, tiled=True)  16.7 us
  transfers between devices with their start and end apart: 83, of which 51 were waited for; matrix products, arithmetic and copies ran while one was open for 7% of the time, Pallas kernels for 16%

profile of v2, /device:TPU:0, one launch (start us, length us, event | category | flops | bytes accessed | tf_op | source)
XLA Modules:
  0.0 699.9 jit_solution(5176124580138882887)
XLA Ops:
  9.5 6.1 shard_map.434
  15.6 7.3 %all-to-all-start = ((f32[32,16,128]{2,1,0:T(8,128)}), f32[32,16,128]{2,1,0:T(8,128)S(1)}, u32[]{:S(2)}, u32[]{:S(2)}) async-start(f32[32,16,128]{2,1,0:T(8,128)} %get-tuple-element.244), calls=%async_computation | async-start | bytes 524288 | tf_op jit(solution)/shard_map/all_to_all | solution.py:668
  23.2 9.9 %all-to-all-done.stat_ref.count_ref.in_stat_ref = f32[32,16,128]{2,1,0:T(8,128)S(1)} async-done(((f32[32,16,128]{2,1,0:T(8,128)}), f32[32,16,128]{2,1,0:T(8,128)S(1)}, u32[]{:S(2)}, u32[]{:S(2)}) %all-to-all-start) | async-done | bytes 262176 | tf_op jit(solution)/shard_map/all_to_all | solution.py:668
  33.8 7.3 %shard_map.435 = (bf16[4,256,512]{2,1,0:T(8,128)(2,1)}, f32[256,512]{1,0:T(8,128)}, f32[32,8,128]{2,1,0:T(8,128)}) custom-call(f32[4,256,512]{2,1,0:T(8,128)} %get-tuple-element.243.pre_ref.in_ref, f32[32,16,128]{2,1,0:T(8,128)} %copy-done, f32[32,16,128]{2,1,0:T(8,128)} %copy-done, f32[128,128]{1,0:T(8,128)} %copy-done.1, f32[256,128]{1,0:T(8,128)} %bitcast.78, ...), custom_call_target="tpu_custom_call" | custom-call | flops 1207959552 | bytes 8388608 | tf_op jit(solution)/shard_map/pallas_call | solution.py:893
  43.9 5.1 shard_map.437
  52.9 4.8 shard_map.436
  67.5 3.9 collective-permute-done.3
  71.8 4.5 collective-permute-done.4
  77.0 6.1 shard_map.438
  83.1 11.7 %all_to_all.40.stat_ref.in_stat_ref = f32[32,8,128]{2,1,0:T(8,128)} all-to-all(f32[32,8,128]{2,1,0:T(8,128)} %get-tuple-element.253), channel_id=1, replica_groups=mesh['dp'=8,'rep'=4] {'dp','rep'}, dimensions={0} | all-to-all | bytes 262144 | tf_op jit(solution)/shard_map/all_to_all | solution.py:668
  94.8 5.7 shard_map.439
  100.5 11.7 %all_to_all.41.stat_ref.in_stat_ref = f32[32,8,128]{2,1,0:T(8,128)} all-to-all(f32[32,8,128]{2,1,0:T(8,128)} %get-tuple-element.255), channel_id=1, replica_groups=mesh['dp'=8,'rep'=4] {'dp','rep'}, dimensions={0} | all-to-all | bytes 262144 | tf_op jit(solution)/shard_map/all_to_all | solution.py:668
  112.1 4.8 shard_map.440
  126.6 3.7 collective-permute-done.8
  130.7 4.3 collective-permute-done.9
  135.6 5.4 shard_map.441
  150.6 3.7 collective-permute-done.13
  154.7 4.2 collective-permute-done.14
  159.6 6.3 shard_map.442
  168.5 4.8 shard_map.443.refs_0_
  177.5 6.6 shard_map.444
  184.1 7.8 %shard_map.455 = f32[8,832,512]{2,1,0:T(8,128)} custom-call(bf16[256,512]{1,0:T(8,128)(2,1)} %get-tuple-element.298.left_ref, bf16[3,2,160,512]{3,2,1,0:T(8,128)(2,1)} %get-tuple-element.299.right_ref, f32[8,832,512]{2,1,0:T(8,128)} %shard_map.443.refs_0_), custom_call_target="tpu_custom_call", output_to_operand_aliasing={{}: (2, {})} | custom-call | flops 1207959552 | bytes 9437184 | tf_op jit(solution)/shard_map/pallas_call | solution.py:576
  192.8 10.8 %all_to_all.42.gsum_ref = f32[32,8,128]{2,1,0:T(8,128)} all-to-all(f32[32,8,128]{2,1,0:T(8,128)S(1)} %copy-done.33), channel_id=1, replica_groups=mesh['dp'=8,'rep'=4] {'dp','rep'}, dimensions={0} | all-to-all | bytes 262144 | tf_op jit(solution)/shard_map/all_to_all | solution.py:668
  203.6 8.8 %shard_map.445 = (bf16[256,512]{1,0:T(8,128)(2,1)}, f32[256,2048]{1,0:T(8,128)}, f32[64,128]{1,0:T(8,128)}) custom-call(f32[256,512]{1,0:T(8,128)} %get-tuple-element.267.grad_ref, f32[256,512]{1,0:T(8,128)} %get-tuple-element.252.pre_ref.in_ref, f32[32,8,128]{2,1,0:T(8,128)} %all_to_all.40.stat_ref.in_stat_ref, f32[32,8,128]{2,1,0:T(8,128)} %all_to_all.42.gsum_ref, ...), custom_call_target="tpu_custom_call" | custom-call | flops 536870912 | bytes 11534336 | tf_op jit(solution)/shard_map/pallas_call | solution.py:986
  223.0 3.9 collective-permute-done.18
  227.4 4.7 shard_map.446
  232.7 7.6 %shard_map.447 = (bf16[256,2048]{1,0:T(8,128)(2,1)}, bf16[256,2048]{1,0:T(8,128)(2,1)}, f32[256,512]{1,0:T(8,128)}, f32[32,8,128]{2,1,0:T(8,128)}) custom-call(f32[256,2048]{1,0:T(8,128)} %get-tuple-element.269.gj_ref, f32[256,2048]{1,0:T(8,128)} %get-tuple-element.247.pe_ref, f32[256,2048]{1,0:T(8,128)} %get-tuple-element.249.ps_ref, ...), custom_call_target="tpu_custom_call" | custom-call | flops 536870912 | bytes 11534336 | tf_op jit(solution)/shard_map/pallas_call | solution.py:1011
  243.8 4.6 shard_map.449
  248.4 4.5 shard_map.450
  252.9 4.6 shard_map.448
  258.4 9.8 %shard_map.451 = (bf16[4,256,512]{2,1,0:T(8,128)(2,1)}, f32[4,256,512]{2,1,0:T(8,128)}, f32[32,8,128]{2,1,0:T(8,128)}) custom-call(f32[256,512]{1,0:T(8,128)} %get-tuple-element.274.grad_ref, f32[256,512]{1,0:T(8,128)} %get-tuple-element.245.pre_ref.in_ref, f32[32,8,128]{2,1,0:T(8,128)} %copy-done.6, f32[32,8,128]{2,1,0:T(8,128)} %copy-done.20, ...), custom_call_target="tpu_custom_call" | custom-call | flops 1207959552 | bytes 12582912 | tf_op jit(solution)/shard_map/pallas_call | solution.py:1044
  268.1 5.8 shard_map.452
  274.2 5.8 all-to-all-start.7
  280.2 5.4 shard_map.454.short_ref
  285.5 4.9 shard_map.453
  304.7 6.6 shard_map.456
  311.3 4.4 shard_map.457
  329.6 12.0 %collective-permute-done.29 = f32[4,128,512]{2,1,0:T(8,128)} collective-permute-done((f32[4,128,512]{2,1,0:T(8,128)}, f32[4,128,512]{2,1,0:T(8,128)}, u32[]{:S(2)}, u32[]{:S(2)}) %collective-permute-start.29) | collective-permute-done | bytes 1048608 | tf_op jit(solution)/shard_map/ppermute | solution.py:664
  361.5 15.0 %collective-permute-done.32 = f32[4,128,512]{2,1,0:T(8,128)} collective-permute-done((f32[4,128,512]{2,1,0:T(8,128)}, f32[4,128,512]{2,1,0:T(8,128)}, u32[]{:S(2)}, u32[]{:S(2)}) %collective-permute-start.32) | collective-permute-done | bytes 1048608 | tf_op jit(solution)/shard_map/ppermute | solution.py:664
  383.6 7.7 %collective-permute-done.30 = f32[4,64,512]{2,1,0:T(8,128)S(1)} collective-permute-done((f32[4,64,512]{2,1,0:T(8,128)}, f32[4,64,512]{2,1,0:T(8,128)S(1)}, u32[]{:S(2)}, u32[]{:S(2)}) %collective-permute-start.30) | collective-permute-done | bytes 524320 | tf_op jit(solution)/shard_map/ppermute | solution.py:664
  392.8 12.8 %collective-permute-done.37 = f32[4,64,512]{2,1,0:T(8,128)S(1)} collective-permute-done((f32[4,64,512]{2,1,0:T(8,128)S(1)}, f32[4,64,512]{2,1,0:T(8,128)S(1)}, u32[]{:S(2)}, u32[]{:S(2)}) %collective-permute-start.37) | collective-permute-done | bytes 524320 | tf_op jit(solution)/shard_map/ppermute | solution.py:664
  407.9 13.0 %collective-permute-done.35 = f32[4,32,512]{2,1,0:T(8,128)S(1)} collective-permute-done((f32[4,32,512]{2,1,0:T(8,128)S(1)}, f32[4,32,512]{2,1,0:T(8,128)S(1)}, u32[]{:S(2)}, u32[]{:S(2)}) %collective-permute-start.35) | collective-permute-done | bytes 262176 | tf_op jit(solution)/shard_map/ppermute | solution.py:664
  427.9 22.8 %collective-permute-done.40 = f32[4,16,512]{2,1,0:T(8,128)S(1)} collective-permute-done((f32[4,16,512]{2,1,0:T(8,128)S(1)}, f32[4,16,512]{2,1,0:T(8,128)S(1)}, u32[]{:S(2)}, u32[]{:S(2)}) %collective-permute-start.40) | collective-permute-done | bytes 131104 | tf_op jit(solution)/shard_map/ppermute | solution.py:664
  453.9 11.4 %collective-permute-done.43 = f32[4,32,512]{2,1,0:T(8,128)S(1)} collective-permute-done((f32[4,32,512]{2,1,0:T(8,128)S(1)}, f32[4,32,512]{2,1,0:T(8,128)S(1)}, u32[]{:S(2)}, u32[]{:S(2)}) %collective-permute-start.43) | collective-permute-done | bytes 262176 | tf_op jit(solution)/shard_map/ppermute | solution.py:664
  467.0 7.5 %collective-permute-done.48 = f32[4,32,512]{2,1,0:T(8,128)S(1)} collective-permute-done((f32[4,32,512]{2,1,0:T(8,128)S(1)}, f32[4,32,512]{2,1,0:T(8,128)S(1)}, u32[]{:S(2)}, u32[]{:S(2)}) %collective-permute-start.48) | collective-permute-done | bytes 262176 | tf_op jit(solution)/shard_map/ppermute | solution.py:664
  478.1 10.6 %collective-permute-done.53 = f32[4,32,512]{2,1,0:T(8,128)S(1)} collective-permute-done((f32[4,32,512]{2,1,0:T(8,128)S(1)}, f32[4,32,512]{2,1,0:T(8,128)S(1)}, u32[]{:S(2)}, u32[]{:S(2)}) %collective-permute-start.53) | collective-permute-done | bytes 262176 | tf_op jit(solution)/shard_map/ppermute | solution.py:664
  494.9 4.2 collective-permute-done.50
  499.4 8.0 %collective-permute-done.56 = f32[4,16,512]{2,1,0:T(8,128)S(1)} collective-permute-done((f32[4,16,512]{2,1,0:T(8,128)S(1)}, f32[4,16,512]{2,1,0:T(8,128)S(1)}, u32[]{:S(2)}, u32[]{:S(2)}) %collective-permute-start.56) | collective-permute-done | bytes 131104 | tf_op jit(solution)/shard_map/ppermute | solution.py:664
  507.5 8.3 %collective-permute-done.55 = f32[5,16,512]{2,1,0:T(8,128)S(1)} collective-permute-done((f32[5,16,512]{2,1,0:T(8,128)S(1)}, f32[5,16,512]{2,1,0:T(8,128)S(1)}, u32[]{:S(2)}, u32[]{:S(2)}) %collective-permute-start.55) | collective-permute-done | bytes 163872 | tf_op jit(solution)/shard_map/ppermute | solution.py:664
  523.8 10.1 %collective-permute-done.57 = f32[2,16,512]{2,1,0:T(8,128)S(1)} collective-permute-done((f32[2,16,512]{2,1,0:T(8,128)S(1)}, f32[2,16,512]{2,1,0:T(8,128)S(1)}, u32[]{:S(2)}, u32[]{:S(2)}) %collective-permute-start.57) | collective-permute-done | bytes 65568 | tf_op jit(solution)/shard_map/ppermute | solution.py:664
  533.9 6.4 collective-permute-done.62
  543.3 11.3 %collective-permute-done.60 = f32[2,32,512]{2,1,0:T(8,128)S(1)} collective-permute-done((f32[2,32,512]{2,1,0:T(8,128)S(1)}, f32[2,32,512]{2,1,0:T(8,128)S(1)}, u32[]{:S(2)}, u32[]{:S(2)}) %collective-permute-start.60) | collective-permute-done | bytes 131104 | tf_op jit(solution)/shard_map/ppermute | solution.py:664
  554.6 7.0 collective-permute-done.65
  561.8 9.0 %collective-permute-done.64 = f32[5,64,512]{2,1,0:T(8,128)} collective-permute-done((f32[5,64,512]{2,1,0:T(8,128)S(1)}, f32[5,64,512]{2,1,0:T(8,128)}, u32[]{:S(2)}, u32[]{:S(2)}) %collective-permute-start.64) | collective-permute-done | bytes 655392 | tf_op jit(solution)/shard_map/ppermute | solution.py:664
  575.2 32.6 %collective-permute-done.63 = f32[2,64,512]{2,1,0:T(8,128)S(1)} collective-permute-done((f32[2,64,512]{2,1,0:T(8,128)S(1)}, f32[2,64,512]{2,1,0:T(8,128)S(1)}, u32[]{:S(2)}, u32[]{:S(2)}) %collective-permute-start.63) | collective-permute-done | bytes 262176 | tf_op jit(solution)/shard_map/ppermute | solution.py:664
  608.0 22.0 %collective-permute-done.66.near_ref = f32[2,128,512]{2,1,0:T(8,128)S(1)} collective-permute-done((f32[2,128,512]{2,1,0:T(8,128)S(1)}, f32[2,128,512]{2,1,0:T(8,128)S(1)}, u32[]{:S(2)}, u32[]{:S(2)}) %collective-permute-start.66) | collective-permute-done | bytes 524320 | tf_op jit(solution)/shard_map/ppermute | solution.py:664
  645.3 7.4 %shard_map.459.refs_0_ = f32[4608,512]{1,0:T(8,128)} custom-call(s32[4]{0:T(128)} %pad_add_fusion.2.place_ref, f32[5,128,512]{2,1,0:T(8,128)} %copy-done.2, f32[5,128,512]{2,1,0:T(8,128)} %collective-permute-done.72.near_ref, f32[5,128,512]{2,1,0:T(8,128)} %collective-permute-done.73.far_ref, f32[5,128,512]{2,1,0:T(8,128)} %collective-permute-done.74.both_ref), custom_call_target="tpu_custom_call" | custom-call | bytes 10485760 | tf_op jit(solution)/shard_map/pallas_call | solution.py:601
  652.7 5.6 shard_map.460
  658.3 10.8 %shard_map.465 = f32[4608,512]{1,0:T(8,128)} custom-call(f32[32,208,512]{2,1,0:T(8,128)} %all-gather.5.cloned.1.call-done.in_ref), custom_call_target="tpu_custom_call" | custom-call | bytes 18874368 | tf_op jit(solution)/shard_map/pallas_call | solution.py:632
  669.1 4.7 shard_map.466
  673.8 4.7 shard_map.461
  678.6 4.7 shard_map.462.refs_0_
  683.3 4.7 shard_map.464
  688.1 4.7 shard_map.463
  (368 shorter events, 177.8 us)
Async XLA Ops:
  15.6 17.5 %all-to-all-start = ((f32[32,16,128]{2,1,0:T(8,128)}), f32[32,16,128]{2,1,0:T(8,128)S(1)}, u32[]{:S(2)}, u32[]{:S(2)}) async-start(f32[32,16,128]{2,1,0:T(8,128)} %get-tuple-element.244), calls=%async_computation | async-start | bytes 524288 | tf_op jit(solution)/shard_map/all_to_all | solution.py:668
  41.1 11.1 %all-to-all-start.1 = ((f32[32,8,128]{2,1,0:T(8,128)}), f32[32,8,128]{2,1,0:T(8,128)S(1)}, u32[]{:S(2)}, u32[]{:S(2)}) async-start(f32[32,8,128]{2,1,0:T(8,128)} %get-tuple-element.246), calls=%async_computation.1 | async-start | bytes 262144 | tf_op jit(solution)/shard_map/all_to_all | solution.py:668
  71.4 4.9 collective-permute-start.4
  130.3 4.6 collective-permute-start.9
  165.8 11.0 %all-to-all-start.4 = ((f32[32,8,128]{2,1,0:T(8,128)}), f32[32,8,128]{2,1,0:T(8,128)S(1)}, u32[]{:S(2)}, u32[]{:S(2)}) async-start(f32[32,8,128]{2,1,0:T(8,128)} %get-tuple-element.263), calls=%async_computation.4 | async-start | bytes 262144 | tf_op jit(solution)/shard_map/all_to_all | solution.py:668
  168.4 122.3 %reduce-scatter.2.cloned.1.call-start = ((), (), s32[]{:S(2)}) async-start(), calls=%async_computation.9 | async-start | bytes 15335424 | tf_op jit(solution)/shard_map/reduce_scatter | solution.py:983
  226.8 5.2 collective-permute-start.19
  232.7 24.9 %collective-permute-start.20 = (f32[4,256,512]{2,1,0:T(8,128)}, f32[4,256,512]{2,1,0:T(8,128)S(1)}, u32[]{:S(2)}, u32[]{:S(2)}) collective-permute-start(f32[4,256,512]{2,1,0:T(8,128)} %get-tuple-element.283), channel_id=1, source_target_pairs={{0,4},{1,5},{2,6},{3,7},{4,0},{5,1},{6,2},{7,3},{8,12},{9,13},{10,... | collective-permute-start | bytes 6291464 | tf_op jit(solution)/shard_map/ppermute | solution.py:664
  240.3 17.2 %all-to-all-start.6 = ((f32[32,8,128]{2,1,0:T(8,128)}), f32[32,8,128]{2,1,0:T(8,128)S(1)}, u32[]{:S(2)}, u32[]{:S(2)}) async-start(f32[32,8,128]{2,1,0:T(8,128)} %get-tuple-element.275), calls=%async_computation.6 | async-start | bytes 262144 | tf_op jit(solution)/shard_map/all_to_all | solution.py:668
  257.5 33.1 %collective-permute-start.21 = (f32[4,256,512]{2,1,0:T(8,128)}, f32[4,256,512]{2,1,0:T(8,128)}, u32[]{:S(2)}, u32[]{:S(2)}) collective-permute-start(f32[4,256,512]{2,1,0:T(8,128)} %get-tuple-element.292), channel_id=1, source_target_pairs={{0,4},{1,5},{2,6},{3,7},{4,0},{5,1},{6,2},{7,3},{8,12},{9,13},{10,... | collective-permute-start | bytes 6291464 | tf_op jit(solution)/shard_map/ppermute | solution.py:664
  257.8 32.8 %collective-permute-start.22 = (f32[4,256,512]{2,1,0:T(8,128)}, f32[4,256,512]{2,1,0:T(8,128)}, u32[]{:S(2)}, u32[]{:S(2)}) collective-permute-start(f32[4,256,512]{2,1,0:T(8,128)} %get-tuple-element.294), channel_id=1, source_target_pairs={{0,4},{1,5},{2,6},{3,7},{4,0},{5,1},{6,2},{7,3},{8,12},{9,13},{10,... | collective-permute-start | bytes 6291464 | tf_op jit(solution)/shard_map/ppermute | solution.py:664
  258.1 32.5 %collective-permute-start.23 = (f32[4,256,512]{2,1,0:T(8,128)}, f32[4,256,512]{2,1,0:T(8,128)}, u32[]{:S(2)}, u32[]{:S(2)}) collective-permute-start(f32[4,256,512]{2,1,0:T(8,128)} %get-tuple-element.296), channel_id=1, source_target_pairs={{0,4},{1,5},{2,6},{3,7},{4,0},{5,1},{6,2},{7,3},{8,12},{9,13},{10,... | collective-permute-start | bytes 6291464 | tf_op jit(solution)/shard_map/ppermute | solution.py:664
  273.9 47.1 %collective-permute-start.26 = (f32[5,256,512]{2,1,0:T(8,128)}, f32[5,256,512]{2,1,0:T(8,128)}, u32[]{:S(2)}, u32[]{:S(2)}) collective-permute-start(f32[5,256,512]{2,1,0:T(8,128)} %get-tuple-element.315), channel_id=1, source_target_pairs={{0,4},{1,5},{2,6},{3,7},{4,0},{5,1},{6,2},{7,3},{8,12},{9,13},{10,... | collective-permute-start | bytes 7864328 | tf_op jit(solution)/shard_map/ppermute | solution.py:664
  274.2 16.4 %all-to-all-start.7 = ((f32[32,8,128]{2,1,0:T(8,128)}), f32[32,8,128]{2,1,0:T(8,128)S(1)}, u32[]{:S(2)}, u32[]{:S(2)}) async-start(f32[32,8,128]{2,1,0:T(8,128)} %get-tuple-element.286), calls=%async_computation.7 | async-start | bytes 262144 | tf_op jit(solution)/shard_map/all_to_all | solution.py:668
  280.1 378.2 %all-gather.5.cloned.1.call-start = ((), (), s32[]{:S(2)}) async-start(), calls=%async_computation.11 | async-start | bytes 14057472 | tf_op jit(solution)/shard_map/all_gather | solution.py:1125
  290.4 53.1 %collective-permute-start.34 = (f32[4,256,512]{2,1,0:T(8,128)}, f32[4,256,512]{2,1,0:T(8,128)}, u32[]{:S(2)}, u32[]{:S(2)}) collective-permute-start(f32[4,256,512]{2,1,0:T(8,128)} %get-tuple-element.316), channel_id=1, source_target_pairs={{0,4},{1,5},{2,6},{3,7},{4,0},{5,1},{6,2},{7,3},{8,12},{9,13},{10,... | collective-permute-start | bytes 6291464 | tf_op jit(solution)/shard_map/ppermute | solution.py:664
  292.3 23.4 %collective-permute-start.27 = (f32[13,32,512]{2,1,0:T(8,128)S(1)}, f32[13,32,512]{2,1,0:T(8,128)S(1)}, u32[]{:S(2)}, u32[]{:S(2)}) collective-permute-start(f32[13,32,512]{2,1,0:T(8,128)S(1)} %get-tuple-element.464), channel_id=1, source_target_pairs={{0,1},{1,0},{2,3},{3,2},{4,5},{5,4},{6,7},{7,6},{8,9},{9,8},{10,11... | collective-permute-start | bytes 2555912 | tf_op jit(solution)/shard_map/ppermute | solution.py:664
  296.8 29.6 %collective-permute-start.25 = (f32[4,128,512]{2,1,0:T(8,128)}, f32[4,128,512]{2,1,0:T(8,128)}, u32[]{:S(2)}, u32[]{:S(2)}) collective-permute-start(f32[4,128,512]{2,1,0:T(8,128)} %dynamic-slice_add_fusion.11), channel_id=1, source_target_pairs={{0,8},{1,9},{2,10},{3,11},{4,12},{5,13},{6,14},{7,15},{8,0},{9,1},... | collective-permute-start | bytes 3145736 | tf_op jit(solution)/shard_map/ppermute | solution.py:664
  315.7 12.8 %collective-permute-start.24 = (f32[2,256,512]{2,1,0:T(8,128)}, f32[2,256,512]{2,1,0:T(8,128)}, u32[]{:S(2)}, u32[]{:S(2)}) collective-permute-start(f32[2,256,512]{2,1,0:T(8,128)} %get-tuple-element.317), channel_id=1, source_target_pairs={{0,4},{1,5},{2,6},{3,7},{4,0},{5,1},{6,2},{7,3},{8,12},{9,13},{10,... | collective-permute-start | bytes 3145736 | tf_op jit(solution)/shard_map/ppermute | solution.py:664
  315.7 25.9 %collective-permute-start.29 = (f32[4,128,512]{2,1,0:T(8,128)}, f32[4,128,512]{2,1,0:T(8,128)}, u32[]{:S(2)}, u32[]{:S(2)}) collective-permute-start(f32[4,128,512]{2,1,0:T(8,128)} %dynamic-slice_add_fusion.10), channel_id=1, source_target_pairs={{0,16},{1,17},{2,18},{3,19},{4,20},{5,21},{6,22},{7,23},{8,24},{9,... | collective-permute-start | bytes 3145736 | tf_op jit(solution)/shard_map/ppermute | solution.py:664
  321.1 24.9 %collective-permute-start.33 = (f32[13,16,512]{2,1,0:T(8,128)S(1)}, f32[13,16,512]{2,1,0:T(8,128)S(1)}, u32[]{:S(2)}, u32[]{:S(2)}) collective-permute-start(f32[13,16,512]{2,1,0:T(8,128)S(1)} %dynamic-slice_add_fusion.27), channel_id=1, source_target_pairs={{0,2},{1,3},{2,0},{3,1},{4,6},{5,7},{6,4},{7,5},{8,10},{9,11},{10,... | collective-permute-start | bytes 1277960 | tf_op jit(solution)/shard_map/ppermute | solution.py:664
  346.8 327.1 %all-gather.3.cloned.1.call-start = ((), (), s32[]{:S(2)}) async-start(), calls=%async_computation.10 | async-start | bytes 17301504 | tf_op jit(solution)/shard_map/all_gather | solution.py:1125
  347.1 29.5 %collective-permute-start.32 = (f32[4,128,512]{2,1,0:T(8,128)}, f32[4,128,512]{2,1,0:T(8,128)}, u32[]{:S(2)}, u32[]{:S(2)}) collective-permute-start(f32[4,128,512]{2,1,0:T(8,128)} %dynamic-slice_add_fusion.8), channel_id=1, source_target_pairs={{0,8},{1,9},{2,10},{3,11},{4,12},{5,13},{6,14},{7,15},{8,0},{9,1},... | collective-permute-start | bytes 3145736 | tf_op jit(solution)/shard_map/ppermute | solution.py:664
  347.7 31.5 %collective-permute-start.31 = (f32[4,128,512]{2,1,0:T(8,128)}, f32[4,128,512]{2,1,0:T(8,128)}, u32[]{:S(2)}, u32[]{:S(2)}) collective-permute-start(f32[4,128,512]{2,1,0:T(8,128)} %dynamic-slice_add_fusion.9), channel_id=1, source_target_pairs={{0,16},{1,17},{2,18},{3,19},{4,20},{5,21},{6,22},{7,23},{8,24},{9,... | collective-permute-start | bytes 3145736 | tf_op jit(solution)/shard_map/ppermute | solution.py:664
  353.0 53.2 %collective-permute-start.36 = (f32[5,128,512]{2,1,0:T(8,128)S(1)}, f32[5,128,512]{2,1,0:T(8,128)S(1)}, u32[]{:S(2)}, u32[]{:S(2)}) collective-permute-start(f32[5,128,512]{2,1,0:T(8,128)S(1)} %copy-done.16), channel_id=1, source_target_pairs={{0,1},{1,0},{2,3},{3,2},{4,5},{5,4},{6,7},{7,6},{8,9},{9,8},{10,11... | collective-permute-start | bytes 3932168 | tf_op jit(solution)/shard_map/ppermute | solution.py:664
  355.8 66.2 %collective-permute-start.28 = (f32[2,128,512]{2,1,0:T(8,128)S(1)}, f32[2,128,512]{2,1,0:T(8,128)S(1)}, u32[]{:S(2)}, u32[]{:S(2)}) collective-permute-start(f32[2,128,512]{2,1,0:T(8,128)S(1)} %dynamic-slice_add_fusion.24), channel_id=1, source_target_pairs={{0,16},{1,17},{2,18},{3,19},{4,20},{5,21},{6,22},{7,23},{8,24},{9,... | collective-permute-start | bytes 1572872 | tf_op jit(solution)/shard_map/ppermute | solution.py:664
  356.1 35.2 %collective-permute-start.30 = (f32[4,64,512]{2,1,0:T(8,128)}, f32[4,64,512]{2,1,0:T(8,128)S(1)}, u32[]{:S(2)}, u32[]{:S(2)}) collective-permute-start(f32[4,64,512]{2,1,0:T(8,128)} %dynamic-slice_add_fusion.22), channel_id=1, source_target_pairs={{0,8},{1,9},{2,10},{3,11},{4,12},{5,13},{6,14},{7,15},{8,0},{9,1},... | collective-permute-start | bytes 1572872 | tf_op jit(solution)/shard_map/ppermute | solution.py:664
  376.6 29.0 %collective-permute-start.37 = (f32[4,64,512]{2,1,0:T(8,128)S(1)}, f32[4,64,512]{2,1,0:T(8,128)S(1)}, u32[]{:S(2)}, u32[]{:S(2)}) collective-permute-start(f32[4,64,512]{2,1,0:T(8,128)S(1)} %copy-done.31), channel_id=1, source_target_pairs={{0,16},{1,17},{2,18},{3,19},{4,20},{5,21},{6,22},{7,23},{8,24},{9,... | collective-permute-start | bytes 1572872 | tf_op jit(solution)/shard_map/ppermute | solution.py:664
  379.1 48.2 %collective-permute-start.41 = (f32[4,128,512]{2,1,0:T(8,128)S(1)}, f32[4,128,512]{2,1,0:T(8,128)S(1)}, u32[]{:S(2)}, u32[]{:S(2)}) collective-permute-start(f32[4,128,512]{2,1,0:T(8,128)S(1)} %copy-done.27), channel_id=1, source_target_pairs={{0,8},{1,9},{2,10},{3,11},{4,12},{5,13},{6,14},{7,15},{8,0},{9,1},... | collective-permute-start | bytes 3145736 | tf_op jit(solution)/shard_map/ppermute | solution.py:664
  391.3 59.4 %collective-permute-start.39 = (f32[4,64,512]{2,1,0:T(8,128)S(1)}, f32[4,64,512]{2,1,0:T(8,128)S(1)}, u32[]{:S(2)}, u32[]{:S(2)}) collective-permute-start(f32[4,64,512]{2,1,0:T(8,128)S(1)} %dynamic-slice_add_fusion.20), channel_id=1, source_target_pairs={{0,16},{1,17},{2,18},{3,19},{4,20},{5,21},{6,22},{7,23},{8,24},{9,... | collective-permute-start | bytes 1572872 | tf_op jit(solution)/shard_map/ppermute | solution.py:664
  405.6 15.3 %collective-permute-start.35 = (f32[4,32,512]{2,1,0:T(8,128)S(1)}, f32[4,32,512]{2,1,0:T(8,128)S(1)}, u32[]{:S(2)}, u32[]{:S(2)}) collective-permute-start(f32[4,32,512]{2,1,0:T(8,128)S(1)} %dynamic-slice_add_fusion.41), channel_id=1, source_target_pairs={{0,1},{1,0},{2,3},{3,2},{4,5},{5,4},{6,7},{7,6},{8,9},{9,8},{10,11... | collective-permute-start | bytes 786440 | tf_op jit(solution)/shard_map/ppermute | solution.py:664
  406.2 17.7 %collective-permute-start.42 = (f32[4,32,512]{2,1,0:T(8,128)S(1)}, f32[4,32,512]{2,1,0:T(8,128)S(1)}, u32[]{:S(2)}, u32[]{:S(2)}) collective-permute-start(f32[4,32,512]{2,1,0:T(8,128)S(1)} %dynamic-slice_add_fusion.39), channel_id=1, source_target_pairs={{0,1},{1,0},{2,3},{3,2},{4,5},{5,4},{6,7},{7,6},{8,9},{9,8},{10,11... | collective-permute-start | bytes 786440 | tf_op jit(solution)/shard_map/ppermute | solution.py:664
  420.9 30.8 %collective-permute-start.44 = (f32[4,64,512]{2,1,0:T(8,128)S(1)}, f32[4,64,512]{2,1,0:T(8,128)S(1)}, u32[]{:S(2)}, u32[]{:S(2)}) collective-permute-start(f32[4,64,512]{2,1,0:T(8,128)S(1)} %get-tuple-element.478), channel_id=1, source_target_pairs={{0,8},{1,9},{2,10},{3,11},{4,12},{5,13},{6,14},{7,15},{8,0},{9,1},... | collective-permute-start | bytes 1572872 | tf_op jit(solution)/shard_map/ppermute | solution.py:664
  422.0 56.0 %collective-permute-start.38 = (f32[2,64,512]{2,1,0:T(8,128)S(1)}, f32[2,64,512]{2,1,0:T(8,128)S(1)}, u32[]{:S(2)}, u32[]{:S(2)}) collective-permute-start(f32[2,64,512]{2,1,0:T(8,128)S(1)} %dynamic-slice_add_fusion.38), channel_id=1, source_target_pairs={{0,8},{1,9},{2,10},{3,11},{4,12},{5,13},{6,14},{7,15},{8,0},{9,1},... | collective-permute-start | bytes 786440 | tf_op jit(solution)/shard_map/ppermute | solution.py:664
  423.9 27.6 %collective-permute-start.45 = (f32[4,16,512]{2,1,0:T(8,128)S(1)}, f32[4,16,512]{2,1,0:T(8,128)S(1)}, u32[]{:S(2)}, u32[]{:S(2)}) collective-permute-start(f32[4,16,512]{2,1,0:T(8,128)S(1)} %dynamic-slice_add_fusion.53), channel_id=1, source_target_pairs={{0,2},{1,3},{2,0},{3,1},{4,6},{5,7},{6,4},{7,5},{8,10},{9,11},{10,... | collective-permute-start | bytes 393224 | tf_op jit(solution)/shard_map/ppermute | solution.py:664
  427.6 23.0 %collective-permute-start.40 = (f32[4,16,512]{2,1,0:T(8,128)S(1)}, f32[4,16,512]{2,1,0:T(8,128)S(1)}, u32[]{:S(2)}, u32[]{:S(2)}) collective-permute-start(f32[4,16,512]{2,1,0:T(8,128)S(1)} %dynamic-slice_add_fusion.55), channel_id=1, source_target_pairs={{0,2},{1,3},{2,0},{3,1},{4,6},{5,7},{6,4},{7,5},{8,10},{9,11},{10,... | collective-permute-start | bytes 393224 | tf_op jit(solution)/shard_map/ppermute | solution.py:664
  450.7 25.6 %collective-permute-start.47 = (f32[5,64,512]{2,1,0:T(8,128)S(1)}, f32[5,64,512]{2,1,0:T(8,128)S(1)}, u32[]{:S(2)}, u32[]{:S(2)}) collective-permute-start(f32[5,64,512]{2,1,0:T(8,128)S(1)} %dynamic-slice_add_fusion.13), channel_id=1, source_target_pairs={{0,8},{1,9},{2,10},{3,11},{4,12},{5,13},{6,14},{7,15},{8,0},{9,1},... | collective-permute-start | bytes 1966088 | tf_op jit(solution)/shard_map/ppermute | solution.py:664
  450.7 14.8 %collective-permute-start.49 = (f32[4,64,512]{2,1,0:T(8,128)S(1)}, f32[4,64,512]{2,1,0:T(8,128)S(1)}, u32[]{:S(2)}, u32[]{:S(2)}) collective-permute-start(f32[4,64,512]{2,1,0:T(8,128)S(1)} %dynamic-slice_add_fusion.16), channel_id=1, source_target_pairs={{0,16},{1,17},{2,18},{3,19},{4,20},{5,21},{6,22},{7,23},{8,24},{9,... | collective-permute-start | bytes 1572872 | tf_op jit(solution)/shard_map/ppermute | solution.py:664
  451.6 13.8 %collective-permute-start.43 = (f32[4,32,512]{2,1,0:T(8,128)S(1)}, f32[4,32,512]{2,1,0:T(8,128)S(1)}, u32[]{:S(2)}, u32[]{:S(2)}) collective-permute-start(f32[4,32,512]{2,1,0:T(8,128)S(1)} %dynamic-slice_add_fusion.35), channel_id=1, source_target_pairs={{0,1},{1,0},{2,3},{3,2},{4,5},{5,4},{6,7},{7,6},{8,9},{9,8},{10,11... | collective-permute-start | bytes 786440 | tf_op jit(solution)/shard_map/ppermute | solution.py:664
  451.7 22.8 %collective-permute-start.48 = (f32[4,32,512]{2,1,0:T(8,128)S(1)}, f32[4,32,512]{2,1,0:T(8,128)S(1)}, u32[]{:S(2)}, u32[]{:S(2)}) collective-permute-start(f32[4,32,512]{2,1,0:T(8,128)S(1)} %dynamic-slice_add_fusion.33), channel_id=1, source_target_pairs={{0,1},{1,0},{2,3},{3,2},{4,5},{5,4},{6,7},{7,6},{8,9},{9,8},{10,11... | collective-permute-start | bytes 786440 | tf_op jit(solution)/shard_map/ppermute | solution.py:664
  465.4 12.6 %collective-permute-start.46 = (f32[4,16,512]{2,1,0:T(8,128)S(1)}, f32[4,16,512]{2,1,0:T(8,128)S(1)}, u32[]{:S(2)}, u32[]{:S(2)}) collective-permute-start(f32[4,16,512]{2,1,0:T(8,128)S(1)} %dynamic-slice_add_fusion.51), channel_id=1, source_target_pairs={{0,2},{1,3},{2,0},{3,1},{4,6},{5,7},{6,4},{7,5},{8,10},{9,11},{10,... | collective-permute-start | bytes 393224 | tf_op jit(solution)/shard_map/ppermute | solution.py:664
  465.6 23.1 %collective-permute-start.53 = (f32[4,32,512]{2,1,0:T(8,128)S(1)}, f32[4,32,512]{2,1,0:T(8,128)S(1)}, u32[]{:S(2)}, u32[]{:S(2)}) collective-permute-start(f32[4,32,512]{2,1,0:T(8,128)S(1)} %dynamic-slice_add_fusion.31), channel_id=1, source_target_pairs={{0,1},{1,0},{2,3},{3,2},{4,5},{5,4},{6,7},{7,6},{8,9},{9,8},{10,11... | collective-permute-start | bytes 786440 | tf_op jit(solution)/shard_map/ppermute | solution.py:664
  474.6 16.2 %collective-permute-start.51 = (f32[4,16,512]{2,1,0:T(8,128)S(1)}, f32[4,16,512]{2,1,0:T(8,128)S(1)}, u32[]{:S(2)}, u32[]{:S(2)}) collective-permute-start(f32[4,16,512]{2,1,0:T(8,128)S(1)} %dynamic-slice_add_fusion.49), channel_id=1, source_target_pairs={{0,2},{1,3},{2,0},{3,1},{4,6},{5,7},{6,4},{7,5},{8,10},{9,11},{10,... | collective-permute-start | bytes 393224 | tf_op jit(solution)/shard_map/ppermute | solution.py:664
  476.3 12.5 %collective-permute-start.52 = (f32[5,32,512]{2,1,0:T(8,128)S(1)}, f32[5,32,512]{2,1,0:T(8,128)S(1)}, u32[]{:S(2)}, u32[]{:S(2)}) collective-permute-start(f32[5,32,512]{2,1,0:T(8,128)S(1)} %dynamic-slice_add_fusion.29), channel_id=1, source_target_pairs={{0,16},{1,17},{2,18},{3,19},{4,20},{5,21},{6,22},{7,23},{8,24},{9,... | collective-permute-start | bytes 983048 | tf_op jit(solution)/shard_map/ppermute | solution.py:664
  491.7 7.4 %collective-permute-start.50 = (f32[2,32,512]{2,1,0:T(8,128)S(1)}, f32[2,32,512]{2,1,0:T(8,128)S(1)}, u32[]{:S(2)}, u32[]{:S(2)}) collective-permute-start(f32[2,32,512]{2,1,0:T(8,128)S(1)} %dynamic-slice_add_fusion.48), channel_id=1, source_target_pairs={{0,1},{1,0},{2,3},{3,2},{4,5},{5,4},{6,7},{7,6},{8,9},{9,8},{10,11... | collective-permute-start | bytes 393224 | tf_op jit(solution)/shard_map/ppermute | solution.py:664
  491.8 15.6 %collective-permute-start.56 = (f32[4,16,512]{2,1,0:T(8,128)S(1)}, f32[4,16,512]{2,1,0:T(8,128)S(1)}, u32[]{:S(2)}, u32[]{:S(2)}) collective-permute-start(f32[4,16,512]{2,1,0:T(8,128)S(1)} %dynamic-slice_add_fusion.45), channel_id=1, source_target_pairs={{0,2},{1,3},{2,0},{3,1},{4,6},{5,7},{6,4},{7,5},{8,10},{9,11},{10,... | collective-permute-start | bytes 393224 | tf_op jit(solution)/shard_map/ppermute | solution.py:664
  492.5 23.4 %collective-permute-start.55 = (f32[5,16,512]{2,1,0:T(8,128)S(1)}, f32[5,16,512]{2,1,0:T(8,128)S(1)}, u32[]{:S(2)}, u32[]{:S(2)}) collective-permute-start(f32[5,16,512]{2,1,0:T(8,128)S(1)} %dynamic-slice_add_fusion.43), channel_id=1, source_target_pairs={{0,2},{1,3},{2,0},{3,1},{4,6},{5,7},{6,4},{7,5},{8,10},{9,11},{10,... | collective-permute-start | bytes 491528 | tf_op jit(solution)/shard_map/ppermute | solution.py:664
  499.1 18.1 %collective-permute-start.54 = (f32[2,16,512]{2,1,0:T(8,128)S(1)}, f32[2,16,512]{2,1,0:T(8,128)S(1)}, u32[]{:S(2)}, u32[]{:S(2)}) collective-permute-start(f32[2,16,512]{2,1,0:T(8,128)S(1)} %dynamic-slice_add_fusion.57), channel_id=1, source_target_pairs={{0,2},{1,3},{2,0},{3,1},{4,6},{5,7},{6,4},{7,5},{8,10},{9,11},{10,... | collective-permute-start | bytes 196616 | tf_op jit(solution)/shard_map/ppermute | solution.py:664
  507.4 12.6 %collective-permute-start.59 = (f32[4,16,512]{2,1,0:T(8,128)S(1)}, f32[4,16,512]{2,1,0:T(8,128)S(1)}, u32[]{:S(2)}, u32[]{:S(2)}) collective-permute-start(f32[4,16,512]{2,1,0:T(8,128)S(1)} %add.553), channel_id=1, source_target_pairs={{0,2},{1,3},{2,0},{3,1},{4,6},{5,7},{6,4},{7,5},{8,10},{9,11},{10,... | collective-permute-start | bytes 393224 | tf_op jit(solution)/shard_map/ppermute | solution.py:664
  515.9 6.4 collective-permute-start.58
  520.1 20.3 %collective-permute-start.62 = (f32[4,32,512]{2,1,0:T(8,128)S(1)}, f32[4,32,512]{2,1,0:T(8,128)S(1)}, u32[]{:S(2)}, u32[]{:S(2)}) collective-permute-start(f32[4,32,512]{2,1,0:T(8,128)S(1)} %maximum_select_fusion.6), channel_id=1, source_target_pairs={{0,1},{1,0},{2,3},{3,2},{4,5},{5,4},{6,7},{7,6},{8,9},{9,8},{10,11... | collective-permute-start | bytes 786440 | tf_op jit(solution)/shard_map/ppermute | solution.py:664
  522.3 18.2 %collective-permute-start.61 = (f32[5,32,512]{2,1,0:T(8,128)S(1)}, f32[5,32,512]{2,1,0:T(8,128)S(1)}, u32[]{:S(2)}, u32[]{:S(2)}) collective-permute-start(f32[5,32,512]{2,1,0:T(8,128)S(1)} %maximum_select_fusion.5), channel_id=1, source_target_pairs={{0,16},{1,17},{2,18},{3,19},{4,20},{5,21},{6,22},{7,23},{8,24},{9,... | collective-permute-start | bytes 983048 | tf_op jit(solution)/shard_map/ppermute | solution.py:664
  522.6 11.3 %collective-permute-start.57 = (f32[2,16,512]{2,1,0:T(8,128)S(1)}, f32[2,16,512]{2,1,0:T(8,128)S(1)}, u32[]{:S(2)}, u32[]{:S(2)}) collective-permute-start(f32[2,16,512]{2,1,0:T(8,128)S(1)} %add.555), channel_id=1, source_target_pairs={{0,2},{1,3},{2,0},{3,1},{4,6},{5,7},{6,4},{7,5},{8,10},{9,11},{10,... | collective-permute-start | bytes 196616 | tf_op jit(solution)/shard_map/ppermute | solution.py:664
  540.4 21.2 %collective-permute-start.65 = (f32[4,64,512]{2,1,0:T(8,128)S(1)}, f32[4,64,512]{2,1,0:T(8,128)S(1)}, u32[]{:S(2)}, u32[]{:S(2)}) collective-permute-start(f32[4,64,512]{2,1,0:T(8,128)S(1)} %maximum_select_fusion.3), channel_id=1, source_target_pairs={{0,16},{1,17},{2,18},{3,19},{4,20},{5,21},{6,22},{7,23},{8,24},{9,... | collective-permute-start | bytes 1572872 | tf_op jit(solution)/shard_map/ppermute | solution.py:664
  540.6 30.3 %collective-permute-start.64 = (f32[5,64,512]{2,1,0:T(8,128)S(1)}, f32[5,64,512]{2,1,0:T(8,128)}, u32[]{:S(2)}, u32[]{:S(2)}) collective-permute-start(f32[5,64,512]{2,1,0:T(8,128)S(1)} %maximum_select_fusion.2), channel_id=1, source_target_pairs={{0,8},{1,9},{2,10},{3,11},{4,12},{5,13},{6,14},{7,15},{8,0},{9,1},... | collective-permute-start | bytes 1966088 | tf_op jit(solution)/shard_map/ppermute | solution.py:664
  543.3 11.3 %collective-permute-start.60 = (f32[2,32,512]{2,1,0:T(8,128)S(1)}, f32[2,32,512]{2,1,0:T(8,128)S(1)}, u32[]{:S(2)}, u32[]{:S(2)}) collective-permute-start(f32[2,32,512]{2,1,0:T(8,128)S(1)} %maximum_select_fusion.8), channel_id=1, source_target_pairs={{0,1},{1,0},{2,3},{3,2},{4,5},{5,4},{6,7},{7,6},{8,9},{9,8},{10,11... | collective-permute-start | bytes 393224 | tf_op jit(solution)/shard_map/ppermute | solution.py:664
  572.4 61.0 %collective-permute-start.72 = (f32[5,128,512]{2,1,0:T(8,128)S(1)}, f32[5,128,512]{2,1,0:T(8,128)}, u32[]{:S(2)}, u32[]{:S(2)}) collective-permute-start(f32[5,128,512]{2,1,0:T(8,128)S(1)} %maximum_select_fusion.own_ref), channel_id=1, source_target_pairs={{0,1},{1,0},{2,3},{3,2},{4,5},{5,4},{6,7},{7,6},{8,9},{9,8},{10,11... | collective-permute-start | bytes 3932168 | tf_op jit(solution)/shard_map/ppermute | solution.py:664
  572.5 57.5 %collective-permute-start.69 = (f32[4,128,512]{2,1,0:T(8,128)S(1)}, f32[4,128,512]{2,1,0:T(8,128)S(1)}, u32[]{:S(2)}, u32[]{:S(2)}) collective-permute-start(f32[4,128,512]{2,1,0:T(8,128)S(1)} %maximum_select_fusion.1.own_ref), channel_id=1, source_target_pairs={{0,8},{1,9},{2,10},{3,11},{4,12},{5,13},{6,14},{7,15},{8,0},{9,1},... | collective-permute-start | bytes 3145736 | tf_op jit(solution)/shard_map/ppermute | solution.py:664
  575.1 32.7 %collective-permute-start.63 = (f32[2,64,512]{2,1,0:T(8,128)S(1)}, f32[2,64,512]{2,1,0:T(8,128)S(1)}, u32[]{:S(2)}, u32[]{:S(2)}) collective-permute-start(f32[2,64,512]{2,1,0:T(8,128)S(1)} %maximum_select_fusion.7), channel_id=1, source_target_pairs={{0,8},{1,9},{2,10},{3,11},{4,12},{5,13},{6,14},{7,15},{8,0},{9,1},... | collective-permute-start | bytes 786440 | tf_op jit(solution)/shard_map/ppermute | solution.py:664
  607.8 22.1 %collective-permute-start.66 = (f32[2,128,512]{2,1,0:T(8,128)S(1)}, f32[2,128,512]{2,1,0:T(8,128)S(1)}, u32[]{:S(2)}, u32[]{:S(2)}) collective-permute-start(f32[2,128,512]{2,1,0:T(8,128)S(1)} %maximum_select_fusion.4.own_ref), channel_id=1, source_target_pairs={{0,16},{1,17},{2,18},{3,19},{4,20},{5,21},{6,22},{7,23},{8,24},{9,... | collective-permute-start | bytes 1572872 | tf_op jit(solution)/shard_map/ppermute | solution.py:664
  607.9 37.4 %collective-permute-start.73 = (f32[5,128,512]{2,1,0:T(8,128)S(1)}, f32[5,128,512]{2,1,0:T(8,128)}, u32[]{:S(2)}, u32[]{:S(2)}) collective-permute-start(f32[5,128,512]{2,1,0:T(8,128)S(1)} %maximum_select_fusion.own_ref), channel_id=1, source_target_pairs={{0,4},{1,5},{2,6},{3,7},{4,0},{5,1},{6,2},{7,3},{8,12},{9,13},{10,... | collective-permute-start | bytes 3932168 | tf_op jit(solution)/shard_map/ppermute | solution.py:664
  633.4 11.9 %collective-permute-start.74 = (f32[5,128,512]{2,1,0:T(8,128)}, f32[5,128,512]{2,1,0:T(8,128)}, u32[]{:S(2)}, u32[]{:S(2)}) collective-permute-start(f32[5,128,512]{2,1,0:T(8,128)} %collective-permute-done.72.near_ref), channel_id=1, source_target_pairs={{0,4},{1,5},{2,6},{3,7},{4,0},{5,1},{6,2},{7,3},{8,12},{9,13},{10,... | collective-permute-start | bytes 3932168 | tf_op jit(solution)/shard_map/ppermute | solution.py:664
  634.5 18.2 %collective-permute-start.70 = (f32[4,128,512]{2,1,0:T(8,128)S(1)}, f32[4,128,512]{2,1,0:T(8,128)}, u32[]{:S(2)}, u32[]{:S(2)}) collective-permute-start(f32[4,128,512]{2,1,0:T(8,128)S(1)} %maximum_select_fusion.1.own_ref), channel_id=1, source_target_pairs={{0,4},{1,5},{2,6},{3,7},{4,0},{5,1},{6,2},{7,3},{8,12},{9,13},{10,... | collective-permute-start | bytes 3145736 | tf_op jit(solution)/shard_map/ppermute | solution.py:664
  634.6 18.1 %collective-permute-start.71 = (f32[4,128,512]{2,1,0:T(8,128)}, f32[4,128,512]{2,1,0:T(8,128)}, u32[]{:S(2)}, u32[]{:S(2)}) collective-permute-start(f32[4,128,512]{2,1,0:T(8,128)} %copy-done.24), channel_id=1, source_target_pairs={{0,4},{1,5},{2,6},{3,7},{4,0},{5,1},{6,2},{7,3},{8,12},{9,13},{10,... | collective-permute-start | bytes 3145736 | tf_op jit(solution)/shard_map/ppermute | solution.py:664
  (69 other events, 1027.9 us)
Sparse Core Ops, SparseCore 0:
  192.0 98.4 reduce-scatter.1
  346.9 161.8 all-gather.4
  511.9 143.7 all-gather.2

commit v3 on v2

--- a/solution.py
+++ b/solution.py
@@ -17,10 +17,9 @@
 ROWS = TILE // LANES
 MIB = 60
 SCHEDULE = (
-    7, 2, 3, 1, 0, 4, 5, 6, 7, 4, 2, 6, 3, 5, 7, 0, 1, 3, 2, 4, 3, 6, 2, 5, 3, 0, 2, 1, 0, 5,
-    1, 4, 0, 6, 5, 4, 1, 6, 5, 5, 4, 4, 6, 6, 5, 4, 6, 5, 4, 6, 5, 4, 6, 6, 5, 4,
+    0, 1, 2, 3, 7, 4, 5, 9, 0, 1, 7, 6, 2, 3, 7, 6, 0, 1, 2, 3, 4, 5, 6, 0, 1, 6, 2, 3, 5, 4,
+    6, 0, 1, 2, 3, 6, 5, 4, 5, 4, 5, 4, 5, 4, 5, 4, 5, 4, 8, 5, 4, 8, 5, 4,
 )
-FIRST = 5
 
 
 def dot(left, right):
@@ -668,9 +667,14 @@
     return lax.all_to_all(tile, AXES, 0, 0, tiled=True)
 
 
-def sync_hops(tile, bits, devices):
-    for bit in bits:
-        tile = tile + swap(tile, bit, devices)
+def sync_hops(tile, rounds, devices):
+    for bits in rounds:
+        near = [swap(tile, bit, devices) for bit in bits]
+        if len(bits) == 2:
+            across = swap(tile, bits[0] + bits[1], devices)
+            tile = (tile + near[0]) + (near[1] + across)
+        else:
+            tile = tile + near[0]
     return tile
 
 
@@ -764,6 +768,29 @@
         ).astype(jnp.int32)
 
 
+class Later:
+    def __init__(self):
+        self.moves = []
+
+
+class Early:
+    def __init__(self, source, make):
+        self.source, self.make, self.whole = source, make, None
+        self.moves, self.results = [], []
+
+    def add_result(self, **how):
+        self.moves.append(functools.partial(self.result, how))
+
+    def gather(self):
+        self.whole = lax.all_gather(self.source.keep.reshape(-1, TILE), AXES, axis=0, tiled=False)
+
+    def result(self, how, token):
+        if self.whole is None:
+            self.gather()
+        self.results.append(self.make(after(self.whole, token), **how))
+        return self.results[-1]
+
+
 def run_streams(streams, schedule, token, to_end=True):
     for k in schedule:
         if streams[k].moves:
@@ -811,12 +838,13 @@
     blocks = c_out // TILE
     devices = dp * rep
     core_bit, x_bits, y_bits, z_bits = mesh_bits(dp, rep)
-    hop_bits = [core_bit] + y_bits + x_bits + z_bits
+    hop_rounds = [(core_bit,)] + list(zip(y_bits, x_bits))
+    hop_rounds += [tuple(z_bits[k : k + 2]) for k in range(0, len(z_bits), 2)]
     xs, ys, zs, rep_bits = x_bits, y_bits, z_bits, bits_of(1, rep)
     flat = lax.axis_index(AXES)
     core = device_bit(flat, core_bit).astype(jnp.int32).reshape(1)
     sync = functools.partial(sync_all, devices=devices)
-    sync_wide = functools.partial(sync_hops, bits=hop_bits, devices=devices)
+    sync_wide = functools.partial(sync_hops, rounds=hop_rounds, devices=devices)
 
     row_ids = lax.broadcasted_iota(jnp.int32, (1, height, 1, LANES), 1)
     col_ids = lax.broadcasted_iota(jnp.int32, (1, 1, width, LANES), 2)
@@ -980,8 +1008,10 @@
     early_made = outer_spread(
         dp, act_squeeze, left_const, gpad_window, full(padded), window_taps, 9, 9, blocks, 9 + blocks, early_made
     )
-    early_sum = lax.psum_scatter(early_made.reshape(-1, TILE), "dp", scatter_dimension=0, tiled=True)
     g_squeeze = sync(gsum)
+    early_sum = lax.psum_scatter(
+        after(early_made, g_squeeze).reshape(-1, TILE), "dp", scatter_dimension=0, tiled=True
+    )
 
     gpre_squeeze, grad_joined, gsum = call(
         squeeze_back_kernel,
@@ -1052,7 +1082,7 @@
         [shaped((4, pixels, mid), BF16), shaped((4, pixels, mid)), one_tile],
         flops=18 * pixels * mid * mid, nbytes=12 << 20,
     )(grad_spatial, pre_spatial, s_spatial, g_spatial, s_reduce, params, mask, w_spatial, pre_reduce, s_reduce, params)
-    order_spatial, order_reduce = (zs[:1] + xs + ys + zs[1:], xs + ys + zs), ys + xs + zs
+    order_spatial, order_reduce = (xs + ys + zs, ys + xs + zs), zs[:1] + xs + ys + zs[1:]
     spatial_parts = ((0, 5), (5, 4))
     late = [
         halving(
@@ -1078,10 +1108,8 @@
     spread = TILE // dp
     early = Halving(early_sum.reshape(9 + blocks, spread, TILE), rep_bits, flat, devices)
     middle = [s_squeeze_grad, s_expand_grad] + s_short_grad
-    token = run_streams(middle + late + [None, early], SCHEDULE[:FIRST], g_reduce, False)
-    g_reduce = after(g_reduce, token)
-
-    gpre_reduce, image_grad = call(
+
+    reduce_back_call = call(
         functools.partial(reduce_back_kernel, quarter),
         (steps,),
         [
@@ -1092,23 +1120,29 @@
         [plane_block(mid), pl.BlockSpec((4 * quarter, c_in), lambda k: (k, 0))],
         [shaped((4, pixels, mid), BF16), shaped((images * 4 * height * width, c_in), BF16)],
         flops=8 * pixels * c_in * mid, nbytes=10 << 20,
-    )(grad_reduce, pre_reduce, s_reduce, g_reduce, s_reduce, params, mask, w_reduce, back_short, perm_back)
-    late.append(
-        halving(
+    )
+
+    def reduce_back(summed):
+        return reduce_back_call(
+            grad_reduce, pre_reduce, s_reduce, summed, s_reduce, params, mask, w_reduce, back_short, perm_back
+        )
+
+    last = Later()
+
+    def input_back(token):
+        gpre_reduce, last.image_grad = reduce_back(after(g_reduce, token))
+        stream = halving(
             outer_halves(
                 core, planes.reshape(4 * pixels, c_in), pl.BlockSpec((4 * pixels, TILE), lambda b, *_: (0, b)),
                 gpre_reduce.reshape(4 * pixels, mid), full((4 * pixels, mid)), whole, in_blocks, 1,
             ),
             order_reduce,
         )
-    )
+        last.stream = stream
+        last.moves.extend(stream.moves)
+        return stream.keep
 
     tall, flat_cols = lambda b: (b, 0), lambda b: (0, b)
-    backs = [Return(stream, core_bit, flat, devices) for stream in late]
-    for stream, back in zip(late, backs):
-        stream.moves.extend(back.moves)
-    token = run_streams(middle + late + [early], SCHEDULE[FIRST:], after(token, late[2].keep))
-
     def starts_of(first, order, rows):
         found = []
         for k in range(devices):
@@ -1120,17 +1154,24 @@
         return tuple(found)
 
     spread_starts = starts_of(lambda k: (k // rep) * spread, rep_bits, spread)
+    early_out = Early(early, functools.partial(regroup, starts=spread_starts, total=9 + blocks))
+    early_out.add_result(place=0, blocks=blocks, shape=(mid, c_out), where=flat_cols)
+    early_out.add_result(place=blocks, blocks=9, shape=(9 * mid, mid), where=tall)
+    backs = [Return(stream, core_bit, flat, devices) for stream in late]
+    for stream, back in zip(late, backs):
+        stream.moves.extend(back.moves)
+    input_step = Later()
+    input_step.moves.append(input_back)
+    token = run_streams(middle + late + [last, early, early_out, input_step], SCHEDULE, g_reduce)
 
     def gathered(shard):
         everything = lax.all_gather(shard.reshape(-1, TILE), AXES, axis=0, tiled=False)
         return functools.partial(regroup, everything, total=shard.shape[0])
 
-    regrouped = gathered(early.keep)
-    grad_w_widen = regrouped(spread_starts, place=0, blocks=blocks, shape=(mid, c_out), where=flat_cols)
-    grad_w_window = regrouped(spread_starts, place=blocks, blocks=9, shape=(9 * mid, mid), where=tall)
+    grad_w_widen, grad_w_window = early_out.results
 
     half_starts = lambda order: starts_of(lambda k: (k // core_bit % 2) * (TILE // 2), order, TILE // 2)
-    regrouped = gathered(jnp.concatenate([s.keep for s in middle], axis=0))
+    regrouped = gathered(jnp.concatenate([s.keep for s in middle + [last.stream]], axis=0))
     grad_w_squeeze = regrouped(half_starts(order_squeeze), place=0, blocks=blocks, shape=(c_out, mid), where=tall)
     grad_w_expand = regrouped(
         half_starts(order_expand), place=blocks, blocks=blocks, shape=(mid, c_out), where=flat_cols
@@ -1148,13 +1189,15 @@
             back.places(), back.pieces(), 0, count, (9 * mid, mid), lambda b, place=place: (place + b, 0),
             into=grad_w_spatial,
         )
-    grad_w_reduce = assemble(backs[2].places(), backs[2].pieces(), 0, in_blocks, (c_in, mid), tall)
+    grad_w_reduce = regrouped(
+        half_starts(order_reduce), place=(2 + in_blocks) * blocks, blocks=in_blocks, shape=(c_in, mid), where=tall
+    )
     grad_w_window, grad_w_spatial = (g.reshape(3, 3, mid, mid) for g in (grad_w_window, grad_w_spatial))
 
     shift_total = vector(g_both, 0, 16)
     return (
         block_out.reshape(cotangent.shape),
-        image_grad.reshape(image_input.shape),
+        last.image_grad.reshape(image_input.shape),
         grad_w_reduce,
         grad_w_spatial,
         grad_w_expand,

time: 704 us -> 672 us (0.955)
  waiting for transfers between devices: 323 us -> 270 us
  starting transfers between devices: 73.5 us -> 99.5 us
  blocking collectives: 34.1 us -> 23.9 us
    ppermute x75 -> x77, waiting for transfers between devices: 306 us -> 242 us  [swap(): return lax.ppermute(values, AXES, [(i, i ^ bit) for i in range(devices)])]
    ppermute x75 -> x77, starting transfers between devices: 51.3 us -> 74.4 us  [swap(): return lax.ppermute(values, AXES, [(i, i ^ bit) for i in range(devices)])]
    all_to_all x3 -> x2, blocking collectives: 34.1 us -> 23.9 us  [sync_all(): return lax.all_to_all(tile, AXES, 0, 0, tiled=True)]
    pallas_call x3 -> x2, Pallas kernels: 16.3 us -> 12.5 us  [assemble(): pl.pallas_call(functools.partial(assemble_kernel, chunks), grid_spec=pltp...]
    pallas_call x6 -> x7, Pallas kernels: 34.5 us -> 37.4 us  [regroup(): pl.pallas_call(functools.partial(regroup_kernel, starts), grid=(blocks,),...]
    all_to_all x5 -> x6, starting transfers between devices: 21.9 us -> 24.6 us  [sync_all(): return lax.all_to_all(tile, AXES, 0, 0, tiled=True)]
    all_to_all x5 -> x6, waiting for transfers between devices: 16.7 us -> 17.1 us  [sync_all(): return lax.all_to_all(tile, AXES, 0, 0, tiled=True)]
  transfers between devices with their start and end apart: 83 -> 86, of which waited for: 51 -> 57; matrix products, arithmetic and copies ran while one was open for 7% -> 9% of each run, Pallas kernels for 16% -> 17%
where the time goes in v3:
time: 672 us; the launch traced here: 668 us
  waiting for transfers between devices  270 us (40%)
  Pallas kernels  191 us (28%)
  starting transfers between devices  99.5 us (15%)
  other arithmetic  58.5 us (9%)
  blocking collectives  23.9 us (4%)
  between operations  15 us (2%)
  local copies, waits for them, and re-layouts  9.68 us (1%)
    ppermute x77, waiting for transfers between devices, swap(): return lax.ppermute(values, AXES, [(i, i ^ bit) for i in range(devices)])  242 us
    ppermute x77, starting transfers between devices, swap(): return lax.ppermute(values, AXES, [(i, i ^ bit) for i in range(devices)])  74.4 us
    add x57, other arithmetic, half_sum(): first + lax.dynamic_slice_in_dim(received, which * rows, rows, axis=1)  44.3 us
    pallas_call x7, Pallas kernels, regroup(): pl.pallas_call(functools.partial(regroup_kernel, starts), grid=(blocks,),...  37.4 us
    pallas_call x7, Pallas kernels, outer_halves(): pl.pallas_call(functools.partial(halves_kernel, pick, per_left), grid_spe...  33.8 us
    all_to_all x6, starting transfers between devices, sync_all(): return lax.all_to_all(tile, AXES, 0, 0, tiled=True)  24.6 us
    all_to_all x2, blocking collectives, sync_all(): return lax.all_to_all(tile, AXES, 0, 0, tiled=True)  23.9 us
    all_to_all x6, waiting for transfers between devices, sync_all(): return lax.all_to_all(tile, AXES, 0, 0, tiled=True)  17.1 us
  transfers between devices with their start and end apart: 86, of which 57 were waited for; matrix products, arithmetic and copies ran while one was open for 9% of the time, Pallas kernels for 17%

profile of v3, /device:TPU:0, one launch (start us, length us, event | category | flops | bytes accessed | tf_op | source)
XLA Modules:
  0.0 668.1 jit_solution(9727707648005400751)
XLA Ops:
  9.5 6.1 shard_map.434
  15.6 7.3 %all-to-all-start = ((f32[32,16,128]{2,1,0:T(8,128)}), f32[32,16,128]{2,1,0:T(8,128)S(1)}, u32[]{:S(2)}, u32[]{:S(2)}) async-start(f32[32,16,128]{2,1,0:T(8,128)} %get-tuple-element.243), calls=%async_computation | async-start | bytes 524288 | tf_op jit(solution)/shard_map/all_to_all | solution.py:667
  23.2 9.9 %all-to-all-done.stat_ref.count_ref.in_stat_ref = f32[32,16,128]{2,1,0:T(8,128)S(1)} async-done(((f32[32,16,128]{2,1,0:T(8,128)}), f32[32,16,128]{2,1,0:T(8,128)S(1)}, u32[]{:S(2)}, u32[]{:S(2)}) %all-to-all-start) | async-done | bytes 262176 | tf_op jit(solution)/shard_map/all_to_all | solution.py:667
  33.8 7.3 %shard_map.435 = (bf16[4,256,512]{2,1,0:T(8,128)(2,1)}, f32[256,512]{1,0:T(8,128)}, f32[32,8,128]{2,1,0:T(8,128)}) custom-call(f32[4,256,512]{2,1,0:T(8,128)} %get-tuple-element.242.pre_ref.in_ref, f32[32,16,128]{2,1,0:T(8,128)} %copy-done, f32[32,16,128]{2,1,0:T(8,128)} %copy-done, f32[128,128]{1,0:T(8,128)} %copy-done.1, f32[256,128]{1,0:T(8,128)} %bitcast.74, ...), custom_call_target="tpu_custom_call" | custom-call | flops 1207959552 | bytes 8388608 | tf_op jit(solution)/shard_map/pallas_call | solution.py:921
  43.8 5.1 shard_map.437
  52.9 4.8 shard_map.436
  74.8 6.1 shard_map.438
  80.9 12.3 %all_to_all.40.stat_ref.in_stat_ref = f32[32,8,128]{2,1,0:T(8,128)} all-to-all(f32[32,8,128]{2,1,0:T(8,128)} %get-tuple-element.252), channel_id=1, replica_groups=mesh['dp'=8,'rep'=4] {'dp','rep'}, dimensions={0} | all-to-all | bytes 262144 | tf_op jit(solution)/shard_map/all_to_all | solution.py:667
  93.2 5.7 shard_map.439
  98.9 11.7 %all_to_all.41.stat_ref.in_stat_ref = f32[32,8,128]{2,1,0:T(8,128)} all-to-all(f32[32,8,128]{2,1,0:T(8,128)} %get-tuple-element.254), channel_id=1, replica_groups=mesh['dp'=8,'rep'=4] {'dp','rep'}, dimensions={0} | all-to-all | bytes 262144 | tf_op jit(solution)/shard_map/all_to_all | solution.py:667
  110.6 4.8 shard_map.440
  131.4 5.4 shard_map.441
  150.6 3.8 collective-permute-done.20
  155.1 6.2 shard_map.442
  163.9 4.7 shard_map.443.refs_0_
  168.6 3.7 all-to-all-done.4.gsum_ref
  172.9 6.6 shard_map.444
  182.3 7.9 %shard_map.455 = f32[8,832,512]{2,1,0:T(8,128)} custom-call(bf16[256,512]{1,0:T(8,128)(2,1)} %get-tuple-element.299.left_ref, bf16[3,2,160,512]{3,2,1,0:T(8,128)(2,1)} %get-tuple-element.300.right_ref, f32[8,832,512]{2,1,0:T(8,128)} %shard_map.443.refs_0_), custom_call_target="tpu_custom_call", output_to_operand_aliasing={{}: (2, {})} | custom-call | flops 1207959552 | bytes 9437184 | tf_op jit(solution)/shard_map/pallas_call | solution.py:575
  191.1 7.4 %shard_map.445 = (bf16[256,512]{1,0:T(8,128)(2,1)}, f32[256,2048]{1,0:T(8,128)}, f32[64,128]{1,0:T(8,128)}) custom-call(f32[256,512]{1,0:T(8,128)} %get-tuple-element.266.grad_ref, f32[256,512]{1,0:T(8,128)} %get-tuple-element.251.pre_ref.in_ref, f32[32,8,128]{2,1,0:T(8,128)} %all_to_all.40.stat_ref.in_stat_ref, f32[32,8,128]{2,1,0:T(8,128)} %copy-done.22, ...), custom_call_target="tpu_custom_call" | custom-call | flops 536870912 | bytes 11534336 | tf_op jit(solution)/shard_map/pallas_call | solution.py:1016
  212.9 4.6 shard_map.446
  218.9 7.4 %shard_map.447 = (bf16[256,2048]{1,0:T(8,128)(2,1)}, bf16[256,2048]{1,0:T(8,128)(2,1)}, f32[256,512]{1,0:T(8,128)}, f32[32,8,128]{2,1,0:T(8,128)}) custom-call(f32[256,2048]{1,0:T(8,128)} %get-tuple-element.268.gj_ref, f32[256,2048]{1,0:T(8,128)} %get-tuple-element.246.pe_ref, f32[256,2048]{1,0:T(8,128)} %get-tuple-element.248.ps_ref, ...), custom_call_target="tpu_custom_call" | custom-call | flops 536870912 | bytes 11534336 | tf_op jit(solution)/shard_map/pallas_call | solution.py:1041
  226.3 3.9 all-to-all-start.6
  230.2 4.6 shard_map.450
  234.8 4.6 shard_map.449
  239.4 4.5 shard_map.448
  244.9 9.6 %shard_map.451 = (bf16[4,256,512]{2,1,0:T(8,128)(2,1)}, f32[4,256,512]{2,1,0:T(8,128)}, f32[32,8,128]{2,1,0:T(8,128)}) custom-call(f32[256,512]{1,0:T(8,128)} %get-tuple-element.273.grad_ref, f32[256,512]{1,0:T(8,128)} %get-tuple-element.244.pre_ref.in_ref, f32[32,8,128]{2,1,0:T(8,128)} %copy-done.8, f32[32,8,128]{2,1,0:T(8,128)} %copy-done.24, ...), custom_call_target="tpu_custom_call" | custom-call | flops 1207959552 | bytes 12582912 | tf_op jit(solution)/shard_map/pallas_call | solution.py:1074
  254.5 5.5 all-to-all-start.7
  260.1 5.5 shard_map.454.short_ref
  265.6 5.2 shard_map.453
  270.9 5.8 shard_map.452
  291.0 6.6 reduce-scatter.2.cloned.1.call-done
  306.9 6.6 shard_map.456
  313.5 4.4 shard_map.457
  326.9 7.2 %collective-permute-done.39 = f32[4,128,512]{2,1,0:T(8,128)} collective-permute-done((f32[4,128,512]{2,1,0:T(8,128)}, f32[4,128,512]{2,1,0:T(8,128)}, u32[]{:S(2)}, u32[]{:S(2)}) %collective-permute-start.39) | collective-permute-done | bytes 1048608 | tf_op jit(solution)/shard_map/ppermute | solution.py:663
  339.0 4.9 collective-permute-done.37
  349.7 13.2 %collective-permute-done.33 = f32[4,64,512]{2,1,0:T(8,128)} collective-permute-done((f32[4,64,512]{2,1,0:T(8,128)}, f32[4,64,512]{2,1,0:T(8,128)}, u32[]{:S(2)}, u32[]{:S(2)}) %collective-permute-start.33) | collective-permute-done | bytes 524320 | tf_op jit(solution)/shard_map/ppermute | solution.py:663
  369.0 6.9 %collective-permute-done.45 = f32[4,64,512]{2,1,0:T(8,128)S(1)} collective-permute-done((f32[4,64,512]{2,1,0:T(8,128)S(1)}, f32[4,64,512]{2,1,0:T(8,128)S(1)}, u32[]{:S(2)}, u32[]{:S(2)}) %collective-permute-start.45) | collective-permute-done | bytes 524320 | tf_op jit(solution)/shard_map/ppermute | solution.py:663
  376.0 4.9 collective-permute-done.44
  391.7 5.7 collective-permute-done.41
  399.9 7.9 %collective-permute-done.40 = f32[4,32,512]{2,1,0:T(8,128)S(1)} collective-permute-done((f32[4,32,512]{2,1,0:T(8,128)S(1)}, f32[4,32,512]{2,1,0:T(8,128)S(1)}, u32[]{:S(2)}, u32[]{:S(2)}) %collective-permute-start.40) | collective-permute-done | bytes 262176 | tf_op jit(solution)/shard_map/ppermute | solution.py:663
  413.4 15.5 %collective-permute-done.48 = f32[2,64,512]{2,1,0:T(8,128)S(1)} collective-permute-done((f32[2,64,512]{2,1,0:T(8,128)S(1)}, f32[2,64,512]{2,1,0:T(8,128)S(1)}, u32[]{:S(2)}, u32[]{:S(2)}) %collective-permute-start.48) | collective-permute-done | bytes 262176 | tf_op jit(solution)/shard_map/ppermute | solution.py:663
  443.7 10.1 %collective-permute-done.47 = f32[4,16,512]{2,1,0:T(8,128)S(1)} collective-permute-done((f32[4,16,512]{2,1,0:T(8,128)S(1)}, f32[4,16,512]{2,1,0:T(8,128)S(1)}, u32[]{:S(2)}, u32[]{:S(2)}) %collective-permute-start.47) | collective-permute-done | bytes 131104 | tf_op jit(solution)/shard_map/ppermute | solution.py:663
  454.5 11.2 %collective-permute-done.55 = f32[4,16,512]{2,1,0:T(8,128)S(1)} collective-permute-done((f32[4,16,512]{2,1,0:T(8,128)S(1)}, f32[4,16,512]{2,1,0:T(8,128)S(1)}, u32[]{:S(2)}, u32[]{:S(2)}) %collective-permute-start.55) | collective-permute-done | bytes 131104 | tf_op jit(solution)/shard_map/ppermute | solution.py:663
  466.4 5.7 collective-permute-done.56
  472.8 4.6 collective-permute-done.57
  481.4 8.2 %collective-permute-done.59 = f32[4,64,512]{2,1,0:T(8,128)S(1)} collective-permute-done((f32[4,64,512]{2,1,0:T(8,128)}, f32[4,64,512]{2,1,0:T(8,128)S(1)}, u32[]{:S(2)}, u32[]{:S(2)}) %collective-permute-start.59) | collective-permute-done | bytes 524320 | tf_op jit(solution)/shard_map/ppermute | solution.py:663
  492.0 4.6 collective-permute-done.60
  497.1 10.9 %collective-permute-done.63 = f32[5,32,512]{2,1,0:T(8,128)S(1)} collective-permute-done((f32[5,32,512]{2,1,0:T(8,128)S(1)}, f32[5,32,512]{2,1,0:T(8,128)S(1)}, u32[]{:S(2)}, u32[]{:S(2)}) %collective-permute-start.63) | collective-permute-done | bytes 327712 | tf_op jit(solution)/shard_map/ppermute | solution.py:663
  508.0 4.3 collective-permute-start.64
  514.0 8.5 %collective-permute-done.64 = f32[5,16,512]{2,1,0:T(8,128)S(1)} collective-permute-done((f32[5,16,512]{2,1,0:T(8,128)S(1)}, f32[5,16,512]{2,1,0:T(8,128)S(1)}, u32[]{:S(2)}, u32[]{:S(2)}) %collective-permute-start.64) | collective-permute-done | bytes 163872 | tf_op jit(solution)/shard_map/ppermute | solution.py:663
  528.9 9.5 %collective-permute-done.67 = f32[5,16,512]{2,1,0:T(8,128)S(1)} collective-permute-done((f32[5,16,512]{2,1,0:T(8,128)S(1)}, f32[5,16,512]{2,1,0:T(8,128)S(1)}, u32[]{:S(2)}, u32[]{:S(2)}) %collective-permute-start.67) | collective-permute-done | bytes 163872 | tf_op jit(solution)/shard_map/ppermute | solution.py:663
  538.6 12.8 %collective-permute-done.66 = f32[4,32,512]{2,1,0:T(8,128)S(1)} collective-permute-done((f32[4,32,512]{2,1,0:T(8,128)S(1)}, f32[4,32,512]{2,1,0:T(8,128)S(1)}, u32[]{:S(2)}, u32[]{:S(2)}) %collective-permute-start.66) | collective-permute-done | bytes 262176 | tf_op jit(solution)/shard_map/ppermute | solution.py:663
  553.0 9.2 %collective-permute-done.69 = f32[5,32,512]{2,1,0:T(8,128)S(1)} collective-permute-done((f32[5,32,512]{2,1,0:T(8,128)S(1)}, f32[5,32,512]{2,1,0:T(8,128)S(1)}, u32[]{:S(2)}, u32[]{:S(2)}) %collective-permute-start.69) | collective-permute-done | bytes 327712 | tf_op jit(solution)/shard_map/ppermute | solution.py:663
  564.4 5.0 shard_map.459
  569.5 13.4 %collective-permute-done.71 = f32[5,64,512]{2,1,0:T(8,128)} collective-permute-done((f32[5,64,512]{2,1,0:T(8,128)S(1)}, f32[5,64,512]{2,1,0:T(8,128)}, u32[]{:S(2)}, u32[]{:S(2)}) %collective-permute-start.71) | collective-permute-done | bytes 655392 | tf_op jit(solution)/shard_map/ppermute | solution.py:663
  587.8 10.8 %shard_map.460 = f32[4608,512]{1,0:T(8,128)} custom-call(f32[32,208,512]{2,1,0:T(8,128)} %all-gather.5.cloned.1.call-done.in_ref), custom_call_target="tpu_custom_call" | custom-call | bytes 18874368 | tf_op jit(solution)/shard_map/pallas_call | solution.py:631
  598.6 19.4 %collective-permute-done.70.near_ref = f32[4,128,512]{2,1,0:T(8,128)} collective-permute-done((f32[4,128,512]{2,1,0:T(8,128)S(1)}, f32[4,128,512]{2,1,0:T(8,128)}, u32[]{:S(2)}, u32[]{:S(2)}) %collective-permute-start.70) | collective-permute-done | bytes 1048608 | tf_op jit(solution)/shard_map/ppermute | solution.py:663
  622.5 7.1 %shard_map.461.refs_0_ = f32[4608,512]{1,0:T(8,128)} custom-call(s32[4]{0:T(128)} %pad_add_fusion.1.place_ref, f32[5,128,512]{2,1,0:T(8,128)} %copy-done.2, f32[5,128,512]{2,1,0:T(8,128)} %collective-permute-done.74.near_ref, f32[5,128,512]{2,1,0:T(8,128)} %collective-permute-done.75.far_ref, f32[5,128,512]{2,1,0:T(8,128)} %collective-permute-done.76.both_ref), custom_call_target="tpu_custom_call" | custom-call | bytes 10485760 | tf_op jit(solution)/shard_map/pallas_call | solution.py:600
  629.6 5.4 shard_map.462
  635.0 4.4 all-gather.3.cloned.1.call-done.in_ref
  639.4 4.7 shard_map.464.refs_0_
  644.1 4.7 shard_map.463
  648.9 4.7 shard_map.466
  656.2 4.7 shard_map.465
  (358 shorter events, 196.9 us)
Async XLA Ops:
  15.6 17.5 %all-to-all-start = ((f32[32,16,128]{2,1,0:T(8,128)}), f32[32,16,128]{2,1,0:T(8,128)S(1)}, u32[]{:S(2)}, u32[]{:S(2)}) async-start(f32[32,16,128]{2,1,0:T(8,128)} %get-tuple-element.243), calls=%async_computation | async-start | bytes 524288 | tf_op jit(solution)/shard_map/all_to_all | solution.py:667
  41.1 11.1 %all-to-all-start.1 = ((f32[32,8,128]{2,1,0:T(8,128)}), f32[32,8,128]{2,1,0:T(8,128)S(1)}, u32[]{:S(2)}, u32[]{:S(2)}) async-start(f32[32,8,128]{2,1,0:T(8,128)} %get-tuple-element.245), calls=%async_computation.1 | async-start | bytes 262144 | tf_op jit(solution)/shard_map/all_to_all | solution.py:667
  68.4 5.7 collective-permute-start.6
  125.2 5.5 collective-permute-start.13
  145.7 5.0 collective-permute-start.19
  148.9 5.5 collective-permute-start.20
  161.3 11.0 %all-to-all-start.4 = ((f32[32,8,128]{2,1,0:T(8,128)}), f32[32,8,128]{2,1,0:T(8,128)S(1)}, u32[]{:S(2)}, u32[]{:S(2)}) async-start(f32[32,8,128]{2,1,0:T(8,128)} %get-tuple-element.262), calls=%async_computation.4 | async-start | bytes 262144 | tf_op jit(solution)/shard_map/all_to_all | solution.py:667
  179.5 11.0 %all-to-all-start.5 = ((f32[32,8,128]{2,1,0:T(8,128)}), f32[32,8,128]{2,1,0:T(8,128)S(1)}, u32[]{:S(2)}, u32[]{:S(2)}) async-start(f32[32,8,128]{2,1,0:T(8,128)} %get-tuple-element.267), calls=%async_computation.5 | async-start | bytes 262144 | tf_op jit(solution)/shard_map/all_to_all | solution.py:667
  182.1 115.5 %reduce-scatter.2.cloned.1.call-start = ((), (), s32[]{:S(2)}) async-start(), calls=%async_computation.9 | async-start | bytes 15335424 | tf_op jit(solution)/shard_map/reduce_scatter | solution.py:1012
  208.5 9.1 %collective-permute-start.25 = (f32[64,128]{1,0:T(8,128)S(1)}, f32[64,128]{1,0:T(8,128)S(1)}, u32[]{:S(2)}, u32[]{:S(2)}) collective-permute-start(f32[64,128]{1,0:T(8,128)S(1)} %add_add_fusion.1), channel_id=1, source_target_pairs={{0,1},{1,0},{2,3},{3,2},{4,5},{5,4},{6,7},{7,6},{8,9},{9,8},{10,11... | collective-permute-start | bytes 98312 | tf_op jit(solution)/shard_map/ppermute | solution.py:663
  210.1 7.5 %collective-permute-start.26 = (f32[64,128]{1,0:T(8,128)S(1)}, f32[64,128]{1,0:T(8,128)S(1)}, u32[]{:S(2)}, u32[]{:S(2)}) collective-permute-start(f32[64,128]{1,0:T(8,128)S(1)} %add_add_fusion.1), channel_id=1, source_target_pairs={{0,2},{1,3},{2,0},{3,1},{4,6},{5,7},{6,4},{7,5},{8,10},{9,11},{10,... | collective-permute-start | bytes 98312 | tf_op jit(solution)/shard_map/ppermute | solution.py:663
  212.6 5.7 collective-permute-start.27
  218.9 25.1 %collective-permute-start.28 = (f32[4,256,512]{2,1,0:T(8,128)}, f32[4,256,512]{2,1,0:T(8,128)S(1)}, u32[]{:S(2)}, u32[]{:S(2)}) collective-permute-start(f32[4,256,512]{2,1,0:T(8,128)} %get-tuple-element.282), channel_id=1, source_target_pairs={{0,4},{1,5},{2,6},{3,7},{4,0},{5,1},{6,2},{7,3},{8,12},{9,13},{10,... | collective-permute-start | bytes 6291464 | tf_op jit(solution)/shard_map/ppermute | solution.py:663
  226.3 17.6 %all-to-all-start.6 = ((f32[32,8,128]{2,1,0:T(8,128)}), f32[32,8,128]{2,1,0:T(8,128)S(1)}, u32[]{:S(2)}, u32[]{:S(2)}) async-start(f32[32,8,128]{2,1,0:T(8,128)} %get-tuple-element.274), calls=%async_computation.6 | async-start | bytes 262144 | tf_op jit(solution)/shard_map/all_to_all | solution.py:667
  244.0 32.7 %collective-permute-start.31 = (f32[4,256,512]{2,1,0:T(8,128)}, f32[4,256,512]{2,1,0:T(8,128)}, u32[]{:S(2)}, u32[]{:S(2)}) collective-permute-start(f32[4,256,512]{2,1,0:T(8,128)} %get-tuple-element.295), channel_id=1, source_target_pairs={{0,4},{1,5},{2,6},{3,7},{4,0},{5,1},{6,2},{7,3},{8,12},{9,13},{10,... | collective-permute-start | bytes 6291464 | tf_op jit(solution)/shard_map/ppermute | solution.py:663
  244.3 32.4 %collective-permute-start.30 = (f32[4,256,512]{2,1,0:T(8,128)}, f32[4,256,512]{2,1,0:T(8,128)}, u32[]{:S(2)}, u32[]{:S(2)}) collective-permute-start(f32[4,256,512]{2,1,0:T(8,128)} %get-tuple-element.293), channel_id=1, source_target_pairs={{0,4},{1,5},{2,6},{3,7},{4,0},{5,1},{6,2},{7,3},{8,12},{9,13},{10,... | collective-permute-start | bytes 6291464 | tf_op jit(solution)/shard_map/ppermute | solution.py:663
  244.5 32.2 %collective-permute-start.29 = (f32[4,256,512]{2,1,0:T(8,128)}, f32[4,256,512]{2,1,0:T(8,128)}, u32[]{:S(2)}, u32[]{:S(2)}) collective-permute-start(f32[4,256,512]{2,1,0:T(8,128)} %get-tuple-element.291), channel_id=1, source_target_pairs={{0,4},{1,5},{2,6},{3,7},{4,0},{5,1},{6,2},{7,3},{8,12},{9,13},{10,... | collective-permute-start | bytes 6291464 | tf_op jit(solution)/shard_map/ppermute | solution.py:663
  254.5 22.2 %all-to-all-start.7 = ((f32[32,8,128]{2,1,0:T(8,128)}), f32[32,8,128]{2,1,0:T(8,128)S(1)}, u32[]{:S(2)}, u32[]{:S(2)}) async-start(f32[32,8,128]{2,1,0:T(8,128)} %get-tuple-element.285), calls=%async_computation.7 | async-start | bytes 262144 | tf_op jit(solution)/shard_map/all_to_all | solution.py:667
  260.0 304.3 %all-gather.5.cloned.1.call-start = ((), (), s32[]{:S(2)}) async-start(), calls=%async_computation.11 | async-start | bytes 14057472 | tf_op jit(solution)/shard_map/all_gather | solution.py:785
  279.4 38.5 %collective-permute-start.32 = (f32[4,128,512]{2,1,0:T(8,128)}, f32[4,128,512]{2,1,0:T(8,128)}, u32[]{:S(2)}, u32[]{:S(2)}) collective-permute-start(f32[4,128,512]{2,1,0:T(8,128)} %dynamic-slice_add_fusion.11), channel_id=1, source_target_pairs={{0,8},{1,9},{2,10},{3,11},{4,12},{5,13},{6,14},{7,15},{8,0},{9,1},... | collective-permute-start | bytes 3145736 | tf_op jit(solution)/shard_map/ppermute | solution.py:663
  283.5 36.5 %collective-permute-start.35 = (f32[4,128,512]{2,1,0:T(8,128)}, f32[4,128,512]{2,1,0:T(8,128)}, u32[]{:S(2)}, u32[]{:S(2)}) collective-permute-start(f32[4,128,512]{2,1,0:T(8,128)} %dynamic-slice_add_fusion.10), channel_id=1, source_target_pairs={{0,16},{1,17},{2,18},{3,19},{4,20},{5,21},{6,22},{7,23},{8,24},{9,... | collective-permute-start | bytes 3145736 | tf_op jit(solution)/shard_map/ppermute | solution.py:663
  287.3 46.8 %collective-permute-start.39 = (f32[4,128,512]{2,1,0:T(8,128)}, f32[4,128,512]{2,1,0:T(8,128)}, u32[]{:S(2)}, u32[]{:S(2)}) collective-permute-start(f32[4,128,512]{2,1,0:T(8,128)} %dynamic-slice_add_fusion.9), channel_id=1, source_target_pairs={{0,8},{1,9},{2,10},{3,11},{4,12},{5,13},{6,14},{7,15},{8,0},{9,1},... | collective-permute-start | bytes 3145736 | tf_op jit(solution)/shard_map/ppermute | solution.py:663
  290.5 45.6 %collective-permute-start.38 = (f32[4,128,512]{2,1,0:T(8,128)}, f32[4,128,512]{2,1,0:T(8,128)}, u32[]{:S(2)}, u32[]{:S(2)}) collective-permute-start(f32[4,128,512]{2,1,0:T(8,128)} %dynamic-slice_add_fusion.8), channel_id=1, source_target_pairs={{0,16},{1,17},{2,18},{3,19},{4,20},{5,21},{6,22},{7,23},{8,24},{9,... | collective-permute-start | bytes 3145736 | tf_op jit(solution)/shard_map/ppermute | solution.py:663
  300.4 21.5 %collective-permute-start.34 = (f32[13,32,512]{2,1,0:T(8,128)}, f32[13,32,512]{2,1,0:T(8,128)}, u32[]{:S(2)}, u32[]{:S(2)}) collective-permute-start(f32[13,32,512]{2,1,0:T(8,128)} %get-tuple-element.472), channel_id=1, source_target_pairs={{0,1},{1,0},{2,3},{3,2},{4,5},{5,4},{6,7},{7,6},{8,9},{9,8},{10,11... | collective-permute-start | bytes 2555912 | tf_op jit(solution)/shard_map/ppermute | solution.py:663
  323.0 20.9 %collective-permute-start.37 = (f32[13,16,512]{2,1,0:T(8,128)S(1)}, f32[13,16,512]{2,1,0:T(8,128)S(1)}, u32[]{:S(2)}, u32[]{:S(2)}) collective-permute-start(f32[13,16,512]{2,1,0:T(8,128)S(1)} %dynamic-slice_add_fusion.27), channel_id=1, source_target_pairs={{0,2},{1,3},{2,0},{3,1},{4,6},{5,7},{6,4},{7,5},{8,10},{9,11},{10,... | collective-permute-start | bytes 1277960 | tf_op jit(solution)/shard_map/ppermute | solution.py:663
  344.7 294.6 %all-gather.3.cloned.1.call-start = ((), (), s32[]{:S(2)}) async-start(), calls=%async_computation.10 | async-start | bytes 19464192 | tf_op jit(solution)/shard_map/all_gather | solution.py:1168
  345.0 38.4 %collective-permute-start.43 = (f32[5,256,512]{2,1,0:T(8,128)}, f32[5,256,512]{2,1,0:T(8,128)}, u32[]{:S(2)}, u32[]{:S(2)}) collective-permute-start(f32[5,256,512]{2,1,0:T(8,128)} %get-tuple-element.311), channel_id=1, source_target_pairs={{0,4},{1,5},{2,6},{3,7},{4,0},{5,1},{6,2},{7,3},{8,12},{9,13},{10,... | collective-permute-start | bytes 7864328 | tf_op jit(solution)/shard_map/ppermute | solution.py:663
  345.1 20.4 %collective-permute-start.36 = (f32[2,256,512]{2,1,0:T(8,128)}, f32[2,256,512]{2,1,0:T(8,128)}, u32[]{:S(2)}, u32[]{:S(2)}) collective-permute-start(f32[2,256,512]{2,1,0:T(8,128)} %get-tuple-element.330), channel_id=1, source_target_pairs={{0,4},{1,5},{2,6},{3,7},{4,0},{5,1},{6,2},{7,3},{8,12},{9,13},{10,... | collective-permute-start | bytes 3145736 | tf_op jit(solution)/shard_map/ppermute | solution.py:663
  345.6 17.3 %collective-permute-start.33 = (f32[4,64,512]{2,1,0:T(8,128)}, f32[4,64,512]{2,1,0:T(8,128)}, u32[]{:S(2)}, u32[]{:S(2)}) collective-permute-start(f32[4,64,512]{2,1,0:T(8,128)} %dynamic-slice_add_fusion.25), channel_id=1, source_target_pairs={{0,16},{1,17},{2,18},{3,19},{4,20},{5,21},{6,22},{7,23},{8,24},{9,... | collective-permute-start | bytes 1572872 | tf_op jit(solution)/shard_map/ppermute | solution.py:663
  347.1 40.0 %collective-permute-start.42 = (f32[4,256,512]{2,1,0:T(8,128)}, f32[4,256,512]{2,1,0:T(8,128)}, u32[]{:S(2)}, u32[]{:S(2)}) collective-permute-start(f32[4,256,512]{2,1,0:T(8,128)} %get-tuple-element.312), channel_id=1, source_target_pairs={{0,4},{1,5},{2,6},{3,7},{4,0},{5,1},{6,2},{7,3},{8,12},{9,13},{10,... | collective-permute-start | bytes 6291464 | tf_op jit(solution)/shard_map/ppermute | solution.py:663
  347.1 21.8 %collective-permute-start.46 = (f32[4,64,512]{2,1,0:T(8,128)}, f32[4,64,512]{2,1,0:T(8,128)S(1)}, u32[]{:S(2)}, u32[]{:S(2)}) collective-permute-start(f32[4,64,512]{2,1,0:T(8,128)} %dynamic-slice_add_fusion.23), channel_id=1, source_target_pairs={{0,8},{1,9},{2,10},{3,11},{4,12},{5,13},{6,14},{7,15},{8,0},{9,1},... | collective-permute-start | bytes 1572872 | tf_op jit(solution)/shard_map/ppermute | solution.py:663
  362.9 13.1 %collective-permute-start.45 = (f32[4,64,512]{2,1,0:T(8,128)S(1)}, f32[4,64,512]{2,1,0:T(8,128)S(1)}, u32[]{:S(2)}, u32[]{:S(2)}) collective-permute-start(f32[4,64,512]{2,1,0:T(8,128)S(1)} %copy-done.30), channel_id=1, source_target_pairs={{0,16},{1,17},{2,18},{3,19},{4,20},{5,21},{6,22},{7,23},{8,24},{9,... | collective-permute-start | bytes 1572872 | tf_op jit(solution)/shard_map/ppermute | solution.py:663
  365.5 15.4 %collective-permute-start.44 = (f32[4,64,512]{2,1,0:T(8,128)S(1)}, f32[4,64,512]{2,1,0:T(8,128)S(1)}, u32[]{:S(2)}, u32[]{:S(2)}) collective-permute-start(f32[4,64,512]{2,1,0:T(8,128)S(1)} %copy-done.29), channel_id=1, source_target_pairs={{0,8},{1,9},{2,10},{3,11},{4,12},{5,13},{6,14},{7,15},{8,0},{9,1},... | collective-permute-start | bytes 1572872 | tf_op jit(solution)/shard_map/ppermute | solution.py:663
  368.9 28.5 %collective-permute-start.41 = (f32[2,128,512]{2,1,0:T(8,128)S(1)}, f32[2,128,512]{2,1,0:T(8,128)S(1)}, u32[]{:S(2)}, u32[]{:S(2)}) collective-permute-start(f32[2,128,512]{2,1,0:T(8,128)S(1)} %dynamic-slice_add_fusion.20), channel_id=1, source_target_pairs={{0,1},{1,0},{2,3},{3,2},{4,5},{5,4},{6,7},{7,6},{8,9},{9,8},{10,11... | collective-permute-start | bytes 1572872 | tf_op jit(solution)/shard_map/ppermute | solution.py:663
  375.9 31.8 %collective-permute-start.40 = (f32[4,32,512]{2,1,0:T(8,128)S(1)}, f32[4,32,512]{2,1,0:T(8,128)S(1)}, u32[]{:S(2)}, u32[]{:S(2)}) collective-permute-start(f32[4,32,512]{2,1,0:T(8,128)S(1)} %dynamic-slice_add_fusion.41), channel_id=1, source_target_pairs={{0,1},{1,0},{2,3},{3,2},{4,5},{5,4},{6,7},{7,6},{8,9},{9,8},{10,11... | collective-permute-start | bytes 786440 | tf_op jit(solution)/shard_map/ppermute | solution.py:663
  380.9 32.5 %collective-permute-start.49 = (f32[4,32,512]{2,1,0:T(8,128)S(1)}, f32[4,32,512]{2,1,0:T(8,128)S(1)}, u32[]{:S(2)}, u32[]{:S(2)}) collective-permute-start(f32[4,32,512]{2,1,0:T(8,128)S(1)} %dynamic-slice_add_fusion.39), channel_id=1, source_target_pairs={{0,1},{1,0},{2,3},{3,2},{4,5},{5,4},{6,7},{7,6},{8,9},{9,8},{10,11... | collective-permute-start | bytes 786440 | tf_op jit(solution)/shard_map/ppermute | solution.py:663
  383.4 45.5 %collective-permute-start.54 = (f32[4,32,512]{2,1,0:T(8,128)S(1)}, f32[4,32,512]{2,1,0:T(8,128)S(1)}, u32[]{:S(2)}, u32[]{:S(2)}) collective-permute-start(f32[4,32,512]{2,1,0:T(8,128)S(1)} %dynamic-slice_add_fusion.38), channel_id=1, source_target_pairs={{0,1},{1,0},{2,3},{3,2},{4,5},{5,4},{6,7},{7,6},{8,9},{9,8},{10,11... | collective-permute-start | bytes 786440 | tf_op jit(solution)/shard_map/ppermute | solution.py:663
  388.6 46.8 %collective-permute-start.52 = (f32[4,128,512]{2,1,0:T(8,128)S(1)}, f32[4,128,512]{2,1,0:T(8,128)S(1)}, u32[]{:S(2)}, u32[]{:S(2)}) collective-permute-start(f32[4,128,512]{2,1,0:T(8,128)S(1)} %dynamic-slice_add_fusion.3), channel_id=1, source_target_pairs={{0,16},{1,17},{2,18},{3,19},{4,20},{5,21},{6,22},{7,23},{8,24},{9,... | collective-permute-start | bytes 3145736 | tf_op jit(solution)/shard_map/ppermute | solution.py:663
  397.4 39.5 %collective-permute-start.51 = (f32[5,128,512]{2,1,0:T(8,128)S(1)}, f32[5,128,512]{2,1,0:T(8,128)S(1)}, u32[]{:S(2)}, u32[]{:S(2)}) collective-permute-start(f32[5,128,512]{2,1,0:T(8,128)S(1)} %dynamic-slice_add_fusion.1), channel_id=1, source_target_pairs={{0,8},{1,9},{2,10},{3,11},{4,12},{5,13},{6,14},{7,15},{8,0},{9,1},... | collective-permute-start | bytes 3932168 | tf_op jit(solution)/shard_map/ppermute | solution.py:663
  407.8 21.2 %collective-permute-start.48 = (f32[2,64,512]{2,1,0:T(8,128)S(1)}, f32[2,64,512]{2,1,0:T(8,128)S(1)}, u32[]{:S(2)}, u32[]{:S(2)}) collective-permute-start(f32[2,64,512]{2,1,0:T(8,128)S(1)} %dynamic-slice_add_fusion.36), channel_id=1, source_target_pairs={{0,8},{1,9},{2,10},{3,11},{4,12},{5,13},{6,14},{7,15},{8,0},{9,1},... | collective-permute-start | bytes 786440 | tf_op jit(solution)/shard_map/ppermute | solution.py:663
  413.4 21.9 %collective-permute-start.53 = (f32[4,32,512]{2,1,0:T(8,128)S(1)}, f32[4,32,512]{2,1,0:T(8,128)S(1)}, u32[]{:S(2)}, u32[]{:S(2)}) collective-permute-start(f32[4,32,512]{2,1,0:T(8,128)S(1)} %dynamic-slice_add_fusion.37), channel_id=1, source_target_pairs={{0,1},{1,0},{2,3},{3,2},{4,5},{5,4},{6,7},{7,6},{8,9},{9,8},{10,11... | collective-permute-start | bytes 786440 | tf_op jit(solution)/shard_map/ppermute | solution.py:663
  428.9 24.8 %collective-permute-start.47 = (f32[4,16,512]{2,1,0:T(8,128)S(1)}, f32[4,16,512]{2,1,0:T(8,128)S(1)}, u32[]{:S(2)}, u32[]{:S(2)}) collective-permute-start(f32[4,16,512]{2,1,0:T(8,128)S(1)} %dynamic-slice_add_fusion.55), channel_id=1, source_target_pairs={{0,2},{1,3},{2,0},{3,1},{4,6},{5,7},{6,4},{7,5},{8,10},{9,11},{10,... | collective-permute-start | bytes 393224 | tf_op jit(solution)/shard_map/ppermute | solution.py:663
  429.0 36.7 %collective-permute-start.55 = (f32[4,16,512]{2,1,0:T(8,128)S(1)}, f32[4,16,512]{2,1,0:T(8,128)S(1)}, u32[]{:S(2)}, u32[]{:S(2)}) collective-permute-start(f32[4,16,512]{2,1,0:T(8,128)S(1)} %dynamic-slice_add_fusion.53), channel_id=1, source_target_pairs={{0,2},{1,3},{2,0},{3,1},{4,6},{5,7},{6,4},{7,5},{8,10},{9,11},{10,... | collective-permute-start | bytes 393224 | tf_op jit(solution)/shard_map/ppermute | solution.py:663
  435.2 7.7 %collective-permute-start.50 = (f32[2,32,512]{2,1,0:T(8,128)S(1)}, f32[2,32,512]{2,1,0:T(8,128)S(1)}, u32[]{:S(2)}, u32[]{:S(2)}) collective-permute-start(f32[2,32,512]{2,1,0:T(8,128)S(1)} %dynamic-slice_add_fusion.52), channel_id=1, source_target_pairs={{0,16},{1,17},{2,18},{3,19},{4,20},{5,21},{6,22},{7,23},{8,24},{9,... | collective-permute-start | bytes 393224 | tf_op jit(solution)/shard_map/ppermute | solution.py:663
  435.4 36.7 %collective-permute-start.56 = (f32[4,16,512]{2,1,0:T(8,128)S(1)}, f32[4,16,512]{2,1,0:T(8,128)S(1)}, u32[]{:S(2)}, u32[]{:S(2)}) collective-permute-start(f32[4,16,512]{2,1,0:T(8,128)S(1)} %dynamic-slice_add_fusion.50), channel_id=1, source_target_pairs={{0,2},{1,3},{2,0},{3,1},{4,6},{5,7},{6,4},{7,5},{8,10},{9,11},{10,... | collective-permute-start | bytes 393224 | tf_op jit(solution)/shard_map/ppermute | solution.py:663
  436.9 40.4 %collective-permute-start.57 = (f32[4,16,512]{2,1,0:T(8,128)S(1)}, f32[4,16,512]{2,1,0:T(8,128)S(1)}, u32[]{:S(2)}, u32[]{:S(2)}) collective-permute-start(f32[4,16,512]{2,1,0:T(8,128)S(1)} %dynamic-slice_add_fusion.49), channel_id=1, source_target_pairs={{0,2},{1,3},{2,0},{3,1},{4,6},{5,7},{6,4},{7,5},{8,10},{9,11},{10,... | collective-permute-start | bytes 393224 | tf_op jit(solution)/shard_map/ppermute | solution.py:663
  443.0 36.5 %collective-permute-start.58 = (f32[2,16,512]{2,1,0:T(8,128)S(1)}, f32[2,16,512]{2,1,0:T(8,128)S(1)}, u32[]{:S(2)}, u32[]{:S(2)}) collective-permute-start(f32[2,16,512]{2,1,0:T(8,128)S(1)} %dynamic-slice_add_fusion.57), channel_id=1, source_target_pairs={{0,2},{1,3},{2,0},{3,1},{4,6},{5,7},{6,4},{7,5},{8,10},{9,11},{10,... | collective-permute-start | bytes 196616 | tf_op jit(solution)/shard_map/ppermute | solution.py:663
  480.2 9.5 %collective-permute-start.59 = (f32[4,64,512]{2,1,0:T(8,128)}, f32[4,64,512]{2,1,0:T(8,128)S(1)}, u32[]{:S(2)}, u32[]{:S(2)}) collective-permute-start(f32[4,64,512]{2,1,0:T(8,128)} %dynamic-slice_add_fusion.15), channel_id=1, source_target_pairs={{0,8},{1,9},{2,10},{3,11},{4,12},{5,13},{6,14},{7,15},{8,0},{9,1},... | collective-permute-start | bytes 1572872 | tf_op jit(solution)/shard_map/ppermute | solution.py:663
  481.0 10.8 %collective-permute-start.61 = (f32[5,64,512]{2,1,0:T(8,128)}, f32[5,64,512]{2,1,0:T(8,128)S(1)}, u32[]{:S(2)}, u32[]{:S(2)}) collective-permute-start(f32[5,64,512]{2,1,0:T(8,128)} %dynamic-slice_add_fusion.13), channel_id=1, source_target_pairs={{0,16},{1,17},{2,18},{3,19},{4,20},{5,21},{6,22},{7,23},{8,24},{9,... | collective-permute-start | bytes 1966088 | tf_op jit(solution)/shard_map/ppermute | solution.py:663
  489.7 7.0 %collective-permute-start.60 = (f32[4,32,512]{2,1,0:T(8,128)S(1)}, f32[4,32,512]{2,1,0:T(8,128)S(1)}, u32[]{:S(2)}, u32[]{:S(2)}) collective-permute-start(f32[4,32,512]{2,1,0:T(8,128)S(1)} %dynamic-slice_add_fusion.31), channel_id=1, source_target_pairs={{0,1},{1,0},{2,3},{3,2},{4,5},{5,4},{6,7},{7,6},{8,9},{9,8},{10,11... | collective-permute-start | bytes 786440 | tf_op jit(solution)/shard_map/ppermute | solution.py:663
  491.9 16.1 %collective-permute-start.63 = (f32[5,32,512]{2,1,0:T(8,128)S(1)}, f32[5,32,512]{2,1,0:T(8,128)S(1)}, u32[]{:S(2)}, u32[]{:S(2)}) collective-permute-start(f32[5,32,512]{2,1,0:T(8,128)S(1)} %dynamic-slice_add_fusion.29), channel_id=1, source_target_pairs={{0,1},{1,0},{2,3},{3,2},{4,5},{5,4},{6,7},{7,6},{8,9},{9,8},{10,11... | collective-permute-start | bytes 983048 | tf_op jit(solution)/shard_map/ppermute | solution.py:663
  496.7 17.2 %collective-permute-start.62 = (f32[4,16,512]{2,1,0:T(8,128)S(1)}, f32[4,16,512]{2,1,0:T(8,128)S(1)}, u32[]{:S(2)}, u32[]{:S(2)}) collective-permute-start(f32[4,16,512]{2,1,0:T(8,128)S(1)} %dynamic-slice_add_fusion.45), channel_id=1, source_target_pairs={{0,2},{1,3},{2,0},{3,1},{4,6},{5,7},{6,4},{7,5},{8,10},{9,11},{10,... | collective-permute-start | bytes 393224 | tf_op jit(solution)/shard_map/ppermute | solution.py:663
  508.0 14.5 %collective-permute-start.64 = (f32[5,16,512]{2,1,0:T(8,128)S(1)}, f32[5,16,512]{2,1,0:T(8,128)S(1)}, u32[]{:S(2)}, u32[]{:S(2)}) collective-permute-start(f32[5,16,512]{2,1,0:T(8,128)S(1)} %dynamic-slice_add_fusion.43), channel_id=1, source_target_pairs={{0,2},{1,3},{2,0},{3,1},{4,6},{5,7},{6,4},{7,5},{8,10},{9,11},{10,... | collective-permute-start | bytes 491528 | tf_op jit(solution)/shard_map/ppermute | solution.py:663
  522.5 6.3 collective-permute-start.65
  522.6 15.8 %collective-permute-start.67 = (f32[5,16,512]{2,1,0:T(8,128)S(1)}, f32[5,16,512]{2,1,0:T(8,128)S(1)}, u32[]{:S(2)}, u32[]{:S(2)}) collective-permute-start(f32[5,16,512]{2,1,0:T(8,128)S(1)} %add.575), channel_id=1, source_target_pairs={{0,2},{1,3},{2,0},{3,1},{4,6},{5,7},{6,4},{7,5},{8,10},{9,11},{10,... | collective-permute-start | bytes 491528 | tf_op jit(solution)/shard_map/ppermute | solution.py:663
  528.9 22.6 %collective-permute-start.66 = (f32[4,32,512]{2,1,0:T(8,128)S(1)}, f32[4,32,512]{2,1,0:T(8,128)S(1)}, u32[]{:S(2)}, u32[]{:S(2)}) collective-permute-start(f32[4,32,512]{2,1,0:T(8,128)S(1)} %maximum_select_fusion.5), channel_id=1, source_target_pairs={{0,1},{1,0},{2,3},{3,2},{4,5},{5,4},{6,7},{7,6},{8,9},{9,8},{10,11... | collective-permute-start | bytes 786440 | tf_op jit(solution)/shard_map/ppermute | solution.py:663
  538.5 23.7 %collective-permute-start.69 = (f32[5,32,512]{2,1,0:T(8,128)S(1)}, f32[5,32,512]{2,1,0:T(8,128)S(1)}, u32[]{:S(2)}, u32[]{:S(2)}) collective-permute-start(f32[5,32,512]{2,1,0:T(8,128)S(1)} %maximum_select_fusion.4), channel_id=1, source_target_pairs={{0,1},{1,0},{2,3},{3,2},{4,5},{5,4},{6,7},{7,6},{8,9},{9,8},{10,11... | collective-permute-start | bytes 983048 | tf_op jit(solution)/shard_map/ppermute | solution.py:663
  551.5 17.9 %collective-permute-start.68 = (f32[4,64,512]{2,1,0:T(8,128)S(1)}, f32[4,64,512]{2,1,0:T(8,128)S(1)}, u32[]{:S(2)}, u32[]{:S(2)}) collective-permute-start(f32[4,64,512]{2,1,0:T(8,128)S(1)} %maximum_select_fusion.3), channel_id=1, source_target_pairs={{0,8},{1,9},{2,10},{3,11},{4,12},{5,13},{6,14},{7,15},{8,0},{9,1},... | collective-permute-start | bytes 1572872 | tf_op jit(solution)/shard_map/ppermute | solution.py:663
  562.3 20.6 %collective-permute-start.71 = (f32[5,64,512]{2,1,0:T(8,128)S(1)}, f32[5,64,512]{2,1,0:T(8,128)}, u32[]{:S(2)}, u32[]{:S(2)}) collective-permute-start(f32[5,64,512]{2,1,0:T(8,128)S(1)} %maximum_select_fusion.2), channel_id=1, source_target_pairs={{0,16},{1,17},{2,18},{3,19},{4,20},{5,21},{6,22},{7,23},{8,24},{9,... | collective-permute-start | bytes 1966088 | tf_op jit(solution)/shard_map/ppermute | solution.py:663
  584.5 33.5 %collective-permute-start.74 = (f32[5,128,512]{2,1,0:T(8,128)S(1)}, f32[5,128,512]{2,1,0:T(8,128)}, u32[]{:S(2)}, u32[]{:S(2)}) collective-permute-start(f32[5,128,512]{2,1,0:T(8,128)S(1)} %maximum_select_fusion.own_ref), channel_id=1, source_target_pairs={{0,8},{1,9},{2,10},{3,11},{4,12},{5,13},{6,14},{7,15},{8,0},{9,1},... | collective-permute-start | bytes 3932168 | tf_op jit(solution)/shard_map/ppermute | solution.py:663
  585.3 32.7 %collective-permute-start.70 = (f32[4,128,512]{2,1,0:T(8,128)S(1)}, f32[4,128,512]{2,1,0:T(8,128)}, u32[]{:S(2)}, u32[]{:S(2)}) collective-permute-start(f32[4,128,512]{2,1,0:T(8,128)S(1)} %maximum_select_fusion.1.own_ref), channel_id=1, source_target_pairs={{0,16},{1,17},{2,18},{3,19},{4,20},{5,21},{6,22},{7,23},{8,24},{9,... | collective-permute-start | bytes 3145736 | tf_op jit(solution)/shard_map/ppermute | solution.py:663
  587.8 34.5 %collective-permute-start.75 = (f32[5,128,512]{2,1,0:T(8,128)S(1)}, f32[5,128,512]{2,1,0:T(8,128)}, u32[]{:S(2)}, u32[]{:S(2)}) collective-permute-start(f32[5,128,512]{2,1,0:T(8,128)S(1)} %maximum_select_fusion.own_ref), channel_id=1, source_target_pairs={{0,4},{1,5},{2,6},{3,7},{4,0},{5,1},{6,2},{7,3},{8,12},{9,13},{10,... | collective-permute-start | bytes 3932168 | tf_op jit(solution)/shard_map/ppermute | solution.py:663
  618.0 11.6 %collective-permute-start.72 = (f32[4,128,512]{2,1,0:T(8,128)S(1)}, f32[4,128,512]{2,1,0:T(8,128)}, u32[]{:S(2)}, u32[]{:S(2)}) collective-permute-start(f32[4,128,512]{2,1,0:T(8,128)S(1)} %maximum_select_fusion.1.own_ref), channel_id=1, source_target_pairs={{0,4},{1,5},{2,6},{3,7},{4,0},{5,1},{6,2},{7,3},{8,12},{9,13},{10,... | collective-permute-start | bytes 3145736 | tf_op jit(solution)/shard_map/ppermute | solution.py:663
  618.5 11.1 %collective-permute-start.73 = (f32[4,128,512]{2,1,0:T(8,128)}, f32[4,128,512]{2,1,0:T(8,128)}, u32[]{:S(2)}, u32[]{:S(2)}) collective-permute-start(f32[4,128,512]{2,1,0:T(8,128)} %collective-permute-done.70.near_ref), channel_id=1, source_target_pairs={{0,4},{1,5},{2,6},{3,7},{4,0},{5,1},{6,2},{7,3},{8,12},{9,13},{10,... | collective-permute-start | bytes 3145736 | tf_op jit(solution)/shard_map/ppermute | solution.py:663
  (71 other events, 819.1 us)
Sparse Core Ops, SparseCore 0:
  190.6 106.9 reduce-scatter.1
  344.9 138.9 all-gather.4
  487.3 152.0 all-gather.2

commit v4 on v3

--- a/solution.py
+++ b/solution.py
@@ -614,13 +614,15 @@
     )(places, *pieces, *extra)
 
 
-def regroup_kernel(starts, in_ref, *refs):
-    out_ref, rows = refs[-1], in_ref.shape[1]
-    for k, start in enumerate(starts):
-        out_ref[start : start + rows, :] = in_ref[k]
-
-
-def regroup(gathered, starts, total, place, blocks, shape, where, into=None):
+def regroup_kernel(starts, rows, down, in_ref, *refs):
+    out_ref = refs[-1]
+    for j in range(in_ref.shape[1] // rows):
+        base, col = (j * TILE, 0) if down else (0, j * TILE)
+        for k, start in enumerate(starts):
+            out_ref[base + start : base + start + rows, col : col + TILE] = in_ref[k, j * rows : (j + 1) * rows, :]
+
+
+def regroup(gathered, starts, total, place, blocks, shape, down, first=0, into=None):
     devices, rows = gathered.shape[0], gathered.shape[1] // total
     extra = () if into is None else (into,)
     if rows % 8:
@@ -628,12 +630,15 @@
         gathered = gathered.reshape(devices, total, rows, TILE)[order].transpose(1, 0, 2, 3)
         gathered = gathered.reshape(1, total * TILE, TILE)
         devices, rows, starts = 1, TILE, (0,)
+    pair = 2 if all(n % 2 == 0 for n in (place, blocks, first if down else 0)) else 1
+    out_block = (pair * TILE, TILE) if down else (TILE, pair * TILE)
+    where = (lambda b: (first // pair + b, 0)) if down else (lambda b: (first, b))
     return pl.pallas_call(
-        functools.partial(regroup_kernel, starts),
-        grid=(blocks,),
-        in_specs=[pl.BlockSpec((devices, rows, TILE), lambda b: (0, place + b, 0))]
+        functools.partial(regroup_kernel, starts, rows, down),
+        grid=(blocks // pair,),
+        in_specs=[pl.BlockSpec((devices, pair * rows, TILE), lambda b: (0, place // pair + b, 0))]
         + [pl.BlockSpec(memory_space=pl.ANY)] * len(extra),
-        out_specs=pl.BlockSpec((TILE, TILE), where),
+        out_specs=pl.BlockSpec(out_block, where),
         out_shape=shaped(shape),
         input_output_aliases={1: 0} if extra else {},
         compiler_params=outer_params(),
@@ -1142,7 +1147,6 @@
         last.moves.extend(stream.moves)
         return stream.keep
 
-    tall, flat_cols = lambda b: (b, 0), lambda b: (0, b)
     def starts_of(first, order, rows):
         found = []
         for k in range(devices):
@@ -1155,8 +1159,8 @@
 
     spread_starts = starts_of(lambda k: (k // rep) * spread, rep_bits, spread)
     early_out = Early(early, functools.partial(regroup, starts=spread_starts, total=9 + blocks))
-    early_out.add_result(place=0, blocks=blocks, shape=(mid, c_out), where=flat_cols)
-    early_out.add_result(place=blocks, blocks=9, shape=(9 * mid, mid), where=tall)
+    early_out.add_result(place=0, blocks=blocks, shape=(mid, c_out), down=False)
+    early_out.add_result(place=blocks, blocks=9, shape=(9 * mid, mid), down=True)
     backs = [Return(stream, core_bit, flat, devices) for stream in late]
     for stream, back in zip(late, backs):
         stream.moves.extend(back.moves)
@@ -1172,15 +1176,15 @@
 
     half_starts = lambda order: starts_of(lambda k: (k // core_bit % 2) * (TILE // 2), order, TILE // 2)
     regrouped = gathered(jnp.concatenate([s.keep for s in middle + [last.stream]], axis=0))
-    grad_w_squeeze = regrouped(half_starts(order_squeeze), place=0, blocks=blocks, shape=(c_out, mid), where=tall)
+    grad_w_squeeze = regrouped(half_starts(order_squeeze), place=0, blocks=blocks, shape=(c_out, mid), down=True)
     grad_w_expand = regrouped(
-        half_starts(order_expand), place=blocks, blocks=blocks, shape=(mid, c_out), where=flat_cols
+        half_starts(order_expand), place=blocks, blocks=blocks, shape=(mid, c_out), down=False
     )
     grad_w_short = None
     for k in range(in_blocks):
         grad_w_short = regrouped(
             half_starts(order_short[k % 2]), place=(2 + k) * blocks, blocks=blocks, shape=(c_in, c_out),
-            where=lambda b, k=k: (k, b), into=grad_w_short,
+            down=False, first=k, into=grad_w_short,
         )
 
     grad_w_spatial = None
@@ -1190,7 +1194,7 @@
             into=grad_w_spatial,
         )
     grad_w_reduce = regrouped(
-        half_starts(order_reduce), place=(2 + in_blocks) * blocks, blocks=in_blocks, shape=(c_in, mid), where=tall
+        half_starts(order_reduce), place=(2 + in_blocks) * blocks, blocks=in_blocks, shape=(c_in, mid), down=True
     )
     grad_w_window, grad_w_spatial = (g.reshape(3, 3, mid, mid) for g in (grad_w_window, grad_w_spatial))
 

time: 672 us -> 668 us (level)
  no operation moved by 1% of the time
where the time goes in v4:
time: 668 us; the launch traced here: 665 us
  waiting for transfers between devices  271 us (41%)
  Pallas kernels  187 us (28%)
  starting transfers between devices  99.5 us (15%)
  other arithmetic  58.5 us (9%)
  blocking collectives  23.9 us (4%)
  between operations  15 us (2%)
  local copies, waits for them, and re-layouts  9.68 us (1%)
    ppermute x77, waiting for transfers between devices, swap(): return lax.ppermute(values, AXES, [(i, i ^ bit) for i in range(devices)])  243 us
    ppermute x77, starting transfers between devices, swap(): return lax.ppermute(values, AXES, [(i, i ^ bit) for i in range(devices)])  74.4 us
    add x57, other arithmetic, half_sum(): first + lax.dynamic_slice_in_dim(received, which * rows, rows, axis=1)  44.3 us
    pallas_call x7, Pallas kernels, outer_halves(): pl.pallas_call(functools.partial(halves_kernel, pick, per_left), grid_spe...  33.8 us
    pallas_call x7, Pallas kernels, regroup(): pl.pallas_call(functools.partial(regroup_kernel, starts, rows, down), gri...  33 us
    all_to_all x6, starting transfers between devices, sync_all(): return lax.all_to_all(tile, AXES, 0, 0, tiled=True)  24.6 us
    all_to_all x2, blocking collectives, sync_all(): return lax.all_to_all(tile, AXES, 0, 0, tiled=True)  23.9 us
    all_to_all x6, waiting for transfers between devices, sync_all(): return lax.all_to_all(tile, AXES, 0, 0, tiled=True)  17.1 us
  transfers between devices with their start and end apart: 86, of which 57 were waited for; matrix products, arithmetic and copies ran while one was open for 9% of the time, Pallas kernels for 17%

profile of v4, /device:TPU:0, one launch (start us, length us, event | category | flops | bytes accessed | tf_op | source)
XLA Modules:
  0.0 664.5 jit_solution(4540818623143948108)
XLA Ops:
  9.5 6.1 shard_map.434
  15.6 7.3 %all-to-all-start = ((f32[32,16,128]{2,1,0:T(8,128)}), f32[32,16,128]{2,1,0:T(8,128)S(1)}, u32[]{:S(2)}, u32[]{:S(2)}) async-start(f32[32,16,128]{2,1,0:T(8,128)} %get-tuple-element.243), calls=%async_computation | async-start | bytes 524288 | tf_op jit(solution)/shard_map/all_to_all | solution.py:672
  23.2 9.9 %all-to-all-done.stat_ref.count_ref.in_stat_ref = f32[32,16,128]{2,1,0:T(8,128)S(1)} async-done(((f32[32,16,128]{2,1,0:T(8,128)}), f32[32,16,128]{2,1,0:T(8,128)S(1)}, u32[]{:S(2)}, u32[]{:S(2)}) %all-to-all-start) | async-done | bytes 262176 | tf_op jit(solution)/shard_map/all_to_all | solution.py:672
  33.8 7.3 %shard_map.435 = (bf16[4,256,512]{2,1,0:T(8,128)(2,1)}, f32[256,512]{1,0:T(8,128)}, f32[32,8,128]{2,1,0:T(8,128)}) custom-call(f32[4,256,512]{2,1,0:T(8,128)} %get-tuple-element.242.pre_ref.in_ref, f32[32,16,128]{2,1,0:T(8,128)} %copy-done, f32[32,16,128]{2,1,0:T(8,128)} %copy-done, f32[128,128]{1,0:T(8,128)} %copy-done.1, f32[256,128]{1,0:T(8,128)} %bitcast.74, ...), custom_call_target="tpu_custom_call" | custom-call | flops 1207959552 | bytes 8388608 | tf_op jit(solution)/shard_map/pallas_call | solution.py:926
  43.8 5.1 shard_map.437
  52.9 4.8 shard_map.436
  74.8 6.1 shard_map.438
  80.9 12.3 %all_to_all.40.stat_ref.in_stat_ref = f32[32,8,128]{2,1,0:T(8,128)} all-to-all(f32[32,8,128]{2,1,0:T(8,128)} %get-tuple-element.252), channel_id=1, replica_groups=mesh['dp'=8,'rep'=4] {'dp','rep'}, dimensions={0} | all-to-all | bytes 262144 | tf_op jit(solution)/shard_map/all_to_all | solution.py:672
  93.2 5.7 shard_map.439
  98.9 11.7 %all_to_all.41.stat_ref.in_stat_ref = f32[32,8,128]{2,1,0:T(8,128)} all-to-all(f32[32,8,128]{2,1,0:T(8,128)} %get-tuple-element.254), channel_id=1, replica_groups=mesh['dp'=8,'rep'=4] {'dp','rep'}, dimensions={0} | all-to-all | bytes 262144 | tf_op jit(solution)/shard_map/all_to_all | solution.py:672
  110.6 4.8 shard_map.440
  131.4 5.4 shard_map.441
  150.6 3.8 collective-permute-done.20
  155.1 6.2 shard_map.442
  163.9 4.7 shard_map.443.refs_0_
  168.6 3.7 all-to-all-done.4.gsum_ref
  172.9 6.6 shard_map.444
  182.3 7.9 %shard_map.455 = f32[8,832,512]{2,1,0:T(8,128)} custom-call(bf16[256,512]{1,0:T(8,128)(2,1)} %get-tuple-element.299.left_ref, bf16[3,2,160,512]{3,2,1,0:T(8,128)(2,1)} %get-tuple-element.300.right_ref, f32[8,832,512]{2,1,0:T(8,128)} %shard_map.443.refs_0_), custom_call_target="tpu_custom_call", output_to_operand_aliasing={{}: (2, {})} | custom-call | flops 1207959552 | bytes 9437184 | tf_op jit(solution)/shard_map/pallas_call | solution.py:575
  191.1 7.4 %shard_map.445 = (bf16[256,512]{1,0:T(8,128)(2,1)}, f32[256,2048]{1,0:T(8,128)}, f32[64,128]{1,0:T(8,128)}) custom-call(f32[256,512]{1,0:T(8,128)} %get-tuple-element.266.grad_ref, f32[256,512]{1,0:T(8,128)} %get-tuple-element.251.pre_ref.in_ref, f32[32,8,128]{2,1,0:T(8,128)} %all_to_all.40.stat_ref.in_stat_ref, f32[32,8,128]{2,1,0:T(8,128)} %copy-done.22, ...), custom_call_target="tpu_custom_call" | custom-call | flops 536870912 | bytes 11534336 | tf_op jit(solution)/shard_map/pallas_call | solution.py:1021
  212.9 4.6 shard_map.446
  218.9 7.4 %shard_map.447 = (bf16[256,2048]{1,0:T(8,128)(2,1)}, bf16[256,2048]{1,0:T(8,128)(2,1)}, f32[256,512]{1,0:T(8,128)}, f32[32,8,128]{2,1,0:T(8,128)}) custom-call(f32[256,2048]{1,0:T(8,128)} %get-tuple-element.268.gj_ref, f32[256,2048]{1,0:T(8,128)} %get-tuple-element.246.pe_ref, f32[256,2048]{1,0:T(8,128)} %get-tuple-element.248.ps_ref, ...), custom_call_target="tpu_custom_call" | custom-call | flops 536870912 | bytes 11534336 | tf_op jit(solution)/shard_map/pallas_call | solution.py:1046
  226.3 3.9 all-to-all-start.6
  230.2 4.6 shard_map.450
  234.8 4.6 shard_map.449
  239.4 4.5 shard_map.448
  244.9 9.6 %shard_map.451 = (bf16[4,256,512]{2,1,0:T(8,128)(2,1)}, f32[4,256,512]{2,1,0:T(8,128)}, f32[32,8,128]{2,1,0:T(8,128)}) custom-call(f32[256,512]{1,0:T(8,128)} %get-tuple-element.273.grad_ref, f32[256,512]{1,0:T(8,128)} %get-tuple-element.244.pre_ref.in_ref, f32[32,8,128]{2,1,0:T(8,128)} %copy-done.8, f32[32,8,128]{2,1,0:T(8,128)} %copy-done.24, ...), custom_call_target="tpu_custom_call" | custom-call | flops 1207959552 | bytes 12582912 | tf_op jit(solution)/shard_map/pallas_call | solution.py:1079
  254.5 5.5 all-to-all-start.7
  260.1 5.5 shard_map.454.short_ref
  265.6 5.2 shard_map.453
  270.9 5.8 shard_map.452
  291.0 6.6 reduce-scatter.2.cloned.1.call-done
  306.9 6.6 shard_map.456
  313.5 4.4 shard_map.457
  326.9 7.2 %collective-permute-done.39 = f32[4,128,512]{2,1,0:T(8,128)} collective-permute-done((f32[4,128,512]{2,1,0:T(8,128)}, f32[4,128,512]{2,1,0:T(8,128)}, u32[]{:S(2)}, u32[]{:S(2)}) %collective-permute-start.39) | collective-permute-done | bytes 1048608 | tf_op jit(solution)/shard_map/ppermute | solution.py:668
  339.0 4.9 collective-permute-done.37
  349.7 13.2 %collective-permute-done.33 = f32[4,64,512]{2,1,0:T(8,128)} collective-permute-done((f32[4,64,512]{2,1,0:T(8,128)}, f32[4,64,512]{2,1,0:T(8,128)}, u32[]{:S(2)}, u32[]{:S(2)}) %collective-permute-start.33) | collective-permute-done | bytes 524320 | tf_op jit(solution)/shard_map/ppermute | solution.py:668
  369.0 6.9 %collective-permute-done.45 = f32[4,64,512]{2,1,0:T(8,128)S(1)} collective-permute-done((f32[4,64,512]{2,1,0:T(8,128)S(1)}, f32[4,64,512]{2,1,0:T(8,128)S(1)}, u32[]{:S(2)}, u32[]{:S(2)}) %collective-permute-start.45) | collective-permute-done | bytes 524320 | tf_op jit(solution)/shard_map/ppermute | solution.py:668
  376.0 4.9 collective-permute-done.44
  391.7 5.7 collective-permute-done.41
  399.9 7.9 %collective-permute-done.40 = f32[4,32,512]{2,1,0:T(8,128)S(1)} collective-permute-done((f32[4,32,512]{2,1,0:T(8,128)S(1)}, f32[4,32,512]{2,1,0:T(8,128)S(1)}, u32[]{:S(2)}, u32[]{:S(2)}) %collective-permute-start.40) | collective-permute-done | bytes 262176 | tf_op jit(solution)/shard_map/ppermute | solution.py:668
  413.4 15.5 %collective-permute-done.48 = f32[2,64,512]{2,1,0:T(8,128)S(1)} collective-permute-done((f32[2,64,512]{2,1,0:T(8,128)S(1)}, f32[2,64,512]{2,1,0:T(8,128)S(1)}, u32[]{:S(2)}, u32[]{:S(2)}) %collective-permute-start.48) | collective-permute-done | bytes 262176 | tf_op jit(solution)/shard_map/ppermute | solution.py:668
  443.7 10.1 %collective-permute-done.47 = f32[4,16,512]{2,1,0:T(8,128)S(1)} collective-permute-done((f32[4,16,512]{2,1,0:T(8,128)S(1)}, f32[4,16,512]{2,1,0:T(8,128)S(1)}, u32[]{:S(2)}, u32[]{:S(2)}) %collective-permute-start.47) | collective-permute-done | bytes 131104 | tf_op jit(solution)/shard_map/ppermute | solution.py:668
  454.5 11.2 %collective-permute-done.55 = f32[4,16,512]{2,1,0:T(8,128)S(1)} collective-permute-done((f32[4,16,512]{2,1,0:T(8,128)S(1)}, f32[4,16,512]{2,1,0:T(8,128)S(1)}, u32[]{:S(2)}, u32[]{:S(2)}) %collective-permute-start.55) | collective-permute-done | bytes 131104 | tf_op jit(solution)/shard_map/ppermute | solution.py:668
  466.4 5.7 collective-permute-done.56
  472.8 4.6 collective-permute-done.57
  481.4 8.2 %collective-permute-done.59 = f32[4,64,512]{2,1,0:T(8,128)S(1)} collective-permute-done((f32[4,64,512]{2,1,0:T(8,128)}, f32[4,64,512]{2,1,0:T(8,128)S(1)}, u32[]{:S(2)}, u32[]{:S(2)}) %collective-permute-start.59) | collective-permute-done | bytes 524320 | tf_op jit(solution)/shard_map/ppermute | solution.py:668
  492.0 4.6 collective-permute-done.60
  497.1 10.9 %collective-permute-done.63 = f32[5,32,512]{2,1,0:T(8,128)S(1)} collective-permute-done((f32[5,32,512]{2,1,0:T(8,128)S(1)}, f32[5,32,512]{2,1,0:T(8,128)S(1)}, u32[]{:S(2)}, u32[]{:S(2)}) %collective-permute-start.63) | collective-permute-done | bytes 327712 | tf_op jit(solution)/shard_map/ppermute | solution.py:668
  508.0 4.3 collective-permute-start.64
  514.0 8.5 %collective-permute-done.64 = f32[5,16,512]{2,1,0:T(8,128)S(1)} collective-permute-done((f32[5,16,512]{2,1,0:T(8,128)S(1)}, f32[5,16,512]{2,1,0:T(8,128)S(1)}, u32[]{:S(2)}, u32[]{:S(2)}) %collective-permute-start.64) | collective-permute-done | bytes 163872 | tf_op jit(solution)/shard_map/ppermute | solution.py:668
  528.9 9.5 %collective-permute-done.67 = f32[5,16,512]{2,1,0:T(8,128)S(1)} collective-permute-done((f32[5,16,512]{2,1,0:T(8,128)S(1)}, f32[5,16,512]{2,1,0:T(8,128)S(1)}, u32[]{:S(2)}, u32[]{:S(2)}) %collective-permute-start.67) | collective-permute-done | bytes 163872 | tf_op jit(solution)/shard_map/ppermute | solution.py:668
  538.6 12.8 %collective-permute-done.66 = f32[4,32,512]{2,1,0:T(8,128)S(1)} collective-permute-done((f32[4,32,512]{2,1,0:T(8,128)S(1)}, f32[4,32,512]{2,1,0:T(8,128)S(1)}, u32[]{:S(2)}, u32[]{:S(2)}) %collective-permute-start.66) | collective-permute-done | bytes 262176 | tf_op jit(solution)/shard_map/ppermute | solution.py:668
  553.0 9.2 %collective-permute-done.69 = f32[5,32,512]{2,1,0:T(8,128)S(1)} collective-permute-done((f32[5,32,512]{2,1,0:T(8,128)S(1)}, f32[5,32,512]{2,1,0:T(8,128)S(1)}, u32[]{:S(2)}, u32[]{:S(2)}) %collective-permute-start.69) | collective-permute-done | bytes 327712 | tf_op jit(solution)/shard_map/ppermute | solution.py:668
  564.4 4.2 shard_map.459
  568.7 14.2 %collective-permute-done.71 = f32[5,64,512]{2,1,0:T(8,128)} collective-permute-done((f32[5,64,512]{2,1,0:T(8,128)S(1)}, f32[5,64,512]{2,1,0:T(8,128)}, u32[]{:S(2)}, u32[]{:S(2)}) %collective-permute-start.71) | collective-permute-done | bytes 655392 | tf_op jit(solution)/shard_map/ppermute | solution.py:668
  587.8 10.8 %shard_map.460 = f32[4608,512]{1,0:T(8,128)} custom-call(f32[32,208,512]{2,1,0:T(8,128)} %all-gather.5.cloned.1.call-done.in_ref), custom_call_target="tpu_custom_call" | custom-call | bytes 18874368 | tf_op jit(solution)/shard_map/pallas_call | solution.py:636
  598.6 19.4 %collective-permute-done.70.near_ref = f32[4,128,512]{2,1,0:T(8,128)} collective-permute-done((f32[4,128,512]{2,1,0:T(8,128)S(1)}, f32[4,128,512]{2,1,0:T(8,128)}, u32[]{:S(2)}, u32[]{:S(2)}) %collective-permute-start.70) | collective-permute-done | bytes 1048608 | tf_op jit(solution)/shard_map/ppermute | solution.py:668
  622.5 7.1 %shard_map.461.refs_0_ = f32[4608,512]{1,0:T(8,128)} custom-call(s32[4]{0:T(128)} %pad_add_fusion.1.place_ref, f32[5,128,512]{2,1,0:T(8,128)} %copy-done.2, f32[5,128,512]{2,1,0:T(8,128)} %collective-permute-done.74.near_ref, f32[5,128,512]{2,1,0:T(8,128)} %collective-permute-done.75.far_ref, f32[5,128,512]{2,1,0:T(8,128)} %collective-permute-done.76.both_ref), custom_call_target="tpu_custom_call" | custom-call | bytes 10485760 | tf_op jit(solution)/shard_map/pallas_call | solution.py:600
  629.6 5.4 shard_map.462
  635.0 4.4 all-gather.3.cloned.1.call-done.in_ref
  639.4 3.7 shard_map.464.refs_0_
  643.1 3.7 shard_map.463
  646.9 3.7 shard_map.466
  653.6 3.7 shard_map.465
  (358 shorter events, 197.3 us)
Async XLA Ops:
  15.6 17.5 %all-to-all-start = ((f32[32,16,128]{2,1,0:T(8,128)}), f32[32,16,128]{2,1,0:T(8,128)S(1)}, u32[]{:S(2)}, u32[]{:S(2)}) async-start(f32[32,16,128]{2,1,0:T(8,128)} %get-tuple-element.243), calls=%async_computation | async-start | bytes 524288 | tf_op jit(solution)/shard_map/all_to_all | solution.py:672
  41.1 11.1 %all-to-all-start.1 = ((f32[32,8,128]{2,1,0:T(8,128)}), f32[32,8,128]{2,1,0:T(8,128)S(1)}, u32[]{:S(2)}, u32[]{:S(2)}) async-start(f32[32,8,128]{2,1,0:T(8,128)} %get-tuple-element.245), calls=%async_computation.1 | async-start | bytes 262144 | tf_op jit(solution)/shard_map/all_to_all | solution.py:672
  68.4 5.7 collective-permute-start.6
  125.2 5.5 collective-permute-start.13
  145.7 5.0 collective-permute-start.19
  148.9 5.5 collective-permute-start.20
  161.3 11.0 %all-to-all-start.4 = ((f32[32,8,128]{2,1,0:T(8,128)}), f32[32,8,128]{2,1,0:T(8,128)S(1)}, u32[]{:S(2)}, u32[]{:S(2)}) async-start(f32[32,8,128]{2,1,0:T(8,128)} %get-tuple-element.262), calls=%async_computation.4 | async-start | bytes 262144 | tf_op jit(solution)/shard_map/all_to_all | solution.py:672
  179.5 11.0 %all-to-all-start.5 = ((f32[32,8,128]{2,1,0:T(8,128)}), f32[32,8,128]{2,1,0:T(8,128)S(1)}, u32[]{:S(2)}, u32[]{:S(2)}) async-start(f32[32,8,128]{2,1,0:T(8,128)} %get-tuple-element.267), calls=%async_computation.5 | async-start | bytes 262144 | tf_op jit(solution)/shard_map/all_to_all | solution.py:672
  182.1 115.5 %reduce-scatter.2.cloned.1.call-start = ((), (), s32[]{:S(2)}) async-start(), calls=%async_computation.9 | async-start | bytes 15335424 | tf_op jit(solution)/shard_map/reduce_scatter | solution.py:1017
  208.5 9.1 %collective-permute-start.25 = (f32[64,128]{1,0:T(8,128)S(1)}, f32[64,128]{1,0:T(8,128)S(1)}, u32[]{:S(2)}, u32[]{:S(2)}) collective-permute-start(f32[64,128]{1,0:T(8,128)S(1)} %add_add_fusion.1), channel_id=1, source_target_pairs={{0,1},{1,0},{2,3},{3,2},{4,5},{5,4},{6,7},{7,6},{8,9},{9,8},{10,11... | collective-permute-start | bytes 98312 | tf_op jit(solution)/shard_map/ppermute | solution.py:668
  210.1 7.5 %collective-permute-start.26 = (f32[64,128]{1,0:T(8,128)S(1)}, f32[64,128]{1,0:T(8,128)S(1)}, u32[]{:S(2)}, u32[]{:S(2)}) collective-permute-start(f32[64,128]{1,0:T(8,128)S(1)} %add_add_fusion.1), channel_id=1, source_target_pairs={{0,2},{1,3},{2,0},{3,1},{4,6},{5,7},{6,4},{7,5},{8,10},{9,11},{10,... | collective-permute-start | bytes 98312 | tf_op jit(solution)/shard_map/ppermute | solution.py:668
  212.6 5.7 collective-permute-start.27
  218.9 25.1 %collective-permute-start.28 = (f32[4,256,512]{2,1,0:T(8,128)}, f32[4,256,512]{2,1,0:T(8,128)S(1)}, u32[]{:S(2)}, u32[]{:S(2)}) collective-permute-start(f32[4,256,512]{2,1,0:T(8,128)} %get-tuple-element.282), channel_id=1, source_target_pairs={{0,4},{1,5},{2,6},{3,7},{4,0},{5,1},{6,2},{7,3},{8,12},{9,13},{10,... | collective-permute-start | bytes 6291464 | tf_op jit(solution)/shard_map/ppermute | solution.py:668
  226.3 17.6 %all-to-all-start.6 = ((f32[32,8,128]{2,1,0:T(8,128)}), f32[32,8,128]{2,1,0:T(8,128)S(1)}, u32[]{:S(2)}, u32[]{:S(2)}) async-start(f32[32,8,128]{2,1,0:T(8,128)} %get-tuple-element.274), calls=%async_computation.6 | async-start | bytes 262144 | tf_op jit(solution)/shard_map/all_to_all | solution.py:672
  244.0 32.7 %collective-permute-start.31 = (f32[4,256,512]{2,1,0:T(8,128)}, f32[4,256,512]{2,1,0:T(8,128)}, u32[]{:S(2)}, u32[]{:S(2)}) collective-permute-start(f32[4,256,512]{2,1,0:T(8,128)} %get-tuple-element.295), channel_id=1, source_target_pairs={{0,4},{1,5},{2,6},{3,7},{4,0},{5,1},{6,2},{7,3},{8,12},{9,13},{10,... | collective-permute-start | bytes 6291464 | tf_op jit(solution)/shard_map/ppermute | solution.py:668
  244.3 32.4 %collective-permute-start.30 = (f32[4,256,512]{2,1,0:T(8,128)}, f32[4,256,512]{2,1,0:T(8,128)}, u32[]{:S(2)}, u32[]{:S(2)}) collective-permute-start(f32[4,256,512]{2,1,0:T(8,128)} %get-tuple-element.293), channel_id=1, source_target_pairs={{0,4},{1,5},{2,6},{3,7},{4,0},{5,1},{6,2},{7,3},{8,12},{9,13},{10,... | collective-permute-start | bytes 6291464 | tf_op jit(solution)/shard_map/ppermute | solution.py:668
  244.5 32.2 %collective-permute-start.29 = (f32[4,256,512]{2,1,0:T(8,128)}, f32[4,256,512]{2,1,0:T(8,128)}, u32[]{:S(2)}, u32[]{:S(2)}) collective-permute-start(f32[4,256,512]{2,1,0:T(8,128)} %get-tuple-element.291), channel_id=1, source_target_pairs={{0,4},{1,5},{2,6},{3,7},{4,0},{5,1},{6,2},{7,3},{8,12},{9,13},{10,... | collective-permute-start | bytes 6291464 | tf_op jit(solution)/shard_map/ppermute | solution.py:668
  254.5 22.2 %all-to-all-start.7 = ((f32[32,8,128]{2,1,0:T(8,128)}), f32[32,8,128]{2,1,0:T(8,128)S(1)}, u32[]{:S(2)}, u32[]{:S(2)}) async-start(f32[32,8,128]{2,1,0:T(8,128)} %get-tuple-element.285), calls=%async_computation.7 | async-start | bytes 262144 | tf_op jit(solution)/shard_map/all_to_all | solution.py:672
  260.0 304.3 %all-gather.5.cloned.1.call-start = ((), (), s32[]{:S(2)}) async-start(), calls=%async_computation.11 | async-start | bytes 14057472 | tf_op jit(solution)/shard_map/all_gather | solution.py:790
  279.4 38.5 %collective-permute-start.32 = (f32[4,128,512]{2,1,0:T(8,128)}, f32[4,128,512]{2,1,0:T(8,128)}, u32[]{:S(2)}, u32[]{:S(2)}) collective-permute-start(f32[4,128,512]{2,1,0:T(8,128)} %dynamic-slice_add_fusion.11), channel_id=1, source_target_pairs={{0,8},{1,9},{2,10},{3,11},{4,12},{5,13},{6,14},{7,15},{8,0},{9,1},... | collective-permute-start | bytes 3145736 | tf_op jit(solution)/shard_map/ppermute | solution.py:668
  283.5 36.5 %collective-permute-start.35 = (f32[4,128,512]{2,1,0:T(8,128)}, f32[4,128,512]{2,1,0:T(8,128)}, u32[]{:S(2)}, u32[]{:S(2)}) collective-permute-start(f32[4,128,512]{2,1,0:T(8,128)} %dynamic-slice_add_fusion.10), channel_id=1, source_target_pairs={{0,16},{1,17},{2,18},{3,19},{4,20},{5,21},{6,22},{7,23},{8,24},{9,... | collective-permute-start | bytes 3145736 | tf_op jit(solution)/shard_map/ppermute | solution.py:668
  287.3 46.8 %collective-permute-start.39 = (f32[4,128,512]{2,1,0:T(8,128)}, f32[4,128,512]{2,1,0:T(8,128)}, u32[]{:S(2)}, u32[]{:S(2)}) collective-permute-start(f32[4,128,512]{2,1,0:T(8,128)} %dynamic-slice_add_fusion.9), channel_id=1, source_target_pairs={{0,8},{1,9},{2,10},{3,11},{4,12},{5,13},{6,14},{7,15},{8,0},{9,1},... | collective-permute-start | bytes 3145736 | tf_op jit(solution)/shard_map/ppermute | solution.py:668
  290.5 45.6 %collective-permute-start.38 = (f32[4,128,512]{2,1,0:T(8,128)}, f32[4,128,512]{2,1,0:T(8,128)}, u32[]{:S(2)}, u32[]{:S(2)}) collective-permute-start(f32[4,128,512]{2,1,0:T(8,128)} %dynamic-slice_add_fusion.8), channel_id=1, source_target_pairs={{0,16},{1,17},{2,18},{3,19},{4,20},{5,21},{6,22},{7,23},{8,24},{9,... | collective-permute-start | bytes 3145736 | tf_op jit(solution)/shard_map/ppermute | solution.py:668
  300.4 21.5 %collective-permute-start.34 = (f32[13,32,512]{2,1,0:T(8,128)}, f32[13,32,512]{2,1,0:T(8,128)}, u32[]{:S(2)}, u32[]{:S(2)}) collective-permute-start(f32[13,32,512]{2,1,0:T(8,128)} %get-tuple-element.472), channel_id=1, source_target_pairs={{0,1},{1,0},{2,3},{3,2},{4,5},{5,4},{6,7},{7,6},{8,9},{9,8},{10,11... | collective-permute-start | bytes 2555912 | tf_op jit(solution)/shard_map/ppermute | solution.py:668
  323.0 20.9 %collective-permute-start.37 = (f32[13,16,512]{2,1,0:T(8,128)S(1)}, f32[13,16,512]{2,1,0:T(8,128)S(1)}, u32[]{:S(2)}, u32[]{:S(2)}) collective-permute-start(f32[13,16,512]{2,1,0:T(8,128)S(1)} %dynamic-slice_add_fusion.27), channel_id=1, source_target_pairs={{0,2},{1,3},{2,0},{3,1},{4,6},{5,7},{6,4},{7,5},{8,10},{9,11},{10,... | collective-permute-start | bytes 1277960 | tf_op jit(solution)/shard_map/ppermute | solution.py:668
  344.7 294.6 %all-gather.3.cloned.1.call-start = ((), (), s32[]{:S(2)}) async-start(), calls=%async_computation.10 | async-start | bytes 19464192 | tf_op jit(solution)/shard_map/all_gather | solution.py:1172
  345.0 38.4 %collective-permute-start.43 = (f32[5,256,512]{2,1,0:T(8,128)}, f32[5,256,512]{2,1,0:T(8,128)}, u32[]{:S(2)}, u32[]{:S(2)}) collective-permute-start(f32[5,256,512]{2,1,0:T(8,128)} %get-tuple-element.311), channel_id=1, source_target_pairs={{0,4},{1,5},{2,6},{3,7},{4,0},{5,1},{6,2},{7,3},{8,12},{9,13},{10,... | collective-permute-start | bytes 7864328 | tf_op jit(solution)/shard_map/ppermute | solution.py:668
  345.1 20.4 %collective-permute-start.36 = (f32[2,256,512]{2,1,0:T(8,128)}, f32[2,256,512]{2,1,0:T(8,128)}, u32[]{:S(2)}, u32[]{:S(2)}) collective-permute-start(f32[2,256,512]{2,1,0:T(8,128)} %get-tuple-element.330), channel_id=1, source_target_pairs={{0,4},{1,5},{2,6},{3,7},{4,0},{5,1},{6,2},{7,3},{8,12},{9,13},{10,... | collective-permute-start | bytes 3145736 | tf_op jit(solution)/shard_map/ppermute | solution.py:668
  345.6 17.3 %collective-permute-start.33 = (f32[4,64,512]{2,1,0:T(8,128)}, f32[4,64,512]{2,1,0:T(8,128)}, u32[]{:S(2)}, u32[]{:S(2)}) collective-permute-start(f32[4,64,512]{2,1,0:T(8,128)} %dynamic-slice_add_fusion.25), channel_id=1, source_target_pairs={{0,16},{1,17},{2,18},{3,19},{4,20},{5,21},{6,22},{7,23},{8,24},{9,... | collective-permute-start | bytes 1572872 | tf_op jit(solution)/shard_map/ppermute | solution.py:668
  347.1 40.0 %collective-permute-start.42 = (f32[4,256,512]{2,1,0:T(8,128)}, f32[4,256,512]{2,1,0:T(8,128)}, u32[]{:S(2)}, u32[]{:S(2)}) collective-permute-start(f32[4,256,512]{2,1,0:T(8,128)} %get-tuple-element.312), channel_id=1, source_target_pairs={{0,4},{1,5},{2,6},{3,7},{4,0},{5,1},{6,2},{7,3},{8,12},{9,13},{10,... | collective-permute-start | bytes 6291464 | tf_op jit(solution)/shard_map/ppermute | solution.py:668
  347.1 21.8 %collective-permute-start.46 = (f32[4,64,512]{2,1,0:T(8,128)}, f32[4,64,512]{2,1,0:T(8,128)S(1)}, u32[]{:S(2)}, u32[]{:S(2)}) collective-permute-start(f32[4,64,512]{2,1,0:T(8,128)} %dynamic-slice_add_fusion.23), channel_id=1, source_target_pairs={{0,8},{1,9},{2,10},{3,11},{4,12},{5,13},{6,14},{7,15},{8,0},{9,1},... | collective-permute-start | bytes 1572872 | tf_op jit(solution)/shard_map/ppermute | solution.py:668
  362.9 13.1 %collective-permute-start.45 = (f32[4,64,512]{2,1,0:T(8,128)S(1)}, f32[4,64,512]{2,1,0:T(8,128)S(1)}, u32[]{:S(2)}, u32[]{:S(2)}) collective-permute-start(f32[4,64,512]{2,1,0:T(8,128)S(1)} %copy-done.30), channel_id=1, source_target_pairs={{0,16},{1,17},{2,18},{3,19},{4,20},{5,21},{6,22},{7,23},{8,24},{9,... | collective-permute-start | bytes 1572872 | tf_op jit(solution)/shard_map/ppermute | solution.py:668
  365.5 15.4 %collective-permute-start.44 = (f32[4,64,512]{2,1,0:T(8,128)S(1)}, f32[4,64,512]{2,1,0:T(8,128)S(1)}, u32[]{:S(2)}, u32[]{:S(2)}) collective-permute-start(f32[4,64,512]{2,1,0:T(8,128)S(1)} %copy-done.29), channel_id=1, source_target_pairs={{0,8},{1,9},{2,10},{3,11},{4,12},{5,13},{6,14},{7,15},{8,0},{9,1},... | collective-permute-start | bytes 1572872 | tf_op jit(solution)/shard_map/ppermute | solution.py:668
  368.9 28.5 %collective-permute-start.41 = (f32[2,128,512]{2,1,0:T(8,128)S(1)}, f32[2,128,512]{2,1,0:T(8,128)S(1)}, u32[]{:S(2)}, u32[]{:S(2)}) collective-permute-start(f32[2,128,512]{2,1,0:T(8,128)S(1)} %dynamic-slice_add_fusion.20), channel_id=1, source_target_pairs={{0,1},{1,0},{2,3},{3,2},{4,5},{5,4},{6,7},{7,6},{8,9},{9,8},{10,11... | collective-permute-start | bytes 1572872 | tf_op jit(solution)/shard_map/ppermute | solution.py:668
  375.9 31.8 %collective-permute-start.40 = (f32[4,32,512]{2,1,0:T(8,128)S(1)}, f32[4,32,512]{2,1,0:T(8,128)S(1)}, u32[]{:S(2)}, u32[]{:S(2)}) collective-permute-start(f32[4,32,512]{2,1,0:T(8,128)S(1)} %dynamic-slice_add_fusion.41), channel_id=1, source_target_pairs={{0,1},{1,0},{2,3},{3,2},{4,5},{5,4},{6,7},{7,6},{8,9},{9,8},{10,11... | collective-permute-start | bytes 786440 | tf_op jit(solution)/shard_map/ppermute | solution.py:668
  380.9 32.5 %collective-permute-start.49 = (f32[4,32,512]{2,1,0:T(8,128)S(1)}, f32[4,32,512]{2,1,0:T(8,128)S(1)}, u32[]{:S(2)}, u32[]{:S(2)}) collective-permute-start(f32[4,32,512]{2,1,0:T(8,128)S(1)} %dynamic-slice_add_fusion.39), channel_id=1, source_target_pairs={{0,1},{1,0},{2,3},{3,2},{4,5},{5,4},{6,7},{7,6},{8,9},{9,8},{10,11... | collective-permute-start | bytes 786440 | tf_op jit(solution)/shard_map/ppermute | solution.py:668
  383.4 45.5 %collective-permute-start.54 = (f32[4,32,512]{2,1,0:T(8,128)S(1)}, f32[4,32,512]{2,1,0:T(8,128)S(1)}, u32[]{:S(2)}, u32[]{:S(2)}) collective-permute-start(f32[4,32,512]{2,1,0:T(8,128)S(1)} %dynamic-slice_add_fusion.38), channel_id=1, source_target_pairs={{0,1},{1,0},{2,3},{3,2},{4,5},{5,4},{6,7},{7,6},{8,9},{9,8},{10,11... | collective-permute-start | bytes 786440 | tf_op jit(solution)/shard_map/ppermute | solution.py:668
  388.6 46.8 %collective-permute-start.52 = (f32[4,128,512]{2,1,0:T(8,128)S(1)}, f32[4,128,512]{2,1,0:T(8,128)S(1)}, u32[]{:S(2)}, u32[]{:S(2)}) collective-permute-start(f32[4,128,512]{2,1,0:T(8,128)S(1)} %dynamic-slice_add_fusion.3), channel_id=1, source_target_pairs={{0,16},{1,17},{2,18},{3,19},{4,20},{5,21},{6,22},{7,23},{8,24},{9,... | collective-permute-start | bytes 3145736 | tf_op jit(solution)/shard_map/ppermute | solution.py:668
  397.4 39.5 %collective-permute-start.51 = (f32[5,128,512]{2,1,0:T(8,128)S(1)}, f32[5,128,512]{2,1,0:T(8,128)S(1)}, u32[]{:S(2)}, u32[]{:S(2)}) collective-permute-start(f32[5,128,512]{2,1,0:T(8,128)S(1)} %dynamic-slice_add_fusion.1), channel_id=1, source_target_pairs={{0,8},{1,9},{2,10},{3,11},{4,12},{5,13},{6,14},{7,15},{8,0},{9,1},... | collective-permute-start | bytes 3932168 | tf_op jit(solution)/shard_map/ppermute | solution.py:668
  407.8 21.2 %collective-permute-start.48 = (f32[2,64,512]{2,1,0:T(8,128)S(1)}, f32[2,64,512]{2,1,0:T(8,128)S(1)}, u32[]{:S(2)}, u32[]{:S(2)}) collective-permute-start(f32[2,64,512]{2,1,0:T(8,128)S(1)} %dynamic-slice_add_fusion.36), channel_id=1, source_target_pairs={{0,8},{1,9},{2,10},{3,11},{4,12},{5,13},{6,14},{7,15},{8,0},{9,1},... | collective-permute-start | bytes 786440 | tf_op jit(solution)/shard_map/ppermute | solution.py:668
  413.4 21.9 %collective-permute-start.53 = (f32[4,32,512]{2,1,0:T(8,128)S(1)}, f32[4,32,512]{2,1,0:T(8,128)S(1)}, u32[]{:S(2)}, u32[]{:S(2)}) collective-permute-start(f32[4,32,512]{2,1,0:T(8,128)S(1)} %dynamic-slice_add_fusion.37), channel_id=1, source_target_pairs={{0,1},{1,0},{2,3},{3,2},{4,5},{5,4},{6,7},{7,6},{8,9},{9,8},{10,11... | collective-permute-start | bytes 786440 | tf_op jit(solution)/shard_map/ppermute | solution.py:668
  428.9 24.8 %collective-permute-start.47 = (f32[4,16,512]{2,1,0:T(8,128)S(1)}, f32[4,16,512]{2,1,0:T(8,128)S(1)}, u32[]{:S(2)}, u32[]{:S(2)}) collective-permute-start(f32[4,16,512]{2,1,0:T(8,128)S(1)} %dynamic-slice_add_fusion.55), channel_id=1, source_target_pairs={{0,2},{1,3},{2,0},{3,1},{4,6},{5,7},{6,4},{7,5},{8,10},{9,11},{10,... | collective-permute-start | bytes 393224 | tf_op jit(solution)/shard_map/ppermute | solution.py:668
  429.0 36.7 %collective-permute-start.55 = (f32[4,16,512]{2,1,0:T(8,128)S(1)}, f32[4,16,512]{2,1,0:T(8,128)S(1)}, u32[]{:S(2)}, u32[]{:S(2)}) collective-permute-start(f32[4,16,512]{2,1,0:T(8,128)S(1)} %dynamic-slice_add_fusion.53), channel_id=1, source_target_pairs={{0,2},{1,3},{2,0},{3,1},{4,6},{5,7},{6,4},{7,5},{8,10},{9,11},{10,... | collective-permute-start | bytes 393224 | tf_op jit(solution)/shard_map/ppermute | solution.py:668
  435.2 7.7 %collective-permute-start.50 = (f32[2,32,512]{2,1,0:T(8,128)S(1)}, f32[2,32,512]{2,1,0:T(8,128)S(1)}, u32[]{:S(2)}, u32[]{:S(2)}) collective-permute-start(f32[2,32,512]{2,1,0:T(8,128)S(1)} %dynamic-slice_add_fusion.52), channel_id=1, source_target_pairs={{0,16},{1,17},{2,18},{3,19},{4,20},{5,21},{6,22},{7,23},{8,24},{9,... | collective-permute-start | bytes 393224 | tf_op jit(solution)/shard_map/ppermute | solution.py:668
  435.4 36.7 %collective-permute-start.56 = (f32[4,16,512]{2,1,0:T(8,128)S(1)}, f32[4,16,512]{2,1,0:T(8,128)S(1)}, u32[]{:S(2)}, u32[]{:S(2)}) collective-permute-start(f32[4,16,512]{2,1,0:T(8,128)S(1)} %dynamic-slice_add_fusion.50), channel_id=1, source_target_pairs={{0,2},{1,3},{2,0},{3,1},{4,6},{5,7},{6,4},{7,5},{8,10},{9,11},{10,... | collective-permute-start | bytes 393224 | tf_op jit(solution)/shard_map/ppermute | solution.py:668
  436.9 40.4 %collective-permute-start.57 = (f32[4,16,512]{2,1,0:T(8,128)S(1)}, f32[4,16,512]{2,1,0:T(8,128)S(1)}, u32[]{:S(2)}, u32[]{:S(2)}) collective-permute-start(f32[4,16,512]{2,1,0:T(8,128)S(1)} %dynamic-slice_add_fusion.49), channel_id=1, source_target_pairs={{0,2},{1,3},{2,0},{3,1},{4,6},{5,7},{6,4},{7,5},{8,10},{9,11},{10,... | collective-permute-start | bytes 393224 | tf_op jit(solution)/shard_map/ppermute | solution.py:668
  443.0 36.5 %collective-permute-start.58 = (f32[2,16,512]{2,1,0:T(8,128)S(1)}, f32[2,16,512]{2,1,0:T(8,128)S(1)}, u32[]{:S(2)}, u32[]{:S(2)}) collective-permute-start(f32[2,16,512]{2,1,0:T(8,128)S(1)} %dynamic-slice_add_fusion.57), channel_id=1, source_target_pairs={{0,2},{1,3},{2,0},{3,1},{4,6},{5,7},{6,4},{7,5},{8,10},{9,11},{10,... | collective-permute-start | bytes 196616 | tf_op jit(solution)/shard_map/ppermute | solution.py:668
  480.2 9.5 %collective-permute-start.59 = (f32[4,64,512]{2,1,0:T(8,128)}, f32[4,64,512]{2,1,0:T(8,128)S(1)}, u32[]{:S(2)}, u32[]{:S(2)}) collective-permute-start(f32[4,64,512]{2,1,0:T(8,128)} %dynamic-slice_add_fusion.15), channel_id=1, source_target_pairs={{0,8},{1,9},{2,10},{3,11},{4,12},{5,13},{6,14},{7,15},{8,0},{9,1},... | collective-permute-start | bytes 1572872 | tf_op jit(solution)/shard_map/ppermute | solution.py:668
  481.0 10.8 %collective-permute-start.61 = (f32[5,64,512]{2,1,0:T(8,128)}, f32[5,64,512]{2,1,0:T(8,128)S(1)}, u32[]{:S(2)}, u32[]{:S(2)}) collective-permute-start(f32[5,64,512]{2,1,0:T(8,128)} %dynamic-slice_add_fusion.13), channel_id=1, source_target_pairs={{0,16},{1,17},{2,18},{3,19},{4,20},{5,21},{6,22},{7,23},{8,24},{9,... | collective-permute-start | bytes 1966088 | tf_op jit(solution)/shard_map/ppermute | solution.py:668
  489.7 7.0 %collective-permute-start.60 = (f32[4,32,512]{2,1,0:T(8,128)S(1)}, f32[4,32,512]{2,1,0:T(8,128)S(1)}, u32[]{:S(2)}, u32[]{:S(2)}) collective-permute-start(f32[4,32,512]{2,1,0:T(8,128)S(1)} %dynamic-slice_add_fusion.31), channel_id=1, source_target_pairs={{0,1},{1,0},{2,3},{3,2},{4,5},{5,4},{6,7},{7,6},{8,9},{9,8},{10,11... | collective-permute-start | bytes 786440 | tf_op jit(solution)/shard_map/ppermute | solution.py:668
  491.9 16.1 %collective-permute-start.63 = (f32[5,32,512]{2,1,0:T(8,128)S(1)}, f32[5,32,512]{2,1,0:T(8,128)S(1)}, u32[]{:S(2)}, u32[]{:S(2)}) collective-permute-start(f32[5,32,512]{2,1,0:T(8,128)S(1)} %dynamic-slice_add_fusion.29), channel_id=1, source_target_pairs={{0,1},{1,0},{2,3},{3,2},{4,5},{5,4},{6,7},{7,6},{8,9},{9,8},{10,11... | collective-permute-start | bytes 983048 | tf_op jit(solution)/shard_map/ppermute | solution.py:668
  496.7 17.2 %collective-permute-start.62 = (f32[4,16,512]{2,1,0:T(8,128)S(1)}, f32[4,16,512]{2,1,0:T(8,128)S(1)}, u32[]{:S(2)}, u32[]{:S(2)}) collective-permute-start(f32[4,16,512]{2,1,0:T(8,128)S(1)} %dynamic-slice_add_fusion.45), channel_id=1, source_target_pairs={{0,2},{1,3},{2,0},{3,1},{4,6},{5,7},{6,4},{7,5},{8,10},{9,11},{10,... | collective-permute-start | bytes 393224 | tf_op jit(solution)/shard_map/ppermute | solution.py:668
  508.0 14.5 %collective-permute-start.64 = (f32[5,16,512]{2,1,0:T(8,128)S(1)}, f32[5,16,512]{2,1,0:T(8,128)S(1)}, u32[]{:S(2)}, u32[]{:S(2)}) collective-permute-start(f32[5,16,512]{2,1,0:T(8,128)S(1)} %dynamic-slice_add_fusion.43), channel_id=1, source_target_pairs={{0,2},{1,3},{2,0},{3,1},{4,6},{5,7},{6,4},{7,5},{8,10},{9,11},{10,... | collective-permute-start | bytes 491528 | tf_op jit(solution)/shard_map/ppermute | solution.py:668
  522.5 6.3 collective-permute-start.65
  522.6 15.8 %collective-permute-start.67 = (f32[5,16,512]{2,1,0:T(8,128)S(1)}, f32[5,16,512]{2,1,0:T(8,128)S(1)}, u32[]{:S(2)}, u32[]{:S(2)}) collective-permute-start(f32[5,16,512]{2,1,0:T(8,128)S(1)} %add.575), channel_id=1, source_target_pairs={{0,2},{1,3},{2,0},{3,1},{4,6},{5,7},{6,4},{7,5},{8,10},{9,11},{10,... | collective-permute-start | bytes 491528 | tf_op jit(solution)/shard_map/ppermute | solution.py:668
  528.9 22.6 %collective-permute-start.66 = (f32[4,32,512]{2,1,0:T(8,128)S(1)}, f32[4,32,512]{2,1,0:T(8,128)S(1)}, u32[]{:S(2)}, u32[]{:S(2)}) collective-permute-start(f32[4,32,512]{2,1,0:T(8,128)S(1)} %maximum_select_fusion.5), channel_id=1, source_target_pairs={{0,1},{1,0},{2,3},{3,2},{4,5},{5,4},{6,7},{7,6},{8,9},{9,8},{10,11... | collective-permute-start | bytes 786440 | tf_op jit(solution)/shard_map/ppermute | solution.py:668
  538.5 23.7 %collective-permute-start.69 = (f32[5,32,512]{2,1,0:T(8,128)S(1)}, f32[5,32,512]{2,1,0:T(8,128)S(1)}, u32[]{:S(2)}, u32[]{:S(2)}) collective-permute-start(f32[5,32,512]{2,1,0:T(8,128)S(1)} %maximum_select_fusion.4), channel_id=1, source_target_pairs={{0,1},{1,0},{2,3},{3,2},{4,5},{5,4},{6,7},{7,6},{8,9},{9,8},{10,11... | collective-permute-start | bytes 983048 | tf_op jit(solution)/shard_map/ppermute | solution.py:668
  551.5 17.1 %collective-permute-start.68 = (f32[4,64,512]{2,1,0:T(8,128)S(1)}, f32[4,64,512]{2,1,0:T(8,128)S(1)}, u32[]{:S(2)}, u32[]{:S(2)}) collective-permute-start(f32[4,64,512]{2,1,0:T(8,128)S(1)} %maximum_select_fusion.3), channel_id=1, source_target_pairs={{0,8},{1,9},{2,10},{3,11},{4,12},{5,13},{6,14},{7,15},{8,0},{9,1},... | collective-permute-start | bytes 1572872 | tf_op jit(solution)/shard_map/ppermute | solution.py:668
  562.3 20.6 %collective-permute-start.71 = (f32[5,64,512]{2,1,0:T(8,128)S(1)}, f32[5,64,512]{2,1,0:T(8,128)}, u32[]{:S(2)}, u32[]{:S(2)}) collective-permute-start(f32[5,64,512]{2,1,0:T(8,128)S(1)} %maximum_select_fusion.2), channel_id=1, source_target_pairs={{0,16},{1,17},{2,18},{3,19},{4,20},{5,21},{6,22},{7,23},{8,24},{9,... | collective-permute-start | bytes 1966088 | tf_op jit(solution)/shard_map/ppermute | solution.py:668
  584.5 33.5 %collective-permute-start.74 = (f32[5,128,512]{2,1,0:T(8,128)S(1)}, f32[5,128,512]{2,1,0:T(8,128)}, u32[]{:S(2)}, u32[]{:S(2)}) collective-permute-start(f32[5,128,512]{2,1,0:T(8,128)S(1)} %maximum_select_fusion.own_ref), channel_id=1, source_target_pairs={{0,8},{1,9},{2,10},{3,11},{4,12},{5,13},{6,14},{7,15},{8,0},{9,1},... | collective-permute-start | bytes 3932168 | tf_op jit(solution)/shard_map/ppermute | solution.py:668
  585.3 32.7 %collective-permute-start.70 = (f32[4,128,512]{2,1,0:T(8,128)S(1)}, f32[4,128,512]{2,1,0:T(8,128)}, u32[]{:S(2)}, u32[]{:S(2)}) collective-permute-start(f32[4,128,512]{2,1,0:T(8,128)S(1)} %maximum_select_fusion.1.own_ref), channel_id=1, source_target_pairs={{0,16},{1,17},{2,18},{3,19},{4,20},{5,21},{6,22},{7,23},{8,24},{9,... | collective-permute-start | bytes 3145736 | tf_op jit(solution)/shard_map/ppermute | solution.py:668
  587.8 34.5 %collective-permute-start.75 = (f32[5,128,512]{2,1,0:T(8,128)S(1)}, f32[5,128,512]{2,1,0:T(8,128)}, u32[]{:S(2)}, u32[]{:S(2)}) collective-permute-start(f32[5,128,512]{2,1,0:T(8,128)S(1)} %maximum_select_fusion.own_ref), channel_id=1, source_target_pairs={{0,4},{1,5},{2,6},{3,7},{4,0},{5,1},{6,2},{7,3},{8,12},{9,13},{10,... | collective-permute-start | bytes 3932168 | tf_op jit(solution)/shard_map/ppermute | solution.py:668
  618.0 11.6 %collective-permute-start.72 = (f32[4,128,512]{2,1,0:T(8,128)S(1)}, f32[4,128,512]{2,1,0:T(8,128)}, u32[]{:S(2)}, u32[]{:S(2)}) collective-permute-start(f32[4,128,512]{2,1,0:T(8,128)S(1)} %maximum_select_fusion.1.own_ref), channel_id=1, source_target_pairs={{0,4},{1,5},{2,6},{3,7},{4,0},{5,1},{6,2},{7,3},{8,12},{9,13},{10,... | collective-permute-start | bytes 3145736 | tf_op jit(solution)/shard_map/ppermute | solution.py:668
  618.5 11.1 %collective-permute-start.73 = (f32[4,128,512]{2,1,0:T(8,128)}, f32[4,128,512]{2,1,0:T(8,128)}, u32[]{:S(2)}, u32[]{:S(2)}) collective-permute-start(f32[4,128,512]{2,1,0:T(8,128)} %collective-permute-done.70.near_ref), channel_id=1, source_target_pairs={{0,4},{1,5},{2,6},{3,7},{4,0},{5,1},{6,2},{7,3},{8,12},{9,13},{10,... | collective-permute-start | bytes 3145736 | tf_op jit(solution)/shard_map/ppermute | solution.py:668
  (71 other events, 816.4 us)
Sparse Core Ops, SparseCore 0:
  190.6 106.9 reduce-scatter.1
  344.9 138.9 all-gather.4
  487.3 152.0 all-gather.2

commit v5 on v4

--- a/solution.py
+++ b/solution.py
@@ -18,7 +18,7 @@
 MIB = 60
 SCHEDULE = (
     0, 1, 2, 3, 7, 4, 5, 9, 0, 1, 7, 6, 2, 3, 7, 6, 0, 1, 2, 3, 4, 5, 6, 0, 1, 6, 2, 3, 5, 4,
-    6, 0, 1, 2, 3, 6, 5, 4, 5, 4, 5, 4, 5, 4, 5, 4, 5, 4, 8, 5, 4, 8, 5, 4,
+    6, 0, 1, 2, 3, 6, 5, 4, 5, 4, 5, 4, 5, 4, 5, 4, 5, 4, 5, 4, 8, 8, 5, 4,
 )
 
 

time: 668 us -> 668 us (level)
  transfers between devices with their start and end apart: 86 -> 86, of which waited for: 57 -> 58; matrix products, arithmetic and copies ran while one was open for 9% -> 9% of each run, Pallas kernels for 17% -> 17%
where the time goes in v5:
time: 668 us; the launch traced here: 665 us
  waiting for transfers between devices  272 us (41%)
  Pallas kernels  186 us (28%)
  starting transfers between devices  99.5 us (15%)
  other arithmetic  58.5 us (9%)
  blocking collectives  23.9 us (4%)
  between operations  15 us (2%)
  local copies, waits for them, and re-layouts  9.68 us (1%)
    ppermute x77, waiting for transfers between devices, swap(): return lax.ppermute(values, AXES, [(i, i ^ bit) for i in range(devices)])  243 us
    ppermute x77, starting transfers between devices, swap(): return lax.ppermute(values, AXES, [(i, i ^ bit) for i in range(devices)])  74.4 us
    add x57, other arithmetic, half_sum(): first + lax.dynamic_slice_in_dim(received, which * rows, rows, axis=1)  44.3 us
    pallas_call x7, Pallas kernels, outer_halves(): pl.pallas_call(functools.partial(halves_kernel, pick, per_left), grid_spe...  33.8 us
    pallas_call x7, Pallas kernels, regroup(): pl.pallas_call(functools.partial(regroup_kernel, starts, rows, down), gri...  32.6 us
    all_to_all x6, starting transfers between devices, sync_all(): return lax.all_to_all(tile, AXES, 0, 0, tiled=True)  24.6 us
    all_to_all x2, blocking collectives, sync_all(): return lax.all_to_all(tile, AXES, 0, 0, tiled=True)  23.9 us
    all_to_all x6, waiting for transfers between devices, sync_all(): return lax.all_to_all(tile, AXES, 0, 0, tiled=True)  17.1 us
  transfers between devices with their start and end apart: 86, of which 58 were waited for; matrix products, arithmetic and copies ran while one was open for 9% of the time, Pallas kernels for 17%

profile of v5, /device:TPU:0, one launch (start us, length us, event | category | flops | bytes accessed | tf_op | source)
XLA Modules:
  0.0 664.5 jit_solution(5938052189904690401)
XLA Ops:
  9.5 6.1 shard_map.434
  15.6 7.3 %all-to-all-start = ((f32[32,16,128]{2,1,0:T(8,128)}), f32[32,16,128]{2,1,0:T(8,128)S(1)}, u32[]{:S(2)}, u32[]{:S(2)}) async-start(f32[32,16,128]{2,1,0:T(8,128)} %get-tuple-element.243), calls=%async_computation | async-start | bytes 524288 | tf_op jit(solution)/shard_map/all_to_all | solution.py:672
  23.2 9.9 %all-to-all-done.stat_ref.count_ref.in_stat_ref = f32[32,16,128]{2,1,0:T(8,128)S(1)} async-done(((f32[32,16,128]{2,1,0:T(8,128)}), f32[32,16,128]{2,1,0:T(8,128)S(1)}, u32[]{:S(2)}, u32[]{:S(2)}) %all-to-all-start) | async-done | bytes 262176 | tf_op jit(solution)/shard_map/all_to_all | solution.py:672
  33.8 7.3 %shard_map.435 = (bf16[4,256,512]{2,1,0:T(8,128)(2,1)}, f32[256,512]{1,0:T(8,128)}, f32[32,8,128]{2,1,0:T(8,128)}) custom-call(f32[4,256,512]{2,1,0:T(8,128)} %get-tuple-element.242.pre_ref.in_ref, f32[32,16,128]{2,1,0:T(8,128)} %copy-done, f32[32,16,128]{2,1,0:T(8,128)} %copy-done, f32[128,128]{1,0:T(8,128)} %copy-done.1, f32[256,128]{1,0:T(8,128)} %bitcast.74, ...), custom_call_target="tpu_custom_call" | custom-call | flops 1207959552 | bytes 8388608 | tf_op jit(solution)/shard_map/pallas_call | solution.py:926
  43.8 5.1 shard_map.437
  52.9 4.8 shard_map.436
  74.8 6.1 shard_map.438
  80.9 12.3 %all_to_all.40.stat_ref.in_stat_ref = f32[32,8,128]{2,1,0:T(8,128)} all-to-all(f32[32,8,128]{2,1,0:T(8,128)} %get-tuple-element.252), channel_id=1, replica_groups=mesh['dp'=8,'rep'=4] {'dp','rep'}, dimensions={0} | all-to-all | bytes 262144 | tf_op jit(solution)/shard_map/all_to_all | solution.py:672
  93.2 5.7 shard_map.439
  98.9 11.7 %all_to_all.41.stat_ref.in_stat_ref = f32[32,8,128]{2,1,0:T(8,128)} all-to-all(f32[32,8,128]{2,1,0:T(8,128)} %get-tuple-element.254), channel_id=1, replica_groups=mesh['dp'=8,'rep'=4] {'dp','rep'}, dimensions={0} | all-to-all | bytes 262144 | tf_op jit(solution)/shard_map/all_to_all | solution.py:672
  110.6 4.8 shard_map.440
  131.4 5.4 shard_map.441
  150.6 3.8 collective-permute-done.20
  155.1 6.2 shard_map.442
  163.9 4.7 shard_map.443.refs_0_
  168.6 3.7 all-to-all-done.4.gsum_ref
  172.9 6.6 shard_map.444
  182.3 7.9 %shard_map.455 = f32[8,832,512]{2,1,0:T(8,128)} custom-call(bf16[256,512]{1,0:T(8,128)(2,1)} %get-tuple-element.299.left_ref, bf16[3,2,160,512]{3,2,1,0:T(8,128)(2,1)} %get-tuple-element.300.right_ref, f32[8,832,512]{2,1,0:T(8,128)} %shard_map.443.refs_0_), custom_call_target="tpu_custom_call", output_to_operand_aliasing={{}: (2, {})} | custom-call | flops 1207959552 | bytes 9437184 | tf_op jit(solution)/shard_map/pallas_call | solution.py:575
  191.1 7.4 %shard_map.445 = (bf16[256,512]{1,0:T(8,128)(2,1)}, f32[256,2048]{1,0:T(8,128)}, f32[64,128]{1,0:T(8,128)}) custom-call(f32[256,512]{1,0:T(8,128)} %get-tuple-element.266.grad_ref, f32[256,512]{1,0:T(8,128)} %get-tuple-element.251.pre_ref.in_ref, f32[32,8,128]{2,1,0:T(8,128)} %all_to_all.40.stat_ref.in_stat_ref, f32[32,8,128]{2,1,0:T(8,128)} %copy-done.22, ...), custom_call_target="tpu_custom_call" | custom-call | flops 536870912 | bytes 11534336 | tf_op jit(solution)/shard_map/pallas_call | solution.py:1021
  212.9 4.6 shard_map.446
  218.9 7.4 %shard_map.447 = (bf16[256,2048]{1,0:T(8,128)(2,1)}, bf16[256,2048]{1,0:T(8,128)(2,1)}, f32[256,512]{1,0:T(8,128)}, f32[32,8,128]{2,1,0:T(8,128)}) custom-call(f32[256,2048]{1,0:T(8,128)} %get-tuple-element.268.gj_ref, f32[256,2048]{1,0:T(8,128)} %get-tuple-element.246.pe_ref, f32[256,2048]{1,0:T(8,128)} %get-tuple-element.248.ps_ref, ...), custom_call_target="tpu_custom_call" | custom-call | flops 536870912 | bytes 11534336 | tf_op jit(solution)/shard_map/pallas_call | solution.py:1046
  226.3 3.9 all-to-all-start.6
  230.2 4.6 shard_map.450
  234.8 4.6 shard_map.449
  239.4 4.5 shard_map.448
  244.9 9.6 %shard_map.451 = (bf16[4,256,512]{2,1,0:T(8,128)(2,1)}, f32[4,256,512]{2,1,0:T(8,128)}, f32[32,8,128]{2,1,0:T(8,128)}) custom-call(f32[256,512]{1,0:T(8,128)} %get-tuple-element.273.grad_ref, f32[256,512]{1,0:T(8,128)} %get-tuple-element.244.pre_ref.in_ref, f32[32,8,128]{2,1,0:T(8,128)} %copy-done.8, f32[32,8,128]{2,1,0:T(8,128)} %copy-done.24, ...), custom_call_target="tpu_custom_call" | custom-call | flops 1207959552 | bytes 12582912 | tf_op jit(solution)/shard_map/pallas_call | solution.py:1079
  254.5 5.5 all-to-all-start.7
  260.1 5.5 shard_map.454.short_ref
  265.6 5.2 shard_map.453
  270.9 5.8 shard_map.452
  291.0 6.6 reduce-scatter.2.cloned.1.call-done
  306.9 6.6 shard_map.456
  313.5 4.4 shard_map.457
  326.9 7.2 %collective-permute-done.39 = f32[4,128,512]{2,1,0:T(8,128)} collective-permute-done((f32[4,128,512]{2,1,0:T(8,128)}, f32[4,128,512]{2,1,0:T(8,128)}, u32[]{:S(2)}, u32[]{:S(2)}) %collective-permute-start.39) | collective-permute-done | bytes 1048608 | tf_op jit(solution)/shard_map/ppermute | solution.py:668
  339.0 4.9 collective-permute-done.37
  349.7 13.2 %collective-permute-done.33 = f32[4,64,512]{2,1,0:T(8,128)} collective-permute-done((f32[4,64,512]{2,1,0:T(8,128)}, f32[4,64,512]{2,1,0:T(8,128)}, u32[]{:S(2)}, u32[]{:S(2)}) %collective-permute-start.33) | collective-permute-done | bytes 524320 | tf_op jit(solution)/shard_map/ppermute | solution.py:668
  369.0 6.9 %collective-permute-done.45 = f32[4,64,512]{2,1,0:T(8,128)S(1)} collective-permute-done((f32[4,64,512]{2,1,0:T(8,128)S(1)}, f32[4,64,512]{2,1,0:T(8,128)S(1)}, u32[]{:S(2)}, u32[]{:S(2)}) %collective-permute-start.45) | collective-permute-done | bytes 524320 | tf_op jit(solution)/shard_map/ppermute | solution.py:668
  376.0 4.9 collective-permute-done.44
  391.7 5.7 collective-permute-done.41
  399.9 7.9 %collective-permute-done.40 = f32[4,32,512]{2,1,0:T(8,128)S(1)} collective-permute-done((f32[4,32,512]{2,1,0:T(8,128)S(1)}, f32[4,32,512]{2,1,0:T(8,128)S(1)}, u32[]{:S(2)}, u32[]{:S(2)}) %collective-permute-start.40) | collective-permute-done | bytes 262176 | tf_op jit(solution)/shard_map/ppermute | solution.py:668
  413.4 15.5 %collective-permute-done.48 = f32[2,64,512]{2,1,0:T(8,128)S(1)} collective-permute-done((f32[2,64,512]{2,1,0:T(8,128)S(1)}, f32[2,64,512]{2,1,0:T(8,128)S(1)}, u32[]{:S(2)}, u32[]{:S(2)}) %collective-permute-start.48) | collective-permute-done | bytes 262176 | tf_op jit(solution)/shard_map/ppermute | solution.py:668
  443.7 10.1 %collective-permute-done.47 = f32[4,16,512]{2,1,0:T(8,128)S(1)} collective-permute-done((f32[4,16,512]{2,1,0:T(8,128)S(1)}, f32[4,16,512]{2,1,0:T(8,128)S(1)}, u32[]{:S(2)}, u32[]{:S(2)}) %collective-permute-start.47) | collective-permute-done | bytes 131104 | tf_op jit(solution)/shard_map/ppermute | solution.py:668
  454.5 11.2 %collective-permute-done.55 = f32[4,16,512]{2,1,0:T(8,128)S(1)} collective-permute-done((f32[4,16,512]{2,1,0:T(8,128)S(1)}, f32[4,16,512]{2,1,0:T(8,128)S(1)}, u32[]{:S(2)}, u32[]{:S(2)}) %collective-permute-start.55) | collective-permute-done | bytes 131104 | tf_op jit(solution)/shard_map/ppermute | solution.py:668
  466.4 5.7 collective-permute-done.56
  472.8 4.6 collective-permute-done.57
  481.4 8.2 %collective-permute-done.59 = f32[4,64,512]{2,1,0:T(8,128)S(1)} collective-permute-done((f32[4,64,512]{2,1,0:T(8,128)}, f32[4,64,512]{2,1,0:T(8,128)S(1)}, u32[]{:S(2)}, u32[]{:S(2)}) %collective-permute-start.59) | collective-permute-done | bytes 524320 | tf_op jit(solution)/shard_map/ppermute | solution.py:668
  492.0 4.6 collective-permute-done.60
  497.1 10.9 %collective-permute-done.63 = f32[5,32,512]{2,1,0:T(8,128)S(1)} collective-permute-done((f32[5,32,512]{2,1,0:T(8,128)S(1)}, f32[5,32,512]{2,1,0:T(8,128)S(1)}, u32[]{:S(2)}, u32[]{:S(2)}) %collective-permute-start.63) | collective-permute-done | bytes 327712 | tf_op jit(solution)/shard_map/ppermute | solution.py:668
  508.0 4.3 collective-permute-start.64
  514.0 8.5 %collective-permute-done.64 = f32[5,16,512]{2,1,0:T(8,128)S(1)} collective-permute-done((f32[5,16,512]{2,1,0:T(8,128)S(1)}, f32[5,16,512]{2,1,0:T(8,128)S(1)}, u32[]{:S(2)}, u32[]{:S(2)}) %collective-permute-start.64) | collective-permute-done | bytes 163872 | tf_op jit(solution)/shard_map/ppermute | solution.py:668
  528.9 9.5 %collective-permute-done.67 = f32[5,16,512]{2,1,0:T(8,128)S(1)} collective-permute-done((f32[5,16,512]{2,1,0:T(8,128)S(1)}, f32[5,16,512]{2,1,0:T(8,128)S(1)}, u32[]{:S(2)}, u32[]{:S(2)}) %collective-permute-start.67) | collective-permute-done | bytes 163872 | tf_op jit(solution)/shard_map/ppermute | solution.py:668
  538.6 12.8 %collective-permute-done.66 = f32[4,32,512]{2,1,0:T(8,128)S(1)} collective-permute-done((f32[4,32,512]{2,1,0:T(8,128)S(1)}, f32[4,32,512]{2,1,0:T(8,128)S(1)}, u32[]{:S(2)}, u32[]{:S(2)}) %collective-permute-start.66) | collective-permute-done | bytes 262176 | tf_op jit(solution)/shard_map/ppermute | solution.py:668
  553.0 9.2 %collective-permute-done.69 = f32[5,32,512]{2,1,0:T(8,128)S(1)} collective-permute-done((f32[5,32,512]{2,1,0:T(8,128)S(1)}, f32[5,32,512]{2,1,0:T(8,128)S(1)}, u32[]{:S(2)}, u32[]{:S(2)}) %collective-permute-start.69) | collective-permute-done | bytes 327712 | tf_op jit(solution)/shard_map/ppermute | solution.py:668
  566.5 16.4 %collective-permute-done.71 = f32[5,64,512]{2,1,0:T(8,128)} collective-permute-done((f32[5,64,512]{2,1,0:T(8,128)S(1)}, f32[5,64,512]{2,1,0:T(8,128)}, u32[]{:S(2)}, u32[]{:S(2)}) %collective-permute-start.71) | collective-permute-done | bytes 655392 | tf_op jit(solution)/shard_map/ppermute | solution.py:668
  587.8 3.7 shard_map.459
  591.5 10.9 %shard_map.460 = f32[4608,512]{1,0:T(8,128)} custom-call(f32[32,208,512]{2,1,0:T(8,128)} %all-gather.5.cloned.1.call-done.in_ref), custom_call_target="tpu_custom_call" | custom-call | bytes 18874368 | tf_op jit(solution)/shard_map/pallas_call | solution.py:636
  602.4 15.5 %collective-permute-done.70.near_ref = f32[4,128,512]{2,1,0:T(8,128)} collective-permute-done((f32[4,128,512]{2,1,0:T(8,128)S(1)}, f32[4,128,512]{2,1,0:T(8,128)}, u32[]{:S(2)}, u32[]{:S(2)}) %collective-permute-start.70) | collective-permute-done | bytes 1048608 | tf_op jit(solution)/shard_map/ppermute | solution.py:668
  622.5 7.1 %shard_map.461.refs_0_ = f32[4608,512]{1,0:T(8,128)} custom-call(s32[4]{0:T(128)} %pad_add_fusion.1.place_ref, f32[5,128,512]{2,1,0:T(8,128)} %copy-done.2, f32[5,128,512]{2,1,0:T(8,128)} %collective-permute-done.74.near_ref, f32[5,128,512]{2,1,0:T(8,128)} %collective-permute-done.75.far_ref, f32[5,128,512]{2,1,0:T(8,128)} %collective-permute-done.76.both_ref), custom_call_target="tpu_custom_call" | custom-call | bytes 10485760 | tf_op jit(solution)/shard_map/pallas_call | solution.py:600
  629.6 5.4 shard_map.462
  635.0 4.4 all-gather.3.cloned.1.call-done.in_ref
  639.4 3.7 shard_map.464.refs_0_
  643.1 3.7 shard_map.463
  646.9 3.7 shard_map.466
  653.7 3.7 shard_map.465
  (358 shorter events, 199.4 us)
Async XLA Ops:
  15.6 17.5 %all-to-all-start = ((f32[32,16,128]{2,1,0:T(8,128)}), f32[32,16,128]{2,1,0:T(8,128)S(1)}, u32[]{:S(2)}, u32[]{:S(2)}) async-start(f32[32,16,128]{2,1,0:T(8,128)} %get-tuple-element.243), calls=%async_computation | async-start | bytes 524288 | tf_op jit(solution)/shard_map/all_to_all | solution.py:672
  41.1 11.1 %all-to-all-start.1 = ((f32[32,8,128]{2,1,0:T(8,128)}), f32[32,8,128]{2,1,0:T(8,128)S(1)}, u32[]{:S(2)}, u32[]{:S(2)}) async-start(f32[32,8,128]{2,1,0:T(8,128)} %get-tuple-element.245), calls=%async_computation.1 | async-start | bytes 262144 | tf_op jit(solution)/shard_map/all_to_all | solution.py:672
  68.4 5.7 collective-permute-start.6
  125.2 5.5 collective-permute-start.13
  145.7 5.0 collective-permute-start.19
  148.9 5.5 collective-permute-start.20
  161.3 11.0 %all-to-all-start.4 = ((f32[32,8,128]{2,1,0:T(8,128)}), f32[32,8,128]{2,1,0:T(8,128)S(1)}, u32[]{:S(2)}, u32[]{:S(2)}) async-start(f32[32,8,128]{2,1,0:T(8,128)} %get-tuple-element.262), calls=%async_computation.4 | async-start | bytes 262144 | tf_op jit(solution)/shard_map/all_to_all | solution.py:672
  179.5 11.0 %all-to-all-start.5 = ((f32[32,8,128]{2,1,0:T(8,128)}), f32[32,8,128]{2,1,0:T(8,128)S(1)}, u32[]{:S(2)}, u32[]{:S(2)}) async-start(f32[32,8,128]{2,1,0:T(8,128)} %get-tuple-element.267), calls=%async_computation.5 | async-start | bytes 262144 | tf_op jit(solution)/shard_map/all_to_all | solution.py:672
  182.1 115.5 %reduce-scatter.2.cloned.1.call-start = ((), (), s32[]{:S(2)}) async-start(), calls=%async_computation.9 | async-start | bytes 15335424 | tf_op jit(solution)/shard_map/reduce_scatter | solution.py:1017
  208.5 9.1 %collective-permute-start.25 = (f32[64,128]{1,0:T(8,128)S(1)}, f32[64,128]{1,0:T(8,128)S(1)}, u32[]{:S(2)}, u32[]{:S(2)}) collective-permute-start(f32[64,128]{1,0:T(8,128)S(1)} %add_add_fusion.1), channel_id=1, source_target_pairs={{0,1},{1,0},{2,3},{3,2},{4,5},{5,4},{6,7},{7,6},{8,9},{9,8},{10,11... | collective-permute-start | bytes 98312 | tf_op jit(solution)/shard_map/ppermute | solution.py:668
  210.1 7.5 %collective-permute-start.26 = (f32[64,128]{1,0:T(8,128)S(1)}, f32[64,128]{1,0:T(8,128)S(1)}, u32[]{:S(2)}, u32[]{:S(2)}) collective-permute-start(f32[64,128]{1,0:T(8,128)S(1)} %add_add_fusion.1), channel_id=1, source_target_pairs={{0,2},{1,3},{2,0},{3,1},{4,6},{5,7},{6,4},{7,5},{8,10},{9,11},{10,... | collective-permute-start | bytes 98312 | tf_op jit(solution)/shard_map/ppermute | solution.py:668
  212.6 5.7 collective-permute-start.27
  218.9 25.1 %collective-permute-start.28 = (f32[4,256,512]{2,1,0:T(8,128)}, f32[4,256,512]{2,1,0:T(8,128)S(1)}, u32[]{:S(2)}, u32[]{:S(2)}) collective-permute-start(f32[4,256,512]{2,1,0:T(8,128)} %get-tuple-element.282), channel_id=1, source_target_pairs={{0,4},{1,5},{2,6},{3,7},{4,0},{5,1},{6,2},{7,3},{8,12},{9,13},{10,... | collective-permute-start | bytes 6291464 | tf_op jit(solution)/shard_map/ppermute | solution.py:668
  226.3 17.6 %all-to-all-start.6 = ((f32[32,8,128]{2,1,0:T(8,128)}), f32[32,8,128]{2,1,0:T(8,128)S(1)}, u32[]{:S(2)}, u32[]{:S(2)}) async-start(f32[32,8,128]{2,1,0:T(8,128)} %get-tuple-element.274), calls=%async_computation.6 | async-start | bytes 262144 | tf_op jit(solution)/shard_map/all_to_all | solution.py:672
  244.0 32.7 %collective-permute-start.31 = (f32[4,256,512]{2,1,0:T(8,128)}, f32[4,256,512]{2,1,0:T(8,128)}, u32[]{:S(2)}, u32[]{:S(2)}) collective-permute-start(f32[4,256,512]{2,1,0:T(8,128)} %get-tuple-element.295), channel_id=1, source_target_pairs={{0,4},{1,5},{2,6},{3,7},{4,0},{5,1},{6,2},{7,3},{8,12},{9,13},{10,... | collective-permute-start | bytes 6291464 | tf_op jit(solution)/shard_map/ppermute | solution.py:668
  244.3 32.4 %collective-permute-start.30 = (f32[4,256,512]{2,1,0:T(8,128)}, f32[4,256,512]{2,1,0:T(8,128)}, u32[]{:S(2)}, u32[]{:S(2)}) collective-permute-start(f32[4,256,512]{2,1,0:T(8,128)} %get-tuple-element.293), channel_id=1, source_target_pairs={{0,4},{1,5},{2,6},{3,7},{4,0},{5,1},{6,2},{7,3},{8,12},{9,13},{10,... | collective-permute-start | bytes 6291464 | tf_op jit(solution)/shard_map/ppermute | solution.py:668
  244.5 32.2 %collective-permute-start.29 = (f32[4,256,512]{2,1,0:T(8,128)}, f32[4,256,512]{2,1,0:T(8,128)}, u32[]{:S(2)}, u32[]{:S(2)}) collective-permute-start(f32[4,256,512]{2,1,0:T(8,128)} %get-tuple-element.291), channel_id=1, source_target_pairs={{0,4},{1,5},{2,6},{3,7},{4,0},{5,1},{6,2},{7,3},{8,12},{9,13},{10,... | collective-permute-start | bytes 6291464 | tf_op jit(solution)/shard_map/ppermute | solution.py:668
  254.5 22.2 %all-to-all-start.7 = ((f32[32,8,128]{2,1,0:T(8,128)}), f32[32,8,128]{2,1,0:T(8,128)S(1)}, u32[]{:S(2)}, u32[]{:S(2)}) async-start(f32[32,8,128]{2,1,0:T(8,128)} %get-tuple-element.285), calls=%async_computation.7 | async-start | bytes 262144 | tf_op jit(solution)/shard_map/all_to_all | solution.py:672
  260.0 327.7 %all-gather.5.cloned.1.call-start = ((), (), s32[]{:S(2)}) async-start(), calls=%async_computation.11 | async-start | bytes 14057472 | tf_op jit(solution)/shard_map/all_gather | solution.py:790
  279.4 38.5 %collective-permute-start.32 = (f32[4,128,512]{2,1,0:T(8,128)}, f32[4,128,512]{2,1,0:T(8,128)}, u32[]{:S(2)}, u32[]{:S(2)}) collective-permute-start(f32[4,128,512]{2,1,0:T(8,128)} %dynamic-slice_add_fusion.11), channel_id=1, source_target_pairs={{0,8},{1,9},{2,10},{3,11},{4,12},{5,13},{6,14},{7,15},{8,0},{9,1},... | collective-permute-start | bytes 3145736 | tf_op jit(solution)/shard_map/ppermute | solution.py:668
  283.5 36.5 %collective-permute-start.35 = (f32[4,128,512]{2,1,0:T(8,128)}, f32[4,128,512]{2,1,0:T(8,128)}, u32[]{:S(2)}, u32[]{:S(2)}) collective-permute-start(f32[4,128,512]{2,1,0:T(8,128)} %dynamic-slice_add_fusion.10), channel_id=1, source_target_pairs={{0,16},{1,17},{2,18},{3,19},{4,20},{5,21},{6,22},{7,23},{8,24},{9,... | collective-permute-start | bytes 3145736 | tf_op jit(solution)/shard_map/ppermute | solution.py:668
  287.3 46.8 %collective-permute-start.39 = (f32[4,128,512]{2,1,0:T(8,128)}, f32[4,128,512]{2,1,0:T(8,128)}, u32[]{:S(2)}, u32[]{:S(2)}) collective-permute-start(f32[4,128,512]{2,1,0:T(8,128)} %dynamic-slice_add_fusion.9), channel_id=1, source_target_pairs={{0,8},{1,9},{2,10},{3,11},{4,12},{5,13},{6,14},{7,15},{8,0},{9,1},... | collective-permute-start | bytes 3145736 | tf_op jit(solution)/shard_map/ppermute | solution.py:668
  290.5 45.6 %collective-permute-start.38 = (f32[4,128,512]{2,1,0:T(8,128)}, f32[4,128,512]{2,1,0:T(8,128)}, u32[]{:S(2)}, u32[]{:S(2)}) collective-permute-start(f32[4,128,512]{2,1,0:T(8,128)} %dynamic-slice_add_fusion.8), channel_id=1, source_target_pairs={{0,16},{1,17},{2,18},{3,19},{4,20},{5,21},{6,22},{7,23},{8,24},{9,... | collective-permute-start | bytes 3145736 | tf_op jit(solution)/shard_map/ppermute | solution.py:668
  300.4 21.5 %collective-permute-start.34 = (f32[13,32,512]{2,1,0:T(8,128)}, f32[13,32,512]{2,1,0:T(8,128)}, u32[]{:S(2)}, u32[]{:S(2)}) collective-permute-start(f32[13,32,512]{2,1,0:T(8,128)} %get-tuple-element.472), channel_id=1, source_target_pairs={{0,1},{1,0},{2,3},{3,2},{4,5},{5,4},{6,7},{7,6},{8,9},{9,8},{10,11... | collective-permute-start | bytes 2555912 | tf_op jit(solution)/shard_map/ppermute | solution.py:668
  323.0 20.9 %collective-permute-start.37 = (f32[13,16,512]{2,1,0:T(8,128)S(1)}, f32[13,16,512]{2,1,0:T(8,128)S(1)}, u32[]{:S(2)}, u32[]{:S(2)}) collective-permute-start(f32[13,16,512]{2,1,0:T(8,128)S(1)} %dynamic-slice_add_fusion.27), channel_id=1, source_target_pairs={{0,2},{1,3},{2,0},{3,1},{4,6},{5,7},{6,4},{7,5},{8,10},{9,11},{10,... | collective-permute-start | bytes 1277960 | tf_op jit(solution)/shard_map/ppermute | solution.py:668
  344.7 294.7 %all-gather.3.cloned.1.call-start = ((), (), s32[]{:S(2)}) async-start(), calls=%async_computation.10 | async-start | bytes 19464192 | tf_op jit(solution)/shard_map/all_gather | solution.py:1172
  345.0 38.4 %collective-permute-start.43 = (f32[5,256,512]{2,1,0:T(8,128)}, f32[5,256,512]{2,1,0:T(8,128)}, u32[]{:S(2)}, u32[]{:S(2)}) collective-permute-start(f32[5,256,512]{2,1,0:T(8,128)} %get-tuple-element.311), channel_id=1, source_target_pairs={{0,4},{1,5},{2,6},{3,7},{4,0},{5,1},{6,2},{7,3},{8,12},{9,13},{10,... | collective-permute-start | bytes 7864328 | tf_op jit(solution)/shard_map/ppermute | solution.py:668
  345.1 20.4 %collective-permute-start.36 = (f32[2,256,512]{2,1,0:T(8,128)}, f32[2,256,512]{2,1,0:T(8,128)}, u32[]{:S(2)}, u32[]{:S(2)}) collective-permute-start(f32[2,256,512]{2,1,0:T(8,128)} %get-tuple-element.330), channel_id=1, source_target_pairs={{0,4},{1,5},{2,6},{3,7},{4,0},{5,1},{6,2},{7,3},{8,12},{9,13},{10,... | collective-permute-start | bytes 3145736 | tf_op jit(solution)/shard_map/ppermute | solution.py:668
  345.6 17.3 %collective-permute-start.33 = (f32[4,64,512]{2,1,0:T(8,128)}, f32[4,64,512]{2,1,0:T(8,128)}, u32[]{:S(2)}, u32[]{:S(2)}) collective-permute-start(f32[4,64,512]{2,1,0:T(8,128)} %dynamic-slice_add_fusion.25), channel_id=1, source_target_pairs={{0,16},{1,17},{2,18},{3,19},{4,20},{5,21},{6,22},{7,23},{8,24},{9,... | collective-permute-start | bytes 1572872 | tf_op jit(solution)/shard_map/ppermute | solution.py:668
  347.1 40.0 %collective-permute-start.42 = (f32[4,256,512]{2,1,0:T(8,128)}, f32[4,256,512]{2,1,0:T(8,128)}, u32[]{:S(2)}, u32[]{:S(2)}) collective-permute-start(f32[4,256,512]{2,1,0:T(8,128)} %get-tuple-element.312), channel_id=1, source_target_pairs={{0,4},{1,5},{2,6},{3,7},{4,0},{5,1},{6,2},{7,3},{8,12},{9,13},{10,... | collective-permute-start | bytes 6291464 | tf_op jit(solution)/shard_map/ppermute | solution.py:668
  347.1 21.8 %collective-permute-start.46 = (f32[4,64,512]{2,1,0:T(8,128)}, f32[4,64,512]{2,1,0:T(8,128)S(1)}, u32[]{:S(2)}, u32[]{:S(2)}) collective-permute-start(f32[4,64,512]{2,1,0:T(8,128)} %dynamic-slice_add_fusion.23), channel_id=1, source_target_pairs={{0,8},{1,9},{2,10},{3,11},{4,12},{5,13},{6,14},{7,15},{8,0},{9,1},... | collective-permute-start | bytes 1572872 | tf_op jit(solution)/shard_map/ppermute | solution.py:668
  362.9 13.1 %collective-permute-start.45 = (f32[4,64,512]{2,1,0:T(8,128)S(1)}, f32[4,64,512]{2,1,0:T(8,128)S(1)}, u32[]{:S(2)}, u32[]{:S(2)}) collective-permute-start(f32[4,64,512]{2,1,0:T(8,128)S(1)} %copy-done.30), channel_id=1, source_target_pairs={{0,16},{1,17},{2,18},{3,19},{4,20},{5,21},{6,22},{7,23},{8,24},{9,... | collective-permute-start | bytes 1572872 | tf_op jit(solution)/shard_map/ppermute | solution.py:668
  365.5 15.4 %collective-permute-start.44 = (f32[4,64,512]{2,1,0:T(8,128)S(1)}, f32[4,64,512]{2,1,0:T(8,128)S(1)}, u32[]{:S(2)}, u32[]{:S(2)}) collective-permute-start(f32[4,64,512]{2,1,0:T(8,128)S(1)} %copy-done.29), channel_id=1, source_target_pairs={{0,8},{1,9},{2,10},{3,11},{4,12},{5,13},{6,14},{7,15},{8,0},{9,1},... | collective-permute-start | bytes 1572872 | tf_op jit(solution)/shard_map/ppermute | solution.py:668
  368.9 28.5 %collective-permute-start.41 = (f32[2,128,512]{2,1,0:T(8,128)S(1)}, f32[2,128,512]{2,1,0:T(8,128)S(1)}, u32[]{:S(2)}, u32[]{:S(2)}) collective-permute-start(f32[2,128,512]{2,1,0:T(8,128)S(1)} %dynamic-slice_add_fusion.20), channel_id=1, source_target_pairs={{0,1},{1,0},{2,3},{3,2},{4,5},{5,4},{6,7},{7,6},{8,9},{9,8},{10,11... | collective-permute-start | bytes 1572872 | tf_op jit(solution)/shard_map/ppermute | solution.py:668
  375.9 31.8 %collective-permute-start.40 = (f32[4,32,512]{2,1,0:T(8,128)S(1)}, f32[4,32,512]{2,1,0:T(8,128)S(1)}, u32[]{:S(2)}, u32[]{:S(2)}) collective-permute-start(f32[4,32,512]{2,1,0:T(8,128)S(1)} %dynamic-slice_add_fusion.41), channel_id=1, source_target_pairs={{0,1},{1,0},{2,3},{3,2},{4,5},{5,4},{6,7},{7,6},{8,9},{9,8},{10,11... | collective-permute-start | bytes 786440 | tf_op jit(solution)/shard_map/ppermute | solution.py:668
  380.9 32.5 %collective-permute-start.49 = (f32[4,32,512]{2,1,0:T(8,128)S(1)}, f32[4,32,512]{2,1,0:T(8,128)S(1)}, u32[]{:S(2)}, u32[]{:S(2)}) collective-permute-start(f32[4,32,512]{2,1,0:T(8,128)S(1)} %dynamic-slice_add_fusion.39), channel_id=1, source_target_pairs={{0,1},{1,0},{2,3},{3,2},{4,5},{5,4},{6,7},{7,6},{8,9},{9,8},{10,11... | collective-permute-start | bytes 786440 | tf_op jit(solution)/shard_map/ppermute | solution.py:668
  383.4 45.5 %collective-permute-start.54 = (f32[4,32,512]{2,1,0:T(8,128)S(1)}, f32[4,32,512]{2,1,0:T(8,128)S(1)}, u32[]{:S(2)}, u32[]{:S(2)}) collective-permute-start(f32[4,32,512]{2,1,0:T(8,128)S(1)} %dynamic-slice_add_fusion.38), channel_id=1, source_target_pairs={{0,1},{1,0},{2,3},{3,2},{4,5},{5,4},{6,7},{7,6},{8,9},{9,8},{10,11... | collective-permute-start | bytes 786440 | tf_op jit(solution)/shard_map/ppermute | solution.py:668
  388.6 46.8 %collective-permute-start.52 = (f32[4,128,512]{2,1,0:T(8,128)S(1)}, f32[4,128,512]{2,1,0:T(8,128)S(1)}, u32[]{:S(2)}, u32[]{:S(2)}) collective-permute-start(f32[4,128,512]{2,1,0:T(8,128)S(1)} %dynamic-slice_add_fusion.3), channel_id=1, source_target_pairs={{0,16},{1,17},{2,18},{3,19},{4,20},{5,21},{6,22},{7,23},{8,24},{9,... | collective-permute-start | bytes 3145736 | tf_op jit(solution)/shard_map/ppermute | solution.py:668
  397.4 39.5 %collective-permute-start.51 = (f32[5,128,512]{2,1,0:T(8,128)S(1)}, f32[5,128,512]{2,1,0:T(8,128)S(1)}, u32[]{:S(2)}, u32[]{:S(2)}) collective-permute-start(f32[5,128,512]{2,1,0:T(8,128)S(1)} %dynamic-slice_add_fusion.1), channel_id=1, source_target_pairs={{0,8},{1,9},{2,10},{3,11},{4,12},{5,13},{6,14},{7,15},{8,0},{9,1},... | collective-permute-start | bytes 3932168 | tf_op jit(solution)/shard_map/ppermute | solution.py:668
  407.8 21.2 %collective-permute-start.48 = (f32[2,64,512]{2,1,0:T(8,128)S(1)}, f32[2,64,512]{2,1,0:T(8,128)S(1)}, u32[]{:S(2)}, u32[]{:S(2)}) collective-permute-start(f32[2,64,512]{2,1,0:T(8,128)S(1)} %dynamic-slice_add_fusion.36), channel_id=1, source_target_pairs={{0,8},{1,9},{2,10},{3,11},{4,12},{5,13},{6,14},{7,15},{8,0},{9,1},... | collective-permute-start | bytes 786440 | tf_op jit(solution)/shard_map/ppermute | solution.py:668
  413.4 21.9 %collective-permute-start.53 = (f32[4,32,512]{2,1,0:T(8,128)S(1)}, f32[4,32,512]{2,1,0:T(8,128)S(1)}, u32[]{:S(2)}, u32[]{:S(2)}) collective-permute-start(f32[4,32,512]{2,1,0:T(8,128)S(1)} %dynamic-slice_add_fusion.37), channel_id=1, source_target_pairs={{0,1},{1,0},{2,3},{3,2},{4,5},{5,4},{6,7},{7,6},{8,9},{9,8},{10,11... | collective-permute-start | bytes 786440 | tf_op jit(solution)/shard_map/ppermute | solution.py:668
  428.9 24.8 %collective-permute-start.47 = (f32[4,16,512]{2,1,0:T(8,128)S(1)}, f32[4,16,512]{2,1,0:T(8,128)S(1)}, u32[]{:S(2)}, u32[]{:S(2)}) collective-permute-start(f32[4,16,512]{2,1,0:T(8,128)S(1)} %dynamic-slice_add_fusion.55), channel_id=1, source_target_pairs={{0,2},{1,3},{2,0},{3,1},{4,6},{5,7},{6,4},{7,5},{8,10},{9,11},{10,... | collective-permute-start | bytes 393224 | tf_op jit(solution)/shard_map/ppermute | solution.py:668
  429.0 36.7 %collective-permute-start.55 = (f32[4,16,512]{2,1,0:T(8,128)S(1)}, f32[4,16,512]{2,1,0:T(8,128)S(1)}, u32[]{:S(2)}, u32[]{:S(2)}) collective-permute-start(f32[4,16,512]{2,1,0:T(8,128)S(1)} %dynamic-slice_add_fusion.53), channel_id=1, source_target_pairs={{0,2},{1,3},{2,0},{3,1},{4,6},{5,7},{6,4},{7,5},{8,10},{9,11},{10,... | collective-permute-start | bytes 393224 | tf_op jit(solution)/shard_map/ppermute | solution.py:668
  435.2 7.7 %collective-permute-start.50 = (f32[2,32,512]{2,1,0:T(8,128)S(1)}, f32[2,32,512]{2,1,0:T(8,128)S(1)}, u32[]{:S(2)}, u32[]{:S(2)}) collective-permute-start(f32[2,32,512]{2,1,0:T(8,128)S(1)} %dynamic-slice_add_fusion.52), channel_id=1, source_target_pairs={{0,16},{1,17},{2,18},{3,19},{4,20},{5,21},{6,22},{7,23},{8,24},{9,... | collective-permute-start | bytes 393224 | tf_op jit(solution)/shard_map/ppermute | solution.py:668
  435.4 36.7 %collective-permute-start.56 = (f32[4,16,512]{2,1,0:T(8,128)S(1)}, f32[4,16,512]{2,1,0:T(8,128)S(1)}, u32[]{:S(2)}, u32[]{:S(2)}) collective-permute-start(f32[4,16,512]{2,1,0:T(8,128)S(1)} %dynamic-slice_add_fusion.50), channel_id=1, source_target_pairs={{0,2},{1,3},{2,0},{3,1},{4,6},{5,7},{6,4},{7,5},{8,10},{9,11},{10,... | collective-permute-start | bytes 393224 | tf_op jit(solution)/shard_map/ppermute | solution.py:668
  436.9 40.4 %collective-permute-start.57 = (f32[4,16,512]{2,1,0:T(8,128)S(1)}, f32[4,16,512]{2,1,0:T(8,128)S(1)}, u32[]{:S(2)}, u32[]{:S(2)}) collective-permute-start(f32[4,16,512]{2,1,0:T(8,128)S(1)} %dynamic-slice_add_fusion.49), channel_id=1, source_target_pairs={{0,2},{1,3},{2,0},{3,1},{4,6},{5,7},{6,4},{7,5},{8,10},{9,11},{10,... | collective-permute-start | bytes 393224 | tf_op jit(solution)/shard_map/ppermute | solution.py:668
  443.0 36.5 %collective-permute-start.58 = (f32[2,16,512]{2,1,0:T(8,128)S(1)}, f32[2,16,512]{2,1,0:T(8,128)S(1)}, u32[]{:S(2)}, u32[]{:S(2)}) collective-permute-start(f32[2,16,512]{2,1,0:T(8,128)S(1)} %dynamic-slice_add_fusion.57), channel_id=1, source_target_pairs={{0,2},{1,3},{2,0},{3,1},{4,6},{5,7},{6,4},{7,5},{8,10},{9,11},{10,... | collective-permute-start | bytes 196616 | tf_op jit(solution)/shard_map/ppermute | solution.py:668
  480.2 9.5 %collective-permute-start.59 = (f32[4,64,512]{2,1,0:T(8,128)}, f32[4,64,512]{2,1,0:T(8,128)S(1)}, u32[]{:S(2)}, u32[]{:S(2)}) collective-permute-start(f32[4,64,512]{2,1,0:T(8,128)} %dynamic-slice_add_fusion.15), channel_id=1, source_target_pairs={{0,8},{1,9},{2,10},{3,11},{4,12},{5,13},{6,14},{7,15},{8,0},{9,1},... | collective-permute-start | bytes 1572872 | tf_op jit(solution)/shard_map/ppermute | solution.py:668
  481.0 10.8 %collective-permute-start.61 = (f32[5,64,512]{2,1,0:T(8,128)}, f32[5,64,512]{2,1,0:T(8,128)S(1)}, u32[]{:S(2)}, u32[]{:S(2)}) collective-permute-start(f32[5,64,512]{2,1,0:T(8,128)} %dynamic-slice_add_fusion.13), channel_id=1, source_target_pairs={{0,16},{1,17},{2,18},{3,19},{4,20},{5,21},{6,22},{7,23},{8,24},{9,... | collective-permute-start | bytes 1966088 | tf_op jit(solution)/shard_map/ppermute | solution.py:668
  489.7 7.0 %collective-permute-start.60 = (f32[4,32,512]{2,1,0:T(8,128)S(1)}, f32[4,32,512]{2,1,0:T(8,128)S(1)}, u32[]{:S(2)}, u32[]{:S(2)}) collective-permute-start(f32[4,32,512]{2,1,0:T(8,128)S(1)} %dynamic-slice_add_fusion.31), channel_id=1, source_target_pairs={{0,1},{1,0},{2,3},{3,2},{4,5},{5,4},{6,7},{7,6},{8,9},{9,8},{10,11... | collective-permute-start | bytes 786440 | tf_op jit(solution)/shard_map/ppermute | solution.py:668
  491.9 16.1 %collective-permute-start.63 = (f32[5,32,512]{2,1,0:T(8,128)S(1)}, f32[5,32,512]{2,1,0:T(8,128)S(1)}, u32[]{:S(2)}, u32[]{:S(2)}) collective-permute-start(f32[5,32,512]{2,1,0:T(8,128)S(1)} %dynamic-slice_add_fusion.29), channel_id=1, source_target_pairs={{0,1},{1,0},{2,3},{3,2},{4,5},{5,4},{6,7},{7,6},{8,9},{9,8},{10,11... | collective-permute-start | bytes 983048 | tf_op jit(solution)/shard_map/ppermute | solution.py:668
  496.7 17.2 %collective-permute-start.62 = (f32[4,16,512]{2,1,0:T(8,128)S(1)}, f32[4,16,512]{2,1,0:T(8,128)S(1)}, u32[]{:S(2)}, u32[]{:S(2)}) collective-permute-start(f32[4,16,512]{2,1,0:T(8,128)S(1)} %dynamic-slice_add_fusion.45), channel_id=1, source_target_pairs={{0,2},{1,3},{2,0},{3,1},{4,6},{5,7},{6,4},{7,5},{8,10},{9,11},{10,... | collective-permute-start | bytes 393224 | tf_op jit(solution)/shard_map/ppermute | solution.py:668
  508.0 14.5 %collective-permute-start.64 = (f32[5,16,512]{2,1,0:T(8,128)S(1)}, f32[5,16,512]{2,1,0:T(8,128)S(1)}, u32[]{:S(2)}, u32[]{:S(2)}) collective-permute-start(f32[5,16,512]{2,1,0:T(8,128)S(1)} %dynamic-slice_add_fusion.43), channel_id=1, source_target_pairs={{0,2},{1,3},{2,0},{3,1},{4,6},{5,7},{6,4},{7,5},{8,10},{9,11},{10,... | collective-permute-start | bytes 491528 | tf_op jit(solution)/shard_map/ppermute | solution.py:668
  522.5 6.3 collective-permute-start.65
  522.6 15.8 %collective-permute-start.67 = (f32[5,16,512]{2,1,0:T(8,128)S(1)}, f32[5,16,512]{2,1,0:T(8,128)S(1)}, u32[]{:S(2)}, u32[]{:S(2)}) collective-permute-start(f32[5,16,512]{2,1,0:T(8,128)S(1)} %add.575), channel_id=1, source_target_pairs={{0,2},{1,3},{2,0},{3,1},{4,6},{5,7},{6,4},{7,5},{8,10},{9,11},{10,... | collective-permute-start | bytes 491528 | tf_op jit(solution)/shard_map/ppermute | solution.py:668
  528.9 22.6 %collective-permute-start.66 = (f32[4,32,512]{2,1,0:T(8,128)S(1)}, f32[4,32,512]{2,1,0:T(8,128)S(1)}, u32[]{:S(2)}, u32[]{:S(2)}) collective-permute-start(f32[4,32,512]{2,1,0:T(8,128)S(1)} %maximum_select_fusion.5), channel_id=1, source_target_pairs={{0,1},{1,0},{2,3},{3,2},{4,5},{5,4},{6,7},{7,6},{8,9},{9,8},{10,11... | collective-permute-start | bytes 786440 | tf_op jit(solution)/shard_map/ppermute | solution.py:668
  538.5 23.7 %collective-permute-start.69 = (f32[5,32,512]{2,1,0:T(8,128)S(1)}, f32[5,32,512]{2,1,0:T(8,128)S(1)}, u32[]{:S(2)}, u32[]{:S(2)}) collective-permute-start(f32[5,32,512]{2,1,0:T(8,128)S(1)} %maximum_select_fusion.4), channel_id=1, source_target_pairs={{0,1},{1,0},{2,3},{3,2},{4,5},{5,4},{6,7},{7,6},{8,9},{9,8},{10,11... | collective-permute-start | bytes 983048 | tf_op jit(solution)/shard_map/ppermute | solution.py:668
  551.5 14.9 %collective-permute-start.68 = (f32[4,64,512]{2,1,0:T(8,128)S(1)}, f32[4,64,512]{2,1,0:T(8,128)S(1)}, u32[]{:S(2)}, u32[]{:S(2)}) collective-permute-start(f32[4,64,512]{2,1,0:T(8,128)S(1)} %maximum_select_fusion.3), channel_id=1, source_target_pairs={{0,8},{1,9},{2,10},{3,11},{4,12},{5,13},{6,14},{7,15},{8,0},{9,1},... | collective-permute-start | bytes 1572872 | tf_op jit(solution)/shard_map/ppermute | solution.py:668
  562.3 20.6 %collective-permute-start.71 = (f32[5,64,512]{2,1,0:T(8,128)S(1)}, f32[5,64,512]{2,1,0:T(8,128)}, u32[]{:S(2)}, u32[]{:S(2)}) collective-permute-start(f32[5,64,512]{2,1,0:T(8,128)S(1)} %maximum_select_fusion.2), channel_id=1, source_target_pairs={{0,16},{1,17},{2,18},{3,19},{4,20},{5,21},{6,22},{7,23},{8,24},{9,... | collective-permute-start | bytes 1966088 | tf_op jit(solution)/shard_map/ppermute | solution.py:668
  584.4 33.6 %collective-permute-start.74 = (f32[5,128,512]{2,1,0:T(8,128)S(1)}, f32[5,128,512]{2,1,0:T(8,128)}, u32[]{:S(2)}, u32[]{:S(2)}) collective-permute-start(f32[5,128,512]{2,1,0:T(8,128)S(1)} %maximum_select_fusion.own_ref), channel_id=1, source_target_pairs={{0,8},{1,9},{2,10},{3,11},{4,12},{5,13},{6,14},{7,15},{8,0},{9,1},... | collective-permute-start | bytes 3932168 | tf_op jit(solution)/shard_map/ppermute | solution.py:668
  585.2 32.7 %collective-permute-start.70 = (f32[4,128,512]{2,1,0:T(8,128)S(1)}, f32[4,128,512]{2,1,0:T(8,128)}, u32[]{:S(2)}, u32[]{:S(2)}) collective-permute-start(f32[4,128,512]{2,1,0:T(8,128)S(1)} %maximum_select_fusion.1.own_ref), channel_id=1, source_target_pairs={{0,16},{1,17},{2,18},{3,19},{4,20},{5,21},{6,22},{7,23},{8,24},{9,... | collective-permute-start | bytes 3145736 | tf_op jit(solution)/shard_map/ppermute | solution.py:668
  587.7 34.6 %collective-permute-start.75 = (f32[5,128,512]{2,1,0:T(8,128)S(1)}, f32[5,128,512]{2,1,0:T(8,128)}, u32[]{:S(2)}, u32[]{:S(2)}) collective-permute-start(f32[5,128,512]{2,1,0:T(8,128)S(1)} %maximum_select_fusion.own_ref), channel_id=1, source_target_pairs={{0,4},{1,5},{2,6},{3,7},{4,0},{5,1},{6,2},{7,3},{8,12},{9,13},{10,... | collective-permute-start | bytes 3932168 | tf_op jit(solution)/shard_map/ppermute | solution.py:668
  618.0 11.6 %collective-permute-start.72 = (f32[4,128,512]{2,1,0:T(8,128)S(1)}, f32[4,128,512]{2,1,0:T(8,128)}, u32[]{:S(2)}, u32[]{:S(2)}) collective-permute-start(f32[4,128,512]{2,1,0:T(8,128)S(1)} %maximum_select_fusion.1.own_ref), channel_id=1, source_target_pairs={{0,4},{1,5},{2,6},{3,7},{4,0},{5,1},{6,2},{7,3},{8,12},{9,13},{10,... | collective-permute-start | bytes 3145736 | tf_op jit(solution)/shard_map/ppermute | solution.py:668
  618.5 11.1 %collective-permute-start.73 = (f32[4,128,512]{2,1,0:T(8,128)}, f32[4,128,512]{2,1,0:T(8,128)}, u32[]{:S(2)}, u32[]{:S(2)}) collective-permute-start(f32[4,128,512]{2,1,0:T(8,128)} %collective-permute-done.70.near_ref), channel_id=1, source_target_pairs={{0,4},{1,5},{2,6},{3,7},{4,0},{5,1},{6,2},{7,3},{8,12},{9,13},{10,... | collective-permute-start | bytes 3145736 | tf_op jit(solution)/shard_map/ppermute | solution.py:668
  (71 other events, 769.0 us)
Sparse Core Ops, SparseCore 0:
  190.6 106.9 reduce-scatter.1
  344.9 138.9 all-gather.4
  487.3 152.1 all-gather.2
